TPU v7x, 256 devices: a whole 4x4x8 slice. The times are simulated.
256 devices in a mesh: seq: 32 (over x, z_lo, core), tp: 8 (over y, z_hi).
Axes of the slice: x: 4, y: 4, z: 8 (z_hi: 2, z_lo: 4; z = z_hi * 4 + z_lo), core: 2. Of those that a mesh axis runs over, the one named last changes fastest.
Arguments:
- layer_input: bfloat16 [8192, 4096], P('seq', 'tp'), may hold values from -6 to 6
- value_weight: bfloat16 [4096, 4096], P(None, 'tp'), may hold values from -0.09375 to 0.09375
- filter_taps: bfloat16 [4096, 128], P('tp'), may hold values from -0.5 to 0.5
- query_codes: int32 [8192, 4096], P('seq', 'tp'), may hold values from 0 to 3
- query_low: float32 [8192, 32], P('seq', 'tp'), may hold values from -2 to -0.5
- query_high: float32 [8192, 32], P('seq', 'tp'), may hold values from 0.5 to 2
- key_codes: int32 [8192, 4096], P('seq', 'tp'), may hold values from 0 to 3
- key_low: float32 [8192, 32], P('seq', 'tp'), may hold values from -2 to -0.5
- key_high: float32 [8192, 32], P('seq', 'tp'), may hold values from 0.5 to 2
- out_grad: bfloat16 [8192, 4096], P('seq', 'tp'), may hold values from -6 to 6
Outputs:
- grad_input: float32 [8192, 4096], P('seq', 'tp')
- grad_weight: float32 [4096, 4096], P('seq', 'tp')
- grad_filter: float32 [4096, 128], P('tp')
- grad_query: float32 [8192, 4096], P('seq', 'tp')
- grad_key: float32 [8192, 4096], P('seq', 'tp')
All inputs are finite; a program needn't handle non-finite values.
Results may differ from a plain program's by a relative error of at most 0.0065.
Values may be sent and summed in bfloat16 or wider, within the bound.
No kernel may reach another device: no remote copies, remote signals or barrier semaphores. Data moves between devices by JAX's collectives and lax.ppermute only.
A program may use at most 64 MiB of HBM per device.

v0:
```python
import math

import jax
import jax.numpy as jnp
from jax import lax
from jax.sharding import PartitionSpec as P


def passed_along(block, axis, distance):
    devices = range(lax.axis_size(axis))
    route = [(i - distance, i) for i in devices if i - distance in devices]
    return lax.ppermute(block, axis, route)


def dequantize(code_array, lower, upper):
    token_count, channels = code_array.shape
    groups = lower.shape[1]
    levels = code_array.reshape(token_count, groups, channels // groups).astype(jnp.float32)
    step_size = (upper - lower) / 3.0
    return (lower[:, :, None] + levels * step_size[:, :, None]).reshape(token_count, channels)


def shards(
    layer_input,
    value_weight,
    filter_taps,
    query_codes,
    query_low,
    query_high,
    key_codes,
    key_low,
    key_high,
    out_grad,
):
    row_count = layer_input.shape[0]
    channel_count = filter_taps.shape[0]
    tap_count = filter_taps.shape[1]
    halo_rows = tap_count - 1
    full_input = lax.all_gather(layer_input, "tp", axis=1, tiled=True)
    values = jnp.dot(full_input, value_weight, preferred_element_type=jnp.float32)
    queries = dequantize(query_codes, query_low, query_high)
    key_values = dequantize(key_codes, key_low, key_high)
    product = (key_values * values).astype(jnp.bfloat16)
    earlier_rows = passed_along(product[row_count - halo_rows :], "seq", 1)
    product_ext = jnp.concatenate([earlier_rows, product], 0)
    upstream = out_grad.astype(jnp.float32)
    grad_conv = (upstream * queries).astype(jnp.bfloat16)
    later_rows = passed_along(grad_conv[:halo_rows], "seq", -1)
    grad_ext = jnp.concatenate([grad_conv, later_rows], 0)
    grad_conv_wide = grad_conv.astype(jnp.float32)
    taps_wide = filter_taps.astype(jnp.float32)
    inner = math.gcd(tap_count, 8)

    def tap_block(block, carry):
        conv_out, grad_mix, filter_part = carry
        base = (block * inner).astype(jnp.int32)
        for offset in range(inner):
            index = base + offset
            earlier = lax.dynamic_slice_in_dim(product_ext, halo_rows - index, row_count, 0).astype(
                jnp.float32
            )
            later = lax.dynamic_slice_in_dim(grad_ext, index, row_count, 0).astype(jnp.float32)
            tap_column = lax.dynamic_slice_in_dim(taps_wide, index, 1, 1)[:, 0]
            conv_out = conv_out + earlier * tap_column[None, :]
            grad_mix = grad_mix + later * tap_column[None, :]
            column = jnp.sum(grad_conv_wide * earlier, axis=0)
            filter_part = lax.dynamic_update_slice_in_dim(filter_part, column[:, None], index, 1)
        return (conv_out, grad_mix, filter_part)

    initial_carry = (
        jnp.zeros((row_count, channel_count), jnp.float32),
        jnp.zeros((row_count, channel_count), jnp.float32),
        jnp.zeros((channel_count, tap_count), jnp.float32),
    )
    conv_out, grad_mix, filter_part = lax.fori_loop(0, tap_count // inner, tap_block, initial_carry)
    scale = 1.0 / math.sqrt(row_count * lax.axis_size("seq"))
    grad_filter = lax.psum(filter_part, "seq") * scale
    grad_query = upstream * conv_out
    grad_key = grad_mix * values
    grad_value = (grad_mix * key_values).astype(jnp.bfloat16)
    shares = lax.psum_scatter(
        lax.dot_general(
            value_weight, grad_value, (((1,), (1,)), ((), ())), preferred_element_type=jnp.float32
        ),
        "tp",
        scatter_dimension=0,
        tiled=True,
    )
    grad_input = shares.T
    shares = lax.psum_scatter(
        lax.dot_general(
            full_input, grad_value, (((0,), (0,)), ((), ())), preferred_element_type=jnp.float32
        ),
        "seq",
        scatter_dimension=0,
        tiled=True,
    )
    grad_weight = shares * scale
    return (grad_input, grad_weight, grad_filter, grad_query, grad_key)


def solution(mesh):
    return jax.shard_map(
        shards,
        mesh=mesh,
        in_specs=(
            P("seq", "tp"),
            P(None, "tp"),
            P("tp", None),
            P("seq", "tp"),
            P("seq", "tp"),
            P("seq", "tp"),
            P("seq", "tp"),
            P("seq", "tp"),
            P("seq", "tp"),
            P("seq", "tp"),
        ),
        out_specs=(P("seq", "tp"), P("seq", "tp"), P("tp", None), P("seq", "tp"), P("seq", "tp")),
        check_vma=False,
    )
```

profile of v0, /device:TPU:1, one launch (start us, length us, event | category | flops | bytes accessed | tf_op | source)
XLA Modules:
  0.0 900.0 jit_solution(10020410156195089828)
XLA Ops:
  11.7 5.2 collective-permute-start.1
  17.1 73.0 %all-gather.2.cloned.1.call-done = bf16[256,4096]{1,0:T(8,128)(2,1)} async-done(((bf16[256,512]{1,0:T(8,128)(2,1)}), bf16[256,4096]{1,0:T(8,128)(2,1)}) %all-gather.2.cloned.1.call-update) | async-done | bytes 2097168 | tf_op jit(solution)/shard_map/all_gather | solution.py:39
  90.8 4.9 multiply_convert_fusion.1
  95.7 3.7 collective-permute-start
  103.2 223.4 %while.21 = (s32[]{:T(128)}, f32[256,512]{1,0:T(8,128)S(1)}, f32[256,512]{1,0:T(8,128)S(1)}, f32[512,128]{0,1:T(8,128)}, bf16[383,512]{1,0:T(8,128)(2,1)S(1)}, /...) while((s32[]{:T(128)}, f32[256,512]{1,0:T(8,128)S(1)}, ...), condition=%wide.region_9.0_spmd.clone, body=%wide.region_0.0_spmd.clone.sunk | while | flops 9695315 | bytes 9028992 | solution.py:75
  103.9 1.3 dynamic_update_slice.104
  109.2 1.3 dynamic_update_slice.108
  110.6 1.3 dynamic_update_slice.109
  111.9 1.3 dynamic_update_slice.110
  118.0 1.3 dynamic_update_slice.104
  131.9 1.3 dynamic_update_slice.104
  146.0 1.3 dynamic_update_slice.104
  160.0 1.3 dynamic_update_slice.104
  173.9 1.3 dynamic_update_slice.104
  187.9 1.3 dynamic_update_slice.104
  201.8 1.3 dynamic_update_slice.104
  215.8 1.3 dynamic_update_slice.104
  229.7 1.3 dynamic_update_slice.104
  243.7 1.3 dynamic_update_slice.104
  257.6 1.3 dynamic_update_slice.104
  271.6 1.3 dynamic_update_slice.104
  285.6 1.3 dynamic_update_slice.104
  299.5 1.3 dynamic_update_slice.104
  313.5 1.3 dynamic_update_slice.104
  326.6 1.8 copy.25
  328.5 2.4 fusion.28
  330.9 4.5 convolution_bitcast_fusion
  335.5 5.5 convolution_bitcast_fusion.1
  342.8 259.3 %all-reduce.2.cloned.1.call-done = f32[512,128]{1,0:T(8,128)} async-done(((f32[512,128]{1,0:T(8,128)}), f32[512,128]{1,0:T(8,128)}) %all-reduce.2.cloned.1.call-update) | async-done | bytes 262160 | tf_op jit(solution)/shard_map/psum | solution.py:77
  602.0 1.7 broadcast_multiply_fusion
  603.7 157.9 %reduce-scatter.5.cloned.1.call-done = f32[128,512]{0,1:T(8,128)} async-done(((f32[4096,512]{0,1:T(8,128)}), f32[128,512]{0,1:T(8,128)}) %reduce-scatter.5.cloned.1.call-update) | async-done | bytes 262160 | tf_op jit(solution)/shard_map/reduce_scatter | solution.py:90
  763.4 130.1 %reduce-scatter.3.cloned.1.call-done = f32[512,256]{0,1:T(8,128)} async-done(((f32[4096,256]{0,1:T(8,128)}), f32[512,256]{0,1:T(8,128)}) %reduce-scatter.3.cloned.1.call-update) | async-done | bytes 524304 | tf_op jit(solution)/shard_map/reduce_scatter | solution.py:81
  (220 shorter events, 208.3 us)
Async XLA Ops:
  7.2 9.7 %copy-start.5 = (f32[256,4]{0,1:T(4,128)S(1)}, f32[256,4]{0,1:T(4,128)}, u32[]{:S(2)}) copy-start(f32[256,4]{0,1:T(4,128)} %param.19) | copy-start | bytes 12292
  7.2 9.8 %copy-start.6 = (f32[256,4]{0,1:T(4,128)S(1)}, f32[256,4]{0,1:T(4,128)}, u32[]{:S(2)}) copy-start(f32[256,4]{0,1:T(4,128)} %param.20) | copy-start | bytes 12292
  7.2 83.6 %copy-start.1 = (s32[256,512]{1,0:T(8,128)S(1)}, s32[256,512]{1,0:T(8,128)}, u32[]{:S(2)}) copy-start(s32[256,512]{1,0:T(8,128)} %param.18) | copy-start | bytes 1572868
  7.2 82.9 %all-gather.2.cloned.1.call-start = ((), (), s32[]{:S(2)}) async-start(), calls=%async_computation.2 | async-start | bytes 2359296 | tf_op jit(solution)/shard_map/all_gather | solution.py:39
  7.9 594.1 %all-reduce.2.cloned.1.call-start = ((), (), s32[]{:S(2)}) async-start(), calls=%async_computation.5 | async-start | bytes 524288 | tf_op jit(solution)/shard_map/psum | solution.py:77
  11.7 88.7 %collective-permute-start.1 = (bf16[127,512]{1,0:T(8,128)(2,1)S(1)}, bf16[127,512]{1,0:T(8,128)(2,1)}, u32[]{:S(2)}, u32[]{:S(2)}) collective-permute-start(bf16[127,512]{1,0:T(8,128)(2,1)S(1)} %slice.9), channel_id=1, source_target_pairs={{8,0},{16,8},{24,16},{32,24},{40,32},{48,40},{56,48},{64,56},{72,6... | collective-permute-start | bytes 390152 | tf_op jit(solution)/shard_map/ppermute | solution.py:12
  90.8 8.7 copy-start.4
  95.7 3.8 copy-start.2
  95.7 5.7 collective-permute-start
  328.4 433.2 %reduce-scatter.5.cloned.1.call-start = ((), (), s32[]{:S(2)}) async-start(), calls=%async_computation.4 | async-start | bytes 8650752 | tf_op jit(solution)/shard_map/reduce_scatter | solution.py:90
  328.5 2.4 copy-start
  335.5 558.0 %reduce-scatter.3.cloned.1.call-start = ((), (), s32[]{:S(2)}) async-start(), calls=%async_computation.3 | async-start | bytes 4718592 | tf_op jit(solution)/shard_map/reduce_scatter | solution.py:81
  341.0 0.9 copy-start.3
Sparse Core Ops, SparseCore 0:
  10.5 79.5 all-gather.1
  328.6 273.4 all-reduce.1
  604.8 156.7 reduce-scatter.4
  766.8 126.6 reduce-scatter.2
where the time goes:
time: 914 us; the launch traced here: 900 us
  waiting for transfers between devices  621 us (68%)
  local copies, waits for them, and re-layouts  195 us (21%)
  other arithmetic  44.1 us (5%)
  matrix products  14.9 us (2%)
  between operations  14 us (2%)
    psum x1, waiting for transfers between devices, shards(): grad_filter = lax.psum(filter_part, 'seq') * scale  259 us
    dynamic_update_slice x128, local copies, waits for them, and re-layouts, tap_block(): lax.dynamic_update_slice_in_dim(filter_part, column[:, None], index, 1)  171 us
    reduce_scatter x1, waiting for transfers between devices, shards(): lax.psum_scatter(lax.dot_general(full_input, grad_value, (((0,), (0,)), (...  158 us
    reduce_scatter x1, waiting for transfers between devices, shards(): lax.psum_scatter(lax.dot_general(value_weight, grad_value, (((1,), (1,)),...  130 us
    all_gather x1, waiting for transfers between devices, shards(): full_input = lax.all_gather(layer_input, 'tp', axis=1, tiled=True)  73 us
  transfers between devices with their start and end apart: 6, of which 5 were waited for; matrix products, arithmetic and copies ran while one was open for 3% of the time, Pallas kernels for 0%

commit v1 on v0

v1 whole, which is shorter than its diff:
```python
import functools
import math

import jax
import jax.numpy as jnp
from jax import lax
from jax.experimental import pallas as pl
from jax.experimental.pallas import tpu as pltpu
from jax.sharding import Mesh, PartitionSpec as P

SEQ = ("x", "zl", "core")
TP = ("y", "zh")
LANES = 128
BLOCK = 16
F32 = jnp.float32
BF16 = jnp.bfloat16
VMEM = pl.BlockSpec(memory_space=pltpu.VMEM)
SMEM = pl.BlockSpec(memory_space=pltpu.SMEM)
HBM = pl.BlockSpec(memory_space=pltpu.HBM)
COST = {"prepare": 1.75, "mix": 5.39, "weight": 2.8, "back": 2.59, "pair": 0.7, "split": 0.56, "product": 0.63, "merge": 1.05, "taps": 5.6, "last":0.5,"middle1": 0.35, "middle3":0.5,"middle4":0.5,"middle2": 0.35, "gather": 1.05, "conv": 5.88, "input": 0.56, "finish": 0.91, "ends": 0.91, "after": 0.35}
PARAMS = pltpu.CompilerParams(vmem_limit_bytes=40 * 1024 * 1024)
def room(used):
    return pltpu.CompilerParams(vmem_limit_bytes=int(used * 1024 * 1024))


def shifted(block, axis, k):
    n = lax.axis_size(axis)
    return lax.ppermute(block, axis, [(i, (i + k) % n) for i in range(n)])


def crossed(block, axis, d):
    return lax.ppermute(block, axis, [(i, i ^ d) for i in range(lax.axis_size(axis))])


def along_tokens(block, step):
    n = lax.axis_size(SEQ)
    return lax.ppermute(block, SEQ, [(i, i + step) for i in range(n) if 0 <= i + step < n])


def estimate(name):
    time = COST[name]
    return pl.CostEstimate(
        flops=int(time * 1e9), bytes_accessed=int(time * 3.3e6), transcendentals=0
    )


def staged(kernel, kinds):
    count = len(kinds)
    moved = [i for i, kind in enumerate(kinds) if kind == "in"]

    def body(*refs):
        inputs, rest = list(refs[:count]), list(refs[count:])
        held, sems = rest[len(rest) - len(moved) - 1 : -1], rest[-1]
        copies = [
            pltpu.make_async_copy(inputs[i], held[n], sems.at[n]) for n, i in enumerate(moved)
        ]
        for copy in copies:
            copy.start()
        for n, i in enumerate(moved):
            inputs[i] = held[n]
        for copy in copies:
            copy.wait()
        given = [r for r, kind in zip(inputs, kinds) if kind not in ("tie", "mark")]
        kernel(*given, *rest[: len(rest) - len(moved) - 1])

    return body


SPECS = {"in": HBM, "hbm": HBM, "tie": HBM, "vmem": VMEM, "mark": VMEM, "smem": SMEM}


def call(name, kernel, out, inputs, scratch=(), params=PARAMS):
    kinds = [kind for kind, _ in inputs]
    values = [value for _, value in inputs]
    moved = [v for kind, v in inputs if kind == "in"]
    scratch = list(scratch)
    if moved:
        kernel = staged(kernel, kinds)
        scratch += [pltpu.VMEM(v.shape, v.dtype) for v in moved]
        scratch += [pltpu.SemaphoreType.DMA((len(moved),))]
    else:
        inner, keep = kernel, [i for i, k in enumerate(kinds) if k not in ("tie", "mark")]
        count = len(kinds)

        def kernel(*refs):
            inner(*[refs[i] for i in keep], *refs[count:])

    return pl.pallas_call(
        kernel,
        out_shape=out,
        in_specs=[SPECS[kind] for kind in kinds],
        out_specs=jax.tree.map(lambda _: VMEM, out),
        scratch_shapes=scratch,
        compiler_params=params,
        cost_estimate=estimate(name),
        name=name,
    )(*values)


def after(block, *waits):
    kinds = [kind for kind, _ in waits]
    return pl.pallas_call(
        lambda *refs: None,
        out_shape=struct(block.shape, block.dtype),
        in_specs=[HBM] + [SPECS[kind] for kind in kinds],
        out_specs=HBM,
        input_output_aliases={0: 0},
        compiler_params=PARAMS,
        cost_estimate=estimate("after"),
        name="after",
    )(block, *[value for _, value in waits])


def struct(shape, dtype):
    return jax.ShapeDtypeStruct(shape, dtype)


def spread(natural, tile, wide, count, offset, span):
    @pl.loop(0, count // 8)
    def _(b):
        for i in range(8):
            s = b * 8 + i
            wide[s] = natural[tile, pl.ds(s + offset, 8, stride=span), :]


def convolve(wide, turned, natural_out, tile, span, causal):
    tap_count = turned.shape[1]
    for rb in range(span // BLOCK):

        def body(jb, acc):
            start = (rb - jb) * BLOCK + tap_count - BLOCK if causal else (rb + jb) * BLOCK
            window = [wide[start + i] for i in range(2 * BLOCK - 1)]
            acc = list(acc)
            for j in range(BLOCK):
                tap = jnp.broadcast_to(turned[tile, pl.ds(jb * BLOCK + j, 1), :], (8, LANES))
                for r in range(BLOCK):
                    acc[r] = acc[r] + tap * window[r - j + BLOCK - 1 if causal else r + j]
            return tuple(acc)

        zero = jnp.zeros((8, LANES), F32)
        acc = lax.fori_loop(0, tap_count // BLOCK, body, (zero,) * BLOCK)
        for r in range(BLOCK):
            natural_out[tile, pl.ds(rb * BLOCK + r, 8, stride=span), :] = acc[r]


def columns(low, high, codes, group):
    shape = (LANES, low.shape[1])
    bottom = jnp.broadcast_to(low[group : group + 1, :], shape).T
    step = jnp.broadcast_to((high[group : group + 1, :] - low[group : group + 1, :]) / 3.0, shape).T
    return bottom + codes[:, group * LANES : (group + 1) * LANES].astype(F32) * step


def prepare_kernel(up, codes, low, high, key_codes, key_low, key_high, taps, *outs):
    grad_conv, head, key, turned, mark = outs
    mark[...] = jnp.zeros_like(mark)
    for l in range(codes.shape[1] // LANES):
        cols = pl.ds(l * LANES, LANES)
        g = (up[:, cols].astype(F32) * columns(low, high, codes, l)).astype(BF16)
        grad_conv[:, cols] = g
        head[:, cols] = g[: head.shape[0]]
        key[:, cols] = columns(key_low, key_high, key_codes, l)
        turned[l] = taps[cols, :].astype(F32).T


def product_kernel(value, mix, key, product, tail, key_grad):
    p = (key[...] * value[...]).astype(BF16)
    product[...] = p
    tail[...] = p[p.shape[0] - tail.shape[0] :]
    key_grad[...] = mix[...] * value[...]


def mix_kernel(g, halo, turned, key, mix, value, turned_value, nat, wide, out):
    rows, channels = g.shape
    tiles, tap_count = channels // LANES, halo.shape[0]
    for l in range(tiles):
        cols = pl.ds(l * LANES, LANES)
        nat[l, pl.ds(0, rows), :] = g[:, cols].astype(F32)
        nat[l, pl.ds(rows, tap_count), :] = halo[:, cols].astype(F32)

    @pl.loop(0, tiles)
    def _(l):
        spread(nat, l, wide, wide.shape[0], 0, rows // 8)
        convolve(wide, turned, out, l, rows // 8, False)

    for l in range(tiles):
        cols = pl.ds(l * LANES, LANES)
        m = out[l]
        mix[:, cols] = m
        v = m * key[:, cols]
        value[:, cols] = v.astype(BF16)
        turned_value[cols, :] = v.T.astype(BF16)


def filter_kernel(place, p, halo, g, kept, given, mark, nat, nat_g, wide, wide_g, halves):
    mark[...] = jnp.zeros_like(mark)
    rows, channels = g.shape
    tiles, tap_count, span = channels // LANES, halo.shape[0], g.shape[0] // 8
    core, per_half = place[2], halo.shape[0] // 2 // BLOCK
    for l in range(tiles):
        cols = pl.ds(l * LANES, LANES)
        nat[l, pl.ds(0, tap_count), :] = halo[:, cols].astype(F32)
        nat[l, pl.ds(tap_count, rows), :] = p[:, cols].astype(F32)
        nat_g[l] = g[:, cols].astype(F32)

    for l in range(tiles):
        spread(nat, l, wide, wide.shape[0], 1, span)
        spread(nat_g, l, wide_g, span, 0, span)

        @pl.loop(0, tap_count // BLOCK)
        def _(jb):
            zero = jnp.zeros((8, LANES), F32)
            acc = [zero] * BLOCK
            for rb in range(span // BLOCK):
                start = (rb - jb) * BLOCK + tap_count - BLOCK
                window = [wide[start + i] for i in range(2 * BLOCK - 1)]
                for r in range(BLOCK):
                    up = wide_g[rb * BLOCK + r]
                    for j in range(BLOCK):
                        acc[j] = acc[j] + up * window[r - j + BLOCK - 1]
            rows_of = [jnp.sum(a, axis=0, keepdims=True) for a in acc]
            at = pl.ds(pl.multiple_of(lax.rem(jb, per_half) * BLOCK, BLOCK), BLOCK)
            half = lax.div(jb, per_half) ^ core
            halves[half, at, pl.ds(l * LANES, LANES)] = jnp.concatenate(rows_of, axis=0)

    kept[...] = halves[0]
    given[...] = halves[1]


def middle_kernel(kept, received, total, sent, mark):
    mark[...] = jnp.zeros_like(mark)
    total[...] = kept[...] + received[...].astype(F32)
    sent[...] = total[...].astype(BF16)


def conv_kernel(p, halo, upstream, turned, query_grad, mark, nat, wide, out):
    mark[...] = jnp.zeros_like(mark)
    rows, channels = p.shape
    tiles, tap_count = channels // LANES, halo.shape[0]
    for l in range(tiles):
        cols = pl.ds(l * LANES, LANES)
        nat[l, pl.ds(0, tap_count), :] = halo[:, cols].astype(F32)
        nat[l, pl.ds(tap_count, rows), :] = p[:, cols].astype(F32)

    @pl.loop(0, tiles)
    def _(l):
        spread(nat, l, wide, wide.shape[0], 1, rows // 8)
        convolve(wide, turned, out, l, rows // 8, True)

    for l in range(tiles):
        cols = pl.ds(l * LANES, LANES)
        query_grad[:, cols] = upstream[:, cols].astype(F32) * out[l]


def back_kernel(place, value, held_x, weight, keep, give, values, mark, held, sems):
    mark[...] = jnp.zeros_like(mark)
    x, y, zh = place[0], place[3], place[4]
    depth = held.shape[1]
    copies = []
    order = [(out, q, h) for out in (give, keep) for q in range(2) for h in range(2)]
    owners = [y ^ (1 if out is give else 0) ^ (3 if q else 0) for out, q, h in order]
    for i, (out, q, h) in enumerate(order):
        rows = pl.ds(pl.multiple_of((owners[i] * 2 + (zh ^ h)) * depth, depth), depth)
        copies.append(pltpu.make_async_copy(weight.at[rows, :], held.at[i], sems.at[i]))
    for copy in copies:
        copy.start()
    g = value[...]
    for i, (out, q, h) in enumerate(order):
        copies[i].wait()
        part = lax.dot_general(g, held[i], (((1,), (1,)), ((), ())), preferred_element_type=F32)
        out[q, :, h * depth : (h + 1) * depth] = part.astype(out.dtype)
        block = held_x[lax.rem(owners[i] - x + 4, 4) * 2 + h]
        part = jnp.dot(block, held[i], preferred_element_type=F32)
        values[...] = part if i == 0 else values[...] + part


def pair_kernel(keep, received, own, sent, mark):
    mark[...] = jnp.zeros_like(mark)
    own[...] = keep[0] + received[0].astype(F32)
    sent[...] = (keep[1] + received[1].astype(F32)).astype(BF16)


def split_kernel(own, received, passing, staying, mark):
    mark[...] = jnp.zeros_like(mark)
    width = staying.shape[1]
    for h, out in ((0, staying), (1, passing)):
        cols = pl.ds(h * width, width)
        out[...] = (own[:, cols] + received[:, cols].astype(F32)).astype(out.dtype)


def fetch(place, blocks, held, sems):
    waits = []
    for k in range(4):
        slot = lax.rem(place[3] - place[0] - k + 8, 4)
        for phase in range(2):
            i = 2 * k + phase
            for m in range(4):

                @pl.when(slot == m)
                def _():
                    pltpu.make_async_copy(blocks[4 * phase + m], held.at[i], sems.at[i]).start()

            waits.append(pltpu.make_async_copy(blocks[0], held.at[i], sems.at[i]))
    return waits


def weight_kernel(place, *refs):
    blocks, (value, keep, give, held, mark, sems) = refs[:8], refs[8:]
    mark[...] = jnp.zeros_like(mark)
    core = place[2]
    waits = fetch(place, blocks, held, sems)
    g = value[...]
    for i in range(8):
        waits[i].wait()
        part = jnp.dot(g, held[i], preferred_element_type=F32)
        for j in range(2):
            a = part[:, 2 * j * LANES : (2 * j + 1) * LANES]
            b = part[:, (2 * j + 1) * LANES : (2 * j + 2) * LANES]
            cols = pl.ds(((i % 2) * 2 + j) * LANES, LANES)
            keep[i // 2, :, cols] = jnp.where(core == 0, a, b)
            give[i // 2, :, cols] = jnp.where(core == 0, b, a).astype(BF16)


def merge_kernel(keep, received, r0, r1, r2, r3, mark):
    mark[...] = jnp.zeros_like(mark)
    for k, r in enumerate((r0, r1, r2, r3)):
        r[...] = (keep[k] + received[k].astype(F32)).astype(r.dtype)


def gather_kernel(place, r0, r1, r2, r3, own, a1, a2, a3, mark, total):
    mark[...] = jnp.zeros_like(mark)
    zl, zh = place[1], place[4]
    for q in range(4):
        cols = pl.ds(q * LANES, LANES)
        s = r0[:, cols]
        for r in (r1, r2, r3):
            s = s + r[:, cols].astype(F32)
        total[((zh ^ (q // 2)) * 2 + q % 2) ^ zl] = s
    own[...] = total[0]
    for d, a in enumerate((a1, a2, a3)):
        a[...] = total[d + 1].astype(BF16)


def finish_kernel(scale, own, r1, r2, r3, out):
    s = own[...]
    for r in (r1, r2, r3):
        s = s + r[...].astype(F32)
    out[...] = s.T * scale


def last_kernel(own, received, out):
    out[...] = own[...] + received[...].astype(F32)


def input_kernel(staying, arrived, out):
    out[...] = staying[...].astype(F32) + arrived[...].astype(F32)


def ends_kernel(scale, place, own, other, out, both):
    half = own.shape[0]
    both[pl.ds(pl.multiple_of(place[2] * half, half), half), :] = own[...]
    both[pl.ds(pl.multiple_of((1 - place[2]) * half, half), half), :] = other[...]
    out[...] = both[...].T * scale


def shards(
    layer_input,
    value_weight,
    filter_taps,
    query_codes,
    query_low,
    query_high,
    key_codes,
    key_low,
    key_high,
    out_grad,
):
    rows, width = layer_input.shape
    channels, tap_count = filter_taps.shape
    tiles, span = channels // LANES, rows // 8
    place = jnp.stack([lax.axis_index(axis) for axis in SEQ + TP]).astype(jnp.int32)
    scale = 1.0 / math.sqrt(rows * lax.axis_size(SEQ))

    mark = struct((8, LANES), F32)
    wide_shape = pltpu.VMEM((tap_count + span, 8, LANES), F32)
    nat_shape = pltpu.VMEM((tiles, rows + tap_count + 8, LANES), F32)
    out_scratch = pltpu.VMEM((tiles, rows, LANES), F32)
    plane = struct((rows, channels), F32)
    half_plane = struct((rows, channels), BF16)

    far = crossed(layer_input, "zh", 1)
    near_blocks = [layer_input] + [shifted(layer_input, "y", k) for k in (1, 2, 3)]
    grad_conv, head, key, turned, prepare_mark = call(
        "prepare",
        prepare_kernel,
        (
            half_plane,
            struct((tap_count, channels), BF16),
            plane,
            struct((tiles, tap_count, LANES), F32),
            mark,
        ),
        [("in", v) for v in (out_grad, query_codes, query_low.T, query_high.T)]
        + [("in", v) for v in (key_codes, key_low.T, key_high.T, filter_taps)],
        params=room(60),
    )
    later_rows = along_tokens(head, -1)
    far = after(far, *[("tie", b) for b in near_blocks[1:]], ("mark", prepare_mark))
    far_blocks = [far] + [shifted(far, "y", k) for k in (1, 2, 3)]
    grad_mix, grad_value, turned_value = call(
        "mix",
        mix_kernel,
        (plane, half_plane, struct((channels, rows), BF16)),
        [("in", grad_conv), ("in", later_rows), ("in", turned), ("in", key), ("tie", far)],
        [nat_shape, wide_shape, out_scratch],
        room(62.5),
    )

    eight = pltpu.SemaphoreType.DMA((8,))
    blocks = [("hbm", b) for b in near_blocks + far_blocks]
    keep, give, gathered, weight_mark = call(
        "weight",
        weight_kernel,
        (
            struct((4, channels, 4 * LANES), F32),
            struct((4, channels, 4 * LANES), BF16),
            struct((8, rows, width), BF16),
            mark,
        ),
        [("smem", place)] + blocks + [("vmem", turned_value)],
        [eight],
        room(40),
    )
    given_terms = crossed(give, "core", 1)
    back_keep, back_give, values, _ = call(
        "back",
        back_kernel,
        (
            struct((2, rows, 2 * width), F32),
            struct((2, rows, 2 * width), BF16),
            plane,
            mark,
        ),
        [("smem", place), ("vmem", grad_value), ("vmem", gathered), ("hbm", value_weight)]
        + [("mark", weight_mark)],
        [pltpu.VMEM((8, width, channels), BF16), eight],
        room(46),
    )
    product, tail, grad_key = call(
        "product",
        product_kernel,
        (half_plane, struct((tap_count, channels), BF16), plane),
        [("vmem", values), ("vmem", grad_mix), ("vmem", key)],
    )
    *terms, merge_mark = call(
        "merge",
        merge_kernel,
        (struct((channels, 4 * LANES), F32),)
        + (struct((channels, 4 * LANES), BF16),) * 3
        + (mark,),
        [("vmem", keep), ("in", given_terms)],
    )
    sent = [shifted(terms[k], "x", k) for k in (1, 2, 3)]
    earlier_rows = along_tokens(tail, 1)
    half_taps = struct((tap_count // 2, channels), F32)
    kept, given, taps_mark = call(
        "taps",
        filter_kernel,
        (half_taps, half_taps, mark),
        [("smem", place), ("vmem", product), ("in", earlier_rows), ("vmem", grad_conv)]
        + [("mark", merge_mark)],
        [
            nat_shape,
            out_scratch,
            wide_shape,
            pltpu.VMEM((span, 8, LANES), F32),
            pltpu.VMEM((2, tap_count // 2, channels), F32),
        ],
    )
    filter_sum, filter_sent, middle1_mark = call(
        "middle1",
        middle_kernel,
        (half_taps, struct((tap_count // 2, channels), BF16), mark),
        [("vmem", kept), ("in", crossed(given, "core", 1))],
    )
    back_own, back_sent, pair_mark = call(
        "pair",
        pair_kernel,
        (struct((rows, 2 * width), F32), struct((rows, 2 * width), BF16), mark),
        [("vmem", back_keep), ("in", crossed(back_give, "y", 1)), ("mark", middle1_mark)],
    )
    passing, staying, split_mark = call(
        "split",
        split_kernel,
        (struct((rows, width), BF16), struct((rows, width), F32), mark),
        [("vmem", back_own), ("in", crossed(back_sent, "y", 3))],
    )
    arrived_input = crossed(passing, "zh", 1)
    own, *ahead, gather_mark = call(
        "gather",
        gather_kernel,
        (struct((channels, LANES), F32),)
        + (struct((channels, LANES), BF16),) * 3
        + (mark,),
        [("smem", place), ("vmem", terms[0])]
        + [("in", v) for v in sent],
        [pltpu.VMEM((4, channels, LANES), F32)],
    )
    arrived = [crossed(ahead[d - 1], "zl", d) for d in (1, 2, 3)]
    grad_query, conv_mark = call(
        "conv",
        conv_kernel,
        (plane, mark),
        [("vmem", product), ("in", earlier_rows), ("in", out_grad), ("vmem", turned)]
        + [("mark", gather_mark), ("mark", split_mark)],
        [nat_shape, wide_shape, out_scratch],
    )
    filter_sum, filter_sent, middle2_mark = call(
        "middle2",
        middle_kernel,
        (half_taps, struct((tap_count // 2, channels), BF16), mark),
        [("vmem", filter_sum), ("in", crossed(filter_sent, "zl", 1))],
    )
    filter_sum, filter_sent, middle3_mark = call(
        "middle3",
        middle_kernel,
        (half_taps, struct((tap_count // 2, channels), BF16), mark),
        [("vmem", filter_sum), ("in", crossed(filter_sent, "zl", 2))]
        + [("mark", gather_mark)],
    )
    filter_sum, filter_sent, middle4_mark = call(
        "middle4",
        middle_kernel,
        (half_taps, struct((tap_count // 2, channels), BF16), mark),
        [("vmem", filter_sum), ("in", crossed(filter_sent, "x", 1))],
    )
    filter_sum = call(
        "last",
        last_kernel,
        half_taps,
        [("vmem", filter_sum), ("in", crossed(filter_sent, "x", 3))]
        + [("tie", v) for v in arrived]
        + [("mark", conv_mark)],
    )
    grad_input = call(
        "input",
        input_kernel,
        struct((rows, width), F32),
        [("vmem", staying), ("in", arrived_input)],
    )
    grad_weight = call(
        "finish",
        functools.partial(finish_kernel, scale),
        struct((LANES, channels), F32),
        [("vmem", own)]
        + [("in", v) for v in arrived]
        + [("mark", conv_mark)],
    )
    grad_filter = call(
        "ends",
        functools.partial(ends_kernel, scale),
        struct((channels, tap_count), F32),
        [("smem", place), ("vmem", filter_sum), ("in", crossed(filter_sum, "core", 1))],
        [pltpu.VMEM((tap_count, channels), F32)],
    )
    return (grad_input, grad_weight, grad_filter, grad_query, grad_key)


def solution(mesh):
    fine = Mesh(mesh.devices.reshape(4, 4, 2, 4, 2), SEQ + TP)
    both = P(SEQ, TP)
    return jax.shard_map(
        shards,
        mesh=fine,
        in_specs=(both, P(None, TP), P(TP, None)) + (both,) * 7,
        out_specs=(both, both, P(TP, None), both, both),
        check_vma=False,
    )
```

time: 914 us -> 123 us (0.13); the launches traced: 900 us -> 122 us
  waiting for transfers between devices: 621 us -> 10.5 us
  local copies, waits for them, and re-layouts: 195 us -> 3.35 us
  starting transfers between devices: 9.05 us -> 59.8 us
  Pallas kernels: 0 us -> 47.4 us
  other arithmetic: 44.1 us -> 0 us
  matrix products: 14.9 us -> 0 us
  between operations: 14 us -> 1.16 us
    reduce_scatter x2 -> x0, waiting for transfers between devices: 288 us -> none  [the longest x1 158 us: shards(): lax.psum_scatter(lax.dot_general(full_input, grad_value, (((0,), (0,)), (...]
    psum x1 -> x0, waiting for transfers between devices: 259 us -> none  [shards(): grad_filter = lax.psum(filter_part, 'seq') * scale]
    dynamic_update_slice x128 -> x0, local copies, waits for them, and re-layouts: 171 us -> none  [tap_block(): lax.dynamic_update_slice_in_dim(filter_part, column[:, None], index, 1)]
    all_gather x1 -> x0, waiting for transfers between devices: 73 us -> none  [shards(): full_input = lax.all_gather(layer_input, 'tp', axis=1, tiled=True)]
    ppermute x2 -> x25, starting transfers between devices: 8.89 us -> 59.8 us  [the longest x14 37.1 us: crossed(): lax.ppermute(block, axis, [(i, i ^ d) for i in range(lax.axis_size(axis))])]
    pallas_call x0 -> x20, Pallas kernels: none -> 47.4 us  [the longest x19 47.4 us: call(): pl.pallas_call(kernel, out_shape=out, in_specs=[SPECS[kind] for kind in k...]
    add x32 -> x0, other arithmetic: 22.1 us -> none  [the longest x16 11.1 us: tap_block(): grad_mix = grad_mix + later * tap_column[None, :]]
    dynamic_slice x16 -> x0, local copies, waits for them, and re-layouts: 16.6 us -> none  [tap_block(): tap_column = lax.dynamic_slice_in_dim(taps_wide, index, 1, 1)[:, 0]]
  transfers between devices with their start and end apart: 6 -> 25, of which waited for: 5 -> 5; matrix products, arithmetic and copies ran while one was open for 3% -> 0% of each run, Pallas kernels for 0% -> 35%
where the time goes in v1:
time: 123 us; the launch traced here: 122 us
  starting transfers between devices  59.8 us (49%)
  Pallas kernels  47.4 us (39%)
  waiting for transfers between devices  10.5 us (9%)
  local copies, waits for them, and re-layouts  3.35 us (3%)
    pallas_call x19, Pallas kernels, call(): pl.pallas_call(kernel, out_shape=out, in_specs=[SPECS[kind] for kind in k...  47.4 us
    ppermute x14, starting transfers between devices, crossed(): lax.ppermute(block, axis, [(i, i ^ d) for i in range(lax.axis_size(axis))])  37.1 us
    ppermute x9, starting transfers between devices, shifted(): return lax.ppermute(block, axis, [(i, (i + k) % n) for i in range(n)])  13.8 us
    ppermute x2, starting transfers between devices, along_tokens(): lax.ppermute(block, SEQ, [(i, i + step) for i in range(n) if 0 <= i + ste...  8.94 us
    ppermute x14, waiting for transfers between devices, crossed(): lax.ppermute(block, axis, [(i, i ^ d) for i in range(lax.axis_size(axis))])  5.82 us
    ppermute x2, waiting for transfers between devices, along_tokens(): lax.ppermute(block, SEQ, [(i, i + step) for i in range(n) if 0 <= i + ste...  4.66 us
    unnamed x24, local copies, waits for them, and re-layouts  3.26 us
  transfers between devices with their start and end apart: 25, of which 5 were waited for; matrix products, arithmetic and copies ran while one was open for 0% of the time, Pallas kernels for 35%

profile of v1, /device:TPU:1, one launch (start us, length us, event | category | flops | bytes accessed | tf_op | source)
XLA Modules:
  0.0 122.2 jit_solution(7926509276540587231)
XLA Ops:
  0.6 2.2 %collective-permute-start.2 = (bf16[256,512]{1,0:T(8,128)(2,1)}, bf16[256,512]{1,0:T(8,128)(2,1)S(1)}, u32[]{:S(2)}, u32[]{:S(2)}) collective-permute-start(bf16[256,512]{1,0:T(8,128)(2,1)} %refs_1_.3), channel_id=1, source_target_pairs={{0,2},{2,4},{4,6},{6,0},{1,3},{3,5},{5,7},{7,1},{8,10},{10,12},{12... | collective-permute-start | bytes 786440 | tf_op jit(solution)/shard_map/ppermute | solution.py:28
  2.8 2.6 %collective-permute-start.3 = (bf16[256,512]{1,0:T(8,128)(2,1)}, bf16[256,512]{1,0:T(8,128)(2,1)S(1)}, u32[]{:S(2)}, u32[]{:S(2)}) collective-permute-start(bf16[256,512]{1,0:T(8,128)(2,1)} %refs_1_.3), channel_id=1, source_target_pairs={{0,4},{2,6},{4,0},{6,2},{1,5},{3,7},{5,1},{7,3},{8,12},{10,14},{12... | collective-permute-start | bytes 786440 | tf_op jit(solution)/shard_map/ppermute | solution.py:28
  5.5 1.1 collective-permute-start.4
  6.5 6.9 %collective-permute-start.1 = (bf16[256,512]{1,0:T(8,128)(2,1)}, bf16[256,512]{1,0:T(8,128)(2,1)S(1)}, u32[]{:S(2)}, u32[]{:S(2)}) collective-permute-start(bf16[256,512]{1,0:T(8,128)(2,1)} %refs_1_.3), channel_id=1, source_target_pairs={{0,1},{1,0},{2,3},{3,2},{4,5},{5,4},{6,7},{7,6},{8,9},{9,8},{10,11... | collective-permute-start | bytes 786440 | tf_op jit(solution)/shard_map/ppermute | solution.py:32
  13.4 2.9 %prepare.1 = (bf16[256,512]{1,0:T(8,128)(2,1)}, bf16[128,512]{1,0:T(8,128)(2,1)}, f32[256,512]{1,0:T(8,128)}, f32[4,128,128]{2,1,0:T(8,128)}, f32[8,128]{1,0:T(8,128)}) custom-call(bf16[256,512]{1,0:T(8,128)(2,1)} %refs_2_.1, s32[256,512]{1,0:T(8,128)} %refs_1_.2, f32[4,256]{1,0:T(4,128)} %bitcast.9, f32[4,256]{1,0:T(4,128)} %bitcast.10, ...), custom_call_target="tpu_custom_call" | custom-call | flops 1750000000 | bytes 5775000 | tf_op jit(solution)/shard_map/prepare/pallas_call | solution.py:88
  16.4 3.7 %collective-permute-start = (bf16[128,512]{1,0:T(8,128)(2,1)}, bf16[128,512]{1,0:T(8,128)(2,1)S(1)}, u32[]{:S(2)}, u32[]{:S(2)}) collective-permute-start(bf16[128,512]{1,0:T(8,128)(2,1)} %get-tuple-element.52), channel_id=1, source_target_pairs={{8,0},{16,8},{24,16},{32,24},{40,32},{48,40},{56,48},{64,56},{72,6... | collective-permute-start | bytes 393224 | tf_op jit(solution)/shard_map/ppermute | solution.py:37
  21.8 1.9 %collective-permute-start.7 = (bf16[256,512]{1,0:T(8,128)(2,1)S(1)}, bf16[256,512]{1,0:T(8,128)(2,1)}, u32[]{:S(2)}, u32[]{:S(2)}) collective-permute-start(bf16[256,512]{1,0:T(8,128)(2,1)S(1)} %after.1.refs_4_.refs_5_), channel_id=1, source_target_pairs={{0,6},{2,0},{4,2},{6,4},{1,7},{3,1},{5,3},{7,5},{8,14},{10,8},{12,... | collective-permute-start | bytes 786440 | tf_op jit(solution)/shard_map/ppermute | solution.py:28
  23.7 4.7 %collective-permute-done.refs_1_ = bf16[128,512]{1,0:T(8,128)(2,1)S(1)} collective-permute-done((bf16[128,512]{1,0:T(8,128)(2,1)}, bf16[128,512]{1,0:T(8,128)(2,1)S(1)}, u32[]{:S(2)}, u32[]{:S(2)}) %collective-permute-start) | collective-permute-done | bytes 131104 | tf_op jit(solution)/shard_map/ppermute | solution.py:37
  29.0 9.6 %mix.1 = (f32[256,512]{1,0:T(8,128)}, bf16[256,512]{1,0:T(8,128)(2,1)}, bf16[512,256]{1,0:T(8,128)(2,1)}) custom-call(bf16[256,512]{1,0:T(8,128)(2,1)} %get-tuple-element.51.refs_0_.refs_3_, bf16[128,512]{1,0:T(8,128)(2,1)} %copy-done.11, f32[4,128,128]{2,1,0:T(8,128)} %get-tuple-element.53.refs_2_.refs_3_, f32[256,512]{1,0:T(8,128)} %get-tuple-element.54.refs_3_.refs_2_, ...), custom_call_target="tpu_custom_call" | custom-call | flops 5390000128 | bytes 17787000 | tf_op jit(solution)/shard_map/mix/pallas_call | solution.py:88
  40.6 3.3 %weight.1 = (f32[4,512,512]{2,1,0:T(8,128)S(1)}, bf16[4,512,512]{2,1,0:T(8,128)(2,1)S(1)}, bf16[8,256,512]{2,1,0:T(8,128)(2,1)S(1)}, f32[8,128]{1,0:T(8,128)S(1)}) custom-call(s32[5]{0:T(128)S(1)} %stack.23.refs_0_, bf16[256,512]{1,0:T(8,128)(2,1)S(1)} %copy-done.3, bf16[256,512]{1,0:T(8,128)(2,1)S(1)} %collective-permute-done.2.refs_1_.refs_2_, ...), custom_call_target="tpu_custom_call" | custom-call | flops 2800000000 | bytes 9240000 | tf_op jit(solution)/shard_map/weight/pallas_call | solution.py:88
  44.0 5.1 %back.1 = (f32[2,256,1024]{2,1,0:T(8,128)S(1)}, bf16[2,256,1024]{2,1,0:T(8,128)(2,1)S(1)}, f32[256,512]{1,0:T(8,128)S(1)}, f32[8,128]{1,0:T(8,128)}) custom-call(s32[5]{0:T(128)S(1)} %stack.23.refs_0_, bf16[256,512]{1,0:T(8,128)(2,1)S(1)} %copy-done.7, bf16[8,256,512]{2,1,0:T(8,128)(2,1)S(1)} %get-tuple-element.58.refs_2_, bf16[4096,512]{1,0:T(8,128)(2,1)} %refs_3_.1, ...), custom_call_target="tpu_custom_call" | custom-call | flops 2590000128 | bytes 8547000 | tf_op jit(solution)/shard_map/back/pallas_call | solution.py:88
  51.0 5.2 %collective-permute-start.9 = (bf16[128,512]{1,0:T(8,128)(2,1)S(1)}, bf16[128,512]{1,0:T(8,128)(2,1)S(1)}, u32[]{:S(2)}, u32[]{:S(2)}) collective-permute-start(bf16[128,512]{1,0:T(8,128)(2,1)S(1)} %get-tuple-element.65), channel_id=1, source_target_pairs={{0,8},{8,16},{16,24},{24,32},{32,40},{40,48},{48,56},{56,64},{64,7... | collective-permute-start | bytes 393224 | tf_op jit(solution)/shard_map/ppermute | solution.py:37
  57.9 2.9 %collective-permute-start.15 = (bf16[512,512]{1,0:T(8,128)(2,1)S(1)}, bf16[512,512]{1,0:T(8,128)(2,1)S(1)}, u32[]{:S(2)}, u32[]{:S(2)}) collective-permute-start(bf16[512,512]{1,0:T(8,128)(2,1)S(1)} %get-tuple-element.78), channel_id=1, source_target_pairs={{0,128},{64,192},{128,0},{192,64},{1,129},{65,193},{129,1},{193,65... | collective-permute-start | bytes 1572872 | tf_op jit(solution)/shard_map/ppermute | solution.py:28
  60.9 1.1 collective-permute-start.16
  62.0 8.5 %taps.1 = (f32[64,512]{1,0:T(8,128)S(1)}, f32[64,512]{1,0:T(8,128)S(1)}, f32[8,128]{1,0:T(8,128)}) custom-call(s32[5]{0:T(128)S(1)} %stack.23.refs_0_, bf16[256,512]{1,0:T(8,128)(2,1)S(1)} %get-tuple-element.64.refs_1_.refs_0_, bf16[128,512]{1,0:T(8,128)(2,1)S(1)} %collective-permute-done.9.refs_2_.refs_1_, bf16[256,512]{1,0:T(8,128)(2,1)S(1)} %copy-done.9, ...), custom_call_target="tpu_custom_call" | custom-call | flops 5600000000 | bytes 18480000 | tf_op jit(solution)/shard_map/taps/pallas_call | solution.py:88
  70.6 1.3 %collective-permute-done.11.refs_1_ = f32[64,512]{1,0:T(8,128)S(1)} collective-permute-done((f32[64,512]{1,0:T(8,128)S(1)}, f32[64,512]{1,0:T(8,128)S(1)}, u32[]{:S(2)}, u32[]{:S(2)}) %collective-permute-start.11) | collective-permute-done | bytes 131104 | tf_op jit(solution)/shard_map/ppermute | solution.py:32
  72.1 1.4 %collective-permute-done.8.refs_1_ = bf16[2,256,1024]{2,1,0:T(8,128)(2,1)S(1)} collective-permute-done((bf16[2,256,1024]{2,1,0:T(8,128)(2,1)S(1)}, bf16[2,256,1024]{2,1,0:T(8,128)(2,1)S(1)}, u32[]{:S(2)}, u32[]{:S(2)}) %collective-permute-start.8) | collective-permute-done | bytes 1048608 | tf_op jit(solution)/shard_map/ppermute | solution.py:32
  74.1 1.6 %collective-permute-start.12 = (bf16[256,1024]{1,0:T(8,128)(2,1)S(1)}, bf16[256,1024]{1,0:T(8,128)(2,1)S(1)}, u32[]{:S(2)}, u32[]{:S(2)}) collective-permute-start(bf16[256,1024]{1,0:T(8,128)(2,1)S(1)} %get-tuple-element.73), channel_id=1, source_target_pairs={{0,6},{2,4},{4,2},{6,0},{1,7},{3,5},{5,3},{7,1},{8,14},{10,12},{12... | collective-permute-start | bytes 1572872 | tf_op jit(solution)/shard_map/ppermute | solution.py:32
  75.8 4.0 %collective-permute-start.20 = (bf16[64,512]{1,0:T(8,128)(2,1)S(1)}, bf16[64,512]{1,0:T(8,128)(2,1)S(1)}, u32[]{:S(2)}, u32[]{:S(2)}) collective-permute-start(bf16[64,512]{1,0:T(8,128)(2,1)S(1)} %get-tuple-element.88), channel_id=1, source_target_pairs={{0,16},{16,0},{32,48},{48,32},{1,17},{17,1},{33,49},{49,33},{2,18}... | collective-permute-start | bytes 196616 | tf_op jit(solution)/shard_map/ppermute | solution.py:32
  79.7 1.9 %collective-permute-done.20.refs_1_ = bf16[64,512]{1,0:T(8,128)(2,1)S(1)} collective-permute-done((bf16[64,512]{1,0:T(8,128)(2,1)S(1)}, bf16[64,512]{1,0:T(8,128)(2,1)S(1)}, u32[]{:S(2)}, u32[]{:S(2)}) %collective-permute-start.20) | collective-permute-done | bytes 65568 | tf_op jit(solution)/shard_map/ppermute | solution.py:32
  82.3 4.1 %collective-permute-start.21 = (bf16[64,512]{1,0:T(8,128)(2,1)S(1)}, bf16[64,512]{1,0:T(8,128)(2,1)S(1)}, u32[]{:S(2)}, u32[]{:S(2)}) collective-permute-start(bf16[64,512]{1,0:T(8,128)(2,1)S(1)} %get-tuple-element.90), channel_id=1, source_target_pairs={{0,32},{16,48},{32,0},{48,16},{1,33},{17,49},{33,1},{49,17},{2,34}... | collective-permute-start | bytes 196616 | tf_op jit(solution)/shard_map/ppermute | solution.py:32
  86.5 1.2 gather.1
  87.7 1.2 collective-permute-done.21.refs_1_
  89.5 2.4 %collective-permute-start.22 = (bf16[64,512]{1,0:T(8,128)(2,1)S(1)}, bf16[64,512]{1,0:T(8,128)(2,1)S(1)}, u32[]{:S(2)}, u32[]{:S(2)}) collective-permute-start(bf16[64,512]{1,0:T(8,128)(2,1)S(1)} %get-tuple-element.92), channel_id=1, source_target_pairs={{0,64},{64,0},{128,192},{192,128},{1,65},{65,1},{129,193},{193,129... | collective-permute-start | bytes 196616 | tf_op jit(solution)/shard_map/ppermute | solution.py:32
  91.9 2.2 %collective-permute-start.18 = (bf16[512,128]{1,0:T(8,128)(2,1)S(1)}, bf16[512,128]{1,0:T(8,128)(2,1)S(1)}, u32[]{:S(2)}, u32[]{:S(2)}) collective-permute-start(bf16[512,128]{1,0:T(8,128)(2,1)S(1)} %get-tuple-element.82), channel_id=1, source_target_pairs={{0,32},{16,48},{32,0},{48,16},{1,33},{17,49},{33,1},{49,17},{2,34}... | collective-permute-start | bytes 393224 | tf_op jit(solution)/shard_map/ppermute | solution.py:32
  94.2 1.3 %collective-permute-start.19 = (bf16[512,128]{1,0:T(8,128)(2,1)S(1)}, bf16[512,128]{1,0:T(8,128)(2,1)S(1)}, u32[]{:S(2)}, u32[]{:S(2)}) collective-permute-start(bf16[512,128]{1,0:T(8,128)(2,1)S(1)} %get-tuple-element.83), channel_id=1, source_target_pairs={{0,48},{16,32},{32,16},{48,0},{1,49},{17,33},{33,17},{49,1},{2,50}... | collective-permute-start | bytes 393224 | tf_op jit(solution)/shard_map/ppermute | solution.py:32
  96.1 1.9 %collective-permute-start.23 = (bf16[64,512]{1,0:T(8,128)(2,1)S(1)}, bf16[64,512]{1,0:T(8,128)(2,1)S(1)}, u32[]{:S(2)}, u32[]{:S(2)}) collective-permute-start(bf16[64,512]{1,0:T(8,128)(2,1)S(1)} %get-tuple-element.94), channel_id=1, source_target_pairs={{0,192},{64,128},{128,64},{192,0},{1,193},{65,129},{129,65},{193,1... | collective-permute-start | bytes 196616 | tf_op jit(solution)/shard_map/ppermute | solution.py:32
  98.2 5.1 %collective-permute-start.13 = (bf16[256,512]{1,0:T(8,128)(2,1)S(1)}, bf16[256,512]{1,0:T(8,128)(2,1)S(1)}, u32[]{:S(2)}, u32[]{:S(2)}) collective-permute-start(bf16[256,512]{1,0:T(8,128)(2,1)S(1)} %get-tuple-element.75), channel_id=1, source_target_pairs={{0,1},{1,0},{2,3},{3,2},{4,5},{5,4},{6,7},{7,6},{8,9},{9,8},{10,11... | collective-permute-start | bytes 786440 | tf_op jit(solution)/shard_map/ppermute | solution.py:32
  103.3 8.3 %conv.1 = (f32[256,512]{1,0:T(8,128)}, f32[8,128]{1,0:T(8,128)S(1)}) custom-call(bf16[256,512]{1,0:T(8,128)(2,1)S(1)} %get-tuple-element.64.refs_1_.refs_0_, bf16[128,512]{1,0:T(8,128)(2,1)S(1)} %collective-permute-done.9.refs_2_.refs_1_, bf16[256,512]{1,0:T(8,128)(2,1)S(1)} %copy-done.4, f32[4,128,128]{2,1,0:T(8,128)S(1)} %copy-done.8, ...), custom_call_target="tpu_custom_call" | custom-call | flops 5880000000 | bytes 19404000 | tf_op jit(solution)/shard_map/conv/pallas_call | solution.py:88
  111.8 6.4 %collective-permute-start.24 = (f32[64,512]{1,0:T(8,128)S(1)}, f32[64,512]{1,0:T(8,128)S(1)}, u32[]{:S(2)}, u32[]{:S(2)}) collective-permute-start(f32[64,512]{1,0:T(8,128)S(1)} %last.1.refs_1_), channel_id=1, source_target_pairs={{0,8},{8,0},{1,9},{9,1},{2,10},{10,2},{3,11},{11,3},{4,12},{12,4},... | collective-permute-start | bytes 393224 | tf_op jit(solution)/shard_map/ppermute | solution.py:32
  118.2 1.4 %finish.1 = f32[128,512]{1,0:T(8,128)} custom-call(f32[512,128]{1,0:T(8,128)S(1)} %get-tuple-element.80.refs_0_, bf16[512,128]{1,0:T(8,128)(2,1)S(1)} %collective-permute-done.17.refs_1_.refs_2_, bf16[512,128]{1,0:T(8,128)(2,1)S(1)} %collective-permute-done.18.refs_2_.refs_3_, bf16[512,128]{1,0:T(8,128)(2,1)S(1)} %collective-permute-done.19.refs_3_.refs_4_, ...), custom_call_target="tpu_custom_call" | custom-call | flops 910000000 | bytes 3003000 | tf_op jit(solution)/shard_map/finish/pallas_call | solution.py:88
  119.6 1.6 %ends.1 = f32[512,128]{1,0:T(8,128)} custom-call(s32[5]{0:T(128)S(1)} %stack.23.refs_0_, f32[64,512]{1,0:T(8,128)S(1)} %last.1.refs_1_, f32[64,512]{1,0:T(8,128)S(1)} %collective-permute-done.24.refs_2_), custom_call_target="tpu_custom_call" | custom-call | flops 910000000 | bytes 3003000 | tf_op jit(solution)/shard_map/ends/pallas_call | solution.py:88
  (63 shorter events, 12.0 us)
Async XLA Ops:
  0.6 19.6 %collective-permute-start.2 = (bf16[256,512]{1,0:T(8,128)(2,1)}, bf16[256,512]{1,0:T(8,128)(2,1)S(1)}, u32[]{:S(2)}, u32[]{:S(2)}) collective-permute-start(bf16[256,512]{1,0:T(8,128)(2,1)} %refs_1_.3), channel_id=1, source_target_pairs={{0,2},{2,4},{4,6},{6,0},{1,3},{3,5},{5,7},{7,1},{8,10},{10,12},{12... | collective-permute-start | bytes 786440 | tf_op jit(solution)/shard_map/ppermute | solution.py:28
  2.8 17.4 %collective-permute-start.3 = (bf16[256,512]{1,0:T(8,128)(2,1)}, bf16[256,512]{1,0:T(8,128)(2,1)S(1)}, u32[]{:S(2)}, u32[]{:S(2)}) collective-permute-start(bf16[256,512]{1,0:T(8,128)(2,1)} %refs_1_.3), channel_id=1, source_target_pairs={{0,4},{2,6},{4,0},{6,2},{1,5},{3,7},{5,1},{7,3},{8,12},{10,14},{12... | collective-permute-start | bytes 786440 | tf_op jit(solution)/shard_map/ppermute | solution.py:28
  5.5 14.7 %collective-permute-start.4 = (bf16[256,512]{1,0:T(8,128)(2,1)}, bf16[256,512]{1,0:T(8,128)(2,1)S(1)}, u32[]{:S(2)}, u32[]{:S(2)}) collective-permute-start(bf16[256,512]{1,0:T(8,128)(2,1)} %refs_1_.3), channel_id=1, source_target_pairs={{0,6},{2,0},{4,2},{6,4},{1,7},{3,1},{5,3},{7,5},{8,14},{10,8},{12,... | collective-permute-start | bytes 786440 | tf_op jit(solution)/shard_map/ppermute | solution.py:28
  6.5 13.7 %collective-permute-start.1 = (bf16[256,512]{1,0:T(8,128)(2,1)}, bf16[256,512]{1,0:T(8,128)(2,1)S(1)}, u32[]{:S(2)}, u32[]{:S(2)}) collective-permute-start(bf16[256,512]{1,0:T(8,128)(2,1)} %refs_1_.3), channel_id=1, source_target_pairs={{0,1},{1,0},{2,3},{3,2},{4,5},{5,4},{6,7},{7,6},{8,9},{9,8},{10,11... | collective-permute-start | bytes 786440 | tf_op jit(solution)/shard_map/ppermute | solution.py:32
  16.4 12.0 %collective-permute-start = (bf16[128,512]{1,0:T(8,128)(2,1)}, bf16[128,512]{1,0:T(8,128)(2,1)S(1)}, u32[]{:S(2)}, u32[]{:S(2)}) collective-permute-start(bf16[128,512]{1,0:T(8,128)(2,1)} %get-tuple-element.52), channel_id=1, source_target_pairs={{8,0},{16,8},{24,16},{32,24},{40,32},{48,40},{56,48},{64,56},{72,6... | collective-permute-start | bytes 393224 | tf_op jit(solution)/shard_map/ppermute | solution.py:37
  20.9 7.5 %copy-start = (bf16[256,512]{1,0:T(8,128)(2,1)}, bf16[256,512]{1,0:T(8,128)(2,1)S(1)}, u32[]{:S(2)}) copy-start(bf16[256,512]{1,0:T(8,128)(2,1)S(1)} %after.1.refs_4_.refs_5_) | copy-start | bytes 786436
  20.9 17.8 %collective-permute-start.5 = (bf16[256,512]{1,0:T(8,128)(2,1)S(1)}, bf16[256,512]{1,0:T(8,128)(2,1)}, u32[]{:S(2)}, u32[]{:S(2)}) collective-permute-start(bf16[256,512]{1,0:T(8,128)(2,1)S(1)} %after.1.refs_4_.refs_5_), channel_id=1, source_target_pairs={{0,2},{2,4},{4,6},{6,0},{1,3},{3,5},{5,7},{7,1},{8,10},{10,12},{12... | collective-permute-start | bytes 786440 | tf_op jit(solution)/shard_map/ppermute | solution.py:28
  21.3 17.4 %collective-permute-start.6 = (bf16[256,512]{1,0:T(8,128)(2,1)S(1)}, bf16[256,512]{1,0:T(8,128)(2,1)}, u32[]{:S(2)}, u32[]{:S(2)}) collective-permute-start(bf16[256,512]{1,0:T(8,128)(2,1)S(1)} %after.1.refs_4_.refs_5_), channel_id=1, source_target_pairs={{0,4},{2,6},{4,0},{6,2},{1,5},{3,7},{5,1},{7,3},{8,12},{10,14},{12... | collective-permute-start | bytes 786440 | tf_op jit(solution)/shard_map/ppermute | solution.py:28
  21.8 16.9 %collective-permute-start.7 = (bf16[256,512]{1,0:T(8,128)(2,1)S(1)}, bf16[256,512]{1,0:T(8,128)(2,1)}, u32[]{:S(2)}, u32[]{:S(2)}) collective-permute-start(bf16[256,512]{1,0:T(8,128)(2,1)S(1)} %after.1.refs_4_.refs_5_), channel_id=1, source_target_pairs={{0,6},{2,0},{4,2},{6,4},{1,7},{3,1},{5,3},{7,5},{8,14},{10,8},{12,... | collective-permute-start | bytes 786440 | tf_op jit(solution)/shard_map/ppermute | solution.py:28
  29.0 9.7 %copy-start.3 = (bf16[256,512]{1,0:T(8,128)(2,1)S(1)}, bf16[256,512]{1,0:T(8,128)(2,1)}, u32[]{:S(2)}) copy-start(bf16[256,512]{1,0:T(8,128)(2,1)} %refs_1_.3) | copy-start | bytes 786436
  43.9 12.3 %collective-permute-start.10 = (bf16[4,512,512]{2,1,0:T(8,128)(2,1)S(1)}, bf16[4,512,512]{2,1,0:T(8,128)(2,1)S(1)}, u32[]{:S(2)}, u32[]{:S(2)}) collective-permute-start(bf16[4,512,512]{2,1,0:T(8,128)(2,1)S(1)} %get-tuple-element.67), channel_id=1, source_target_pairs={{0,8},{8,0},{1,9},{9,1},{2,10},{10,2},{3,11},{11,3},{4,12},{12,4},... | collective-permute-start | bytes 6291464 | tf_op jit(solution)/shard_map/ppermute | solution.py:32
  44.0 6.1 %copy-start.5 = (f32[256,512]{1,0:T(8,128)S(1)}, f32[256,512]{1,0:T(8,128)}, u32[]{:S(2)}) copy-start(f32[256,512]{1,0:T(8,128)} %get-tuple-element.54.refs_3_.refs_2_) | copy-start | bytes 1572868
  44.0 6.0 %copy-start.6 = (f32[256,512]{1,0:T(8,128)S(1)}, f32[256,512]{1,0:T(8,128)}, u32[]{:S(2)}) copy-start(f32[256,512]{1,0:T(8,128)} %get-tuple-element.63.refs_1_) | copy-start | bytes 1572868
  49.1 24.3 %collective-permute-start.8 = (bf16[2,256,1024]{2,1,0:T(8,128)(2,1)S(1)}, bf16[2,256,1024]{2,1,0:T(8,128)(2,1)S(1)}, u32[]{:S(2)}, u32[]{:S(2)}) collective-permute-start(bf16[2,256,1024]{2,1,0:T(8,128)(2,1)S(1)} %get-tuple-element.61), channel_id=1, source_target_pairs={{0,2},{2,0},{4,6},{6,4},{1,3},{3,1},{5,7},{7,5},{8,10},{10,8},{12,... | collective-permute-start | bytes 3145736 | tf_op jit(solution)/shard_map/ppermute | solution.py:32
  51.0 11.0 %collective-permute-start.9 = (bf16[128,512]{1,0:T(8,128)(2,1)S(1)}, bf16[128,512]{1,0:T(8,128)(2,1)S(1)}, u32[]{:S(2)}, u32[]{:S(2)}) collective-permute-start(bf16[128,512]{1,0:T(8,128)(2,1)S(1)} %get-tuple-element.65), channel_id=1, source_target_pairs={{0,8},{8,16},{16,24},{24,32},{32,40},{40,48},{48,56},{56,64},{64,7... | collective-permute-start | bytes 393224 | tf_op jit(solution)/shard_map/ppermute | solution.py:37
  56.2 5.8 %copy-start.9 = (bf16[256,512]{1,0:T(8,128)(2,1)S(1)}, bf16[256,512]{1,0:T(8,128)(2,1)}, u32[]{:S(2)}) copy-start(bf16[256,512]{1,0:T(8,128)(2,1)} %get-tuple-element.51.refs_0_.refs_3_) | copy-start | bytes 786436
  56.9 29.5 %collective-permute-start.14 = (bf16[512,512]{1,0:T(8,128)(2,1)S(1)}, bf16[512,512]{1,0:T(8,128)(2,1)S(1)}, u32[]{:S(2)}, u32[]{:S(2)}) collective-permute-start(bf16[512,512]{1,0:T(8,128)(2,1)S(1)} %get-tuple-element.77), channel_id=1, source_target_pairs={{0,64},{64,128},{128,192},{192,0},{1,65},{65,129},{129,193},{193,1... | collective-permute-start | bytes 1572872 | tf_op jit(solution)/shard_map/ppermute | solution.py:28
  57.9 28.5 %collective-permute-start.15 = (bf16[512,512]{1,0:T(8,128)(2,1)S(1)}, bf16[512,512]{1,0:T(8,128)(2,1)S(1)}, u32[]{:S(2)}, u32[]{:S(2)}) collective-permute-start(bf16[512,512]{1,0:T(8,128)(2,1)S(1)} %get-tuple-element.78), channel_id=1, source_target_pairs={{0,128},{64,192},{128,0},{192,64},{1,129},{65,193},{129,1},{193,65... | collective-permute-start | bytes 1572872 | tf_op jit(solution)/shard_map/ppermute | solution.py:28
  60.9 25.6 %collective-permute-start.16 = (bf16[512,512]{1,0:T(8,128)(2,1)S(1)}, bf16[512,512]{1,0:T(8,128)(2,1)S(1)}, u32[]{:S(2)}, u32[]{:S(2)}) collective-permute-start(bf16[512,512]{1,0:T(8,128)(2,1)S(1)} %get-tuple-element.79), channel_id=1, source_target_pairs={{0,192},{64,0},{128,64},{192,128},{1,193},{65,1},{129,65},{193,129... | collective-permute-start | bytes 1572872 | tf_op jit(solution)/shard_map/ppermute | solution.py:28
  70.5 1.4 %collective-permute-start.11 = (f32[64,512]{1,0:T(8,128)S(1)}, f32[64,512]{1,0:T(8,128)S(1)}, u32[]{:S(2)}, u32[]{:S(2)}) collective-permute-start(f32[64,512]{1,0:T(8,128)S(1)} %get-tuple-element.70), channel_id=1, source_target_pairs={{0,8},{8,0},{1,9},{9,1},{2,10},{10,2},{3,11},{11,3},{4,12},{12,4},... | collective-permute-start | bytes 393224 | tf_op jit(solution)/shard_map/ppermute | solution.py:32
  74.1 23.9 %collective-permute-start.12 = (bf16[256,1024]{1,0:T(8,128)(2,1)S(1)}, bf16[256,1024]{1,0:T(8,128)(2,1)S(1)}, u32[]{:S(2)}, u32[]{:S(2)}) collective-permute-start(bf16[256,1024]{1,0:T(8,128)(2,1)S(1)} %get-tuple-element.73), channel_id=1, source_target_pairs={{0,6},{2,4},{4,2},{6,0},{1,7},{3,5},{5,3},{7,1},{8,14},{10,12},{12... | collective-permute-start | bytes 1572872 | tf_op jit(solution)/shard_map/ppermute | solution.py:32
  75.8 5.9 %collective-permute-start.20 = (bf16[64,512]{1,0:T(8,128)(2,1)S(1)}, bf16[64,512]{1,0:T(8,128)(2,1)S(1)}, u32[]{:S(2)}, u32[]{:S(2)}) collective-permute-start(bf16[64,512]{1,0:T(8,128)(2,1)S(1)} %get-tuple-element.88), channel_id=1, source_target_pairs={{0,16},{16,0},{32,48},{48,32},{1,17},{17,1},{33,49},{49,33},{2,18}... | collective-permute-start | bytes 196616 | tf_op jit(solution)/shard_map/ppermute | solution.py:32
  82.3 6.5 %collective-permute-start.21 = (bf16[64,512]{1,0:T(8,128)(2,1)S(1)}, bf16[64,512]{1,0:T(8,128)(2,1)S(1)}, u32[]{:S(2)}, u32[]{:S(2)}) collective-permute-start(bf16[64,512]{1,0:T(8,128)(2,1)S(1)} %get-tuple-element.90), channel_id=1, source_target_pairs={{0,32},{16,48},{32,0},{48,16},{1,33},{17,49},{33,1},{49,17},{2,34}... | collective-permute-start | bytes 196616 | tf_op jit(solution)/shard_map/ppermute | solution.py:32
  89.5 13.9 %copy-start.4 = (bf16[256,512]{1,0:T(8,128)(2,1)S(1)}, bf16[256,512]{1,0:T(8,128)(2,1)}, u32[]{:S(2)}) copy-start(bf16[256,512]{1,0:T(8,128)(2,1)} %refs_2_.1) | copy-start | bytes 786436
  89.5 13.8 %copy-start.8 = (f32[4,128,128]{2,1,0:T(8,128)S(1)}, f32[4,128,128]{2,1,0:T(8,128)}, u32[]{:S(2)}) copy-start(f32[4,128,128]{2,1,0:T(8,128)} %get-tuple-element.53.refs_2_.refs_3_) | copy-start | bytes 786436
  89.5 6.0 %collective-permute-start.22 = (bf16[64,512]{1,0:T(8,128)(2,1)S(1)}, bf16[64,512]{1,0:T(8,128)(2,1)S(1)}, u32[]{:S(2)}, u32[]{:S(2)}) collective-permute-start(bf16[64,512]{1,0:T(8,128)(2,1)S(1)} %get-tuple-element.92), channel_id=1, source_target_pairs={{0,64},{64,0},{128,192},{192,128},{1,65},{65,1},{129,193},{193,129... | collective-permute-start | bytes 196616 | tf_op jit(solution)/shard_map/ppermute | solution.py:32
  91.9 19.8 %collective-permute-start.17 = (bf16[512,128]{1,0:T(8,128)(2,1)S(1)}, bf16[512,128]{1,0:T(8,128)(2,1)S(1)}, u32[]{:S(2)}, u32[]{:S(2)}) collective-permute-start(bf16[512,128]{1,0:T(8,128)(2,1)S(1)} %get-tuple-element.81), channel_id=1, source_target_pairs={{0,16},{16,0},{32,48},{48,32},{1,17},{17,1},{33,49},{49,33},{2,18}... | collective-permute-start | bytes 393224 | tf_op jit(solution)/shard_map/ppermute | solution.py:32
  91.9 19.8 %collective-permute-start.18 = (bf16[512,128]{1,0:T(8,128)(2,1)S(1)}, bf16[512,128]{1,0:T(8,128)(2,1)S(1)}, u32[]{:S(2)}, u32[]{:S(2)}) collective-permute-start(bf16[512,128]{1,0:T(8,128)(2,1)S(1)} %get-tuple-element.82), channel_id=1, source_target_pairs={{0,32},{16,48},{32,0},{48,16},{1,33},{17,49},{33,1},{49,17},{2,34}... | collective-permute-start | bytes 393224 | tf_op jit(solution)/shard_map/ppermute | solution.py:32
  94.2 17.6 %collective-permute-start.19 = (bf16[512,128]{1,0:T(8,128)(2,1)S(1)}, bf16[512,128]{1,0:T(8,128)(2,1)S(1)}, u32[]{:S(2)}, u32[]{:S(2)}) collective-permute-start(bf16[512,128]{1,0:T(8,128)(2,1)S(1)} %get-tuple-element.83), channel_id=1, source_target_pairs={{0,48},{16,32},{32,16},{48,0},{1,49},{17,33},{33,17},{49,1},{2,50}... | collective-permute-start | bytes 393224 | tf_op jit(solution)/shard_map/ppermute | solution.py:32
  96.1 15.5 %collective-permute-start.23 = (bf16[64,512]{1,0:T(8,128)(2,1)S(1)}, bf16[64,512]{1,0:T(8,128)(2,1)S(1)}, u32[]{:S(2)}, u32[]{:S(2)}) collective-permute-start(bf16[64,512]{1,0:T(8,128)(2,1)S(1)} %get-tuple-element.94), channel_id=1, source_target_pairs={{0,192},{64,128},{128,64},{192,0},{1,193},{65,129},{129,65},{193,1... | collective-permute-start | bytes 196616 | tf_op jit(solution)/shard_map/ppermute | solution.py:32
  98.2 22.9 %collective-permute-start.13 = (bf16[256,512]{1,0:T(8,128)(2,1)S(1)}, bf16[256,512]{1,0:T(8,128)(2,1)S(1)}, u32[]{:S(2)}, u32[]{:S(2)}) collective-permute-start(bf16[256,512]{1,0:T(8,128)(2,1)S(1)} %get-tuple-element.75), channel_id=1, source_target_pairs={{0,1},{1,0},{2,3},{3,2},{4,5},{5,4},{6,7},{7,6},{8,9},{9,8},{10,11... | collective-permute-start | bytes 786440 | tf_op jit(solution)/shard_map/ppermute | solution.py:32
  111.8 7.7 %collective-permute-start.24 = (f32[64,512]{1,0:T(8,128)S(1)}, f32[64,512]{1,0:T(8,128)S(1)}, u32[]{:S(2)}, u32[]{:S(2)}) collective-permute-start(f32[64,512]{1,0:T(8,128)S(1)} %last.1.refs_1_), channel_id=1, source_target_pairs={{0,8},{8,0},{1,9},{9,1},{2,10},{10,2},{3,11},{11,3},{4,12},{12,4},... | collective-permute-start | bytes 393224 | tf_op jit(solution)/shard_map/ppermute | solution.py:32
  (5 other events, 6.6 us)

commit v2 on v1

--- a/solution.py
+++ b/solution.py
@@ -115,20 +115,19 @@
     return jax.ShapeDtypeStruct(shape, dtype)
 
 
-def spread(natural, tile, wide, count, offset, span):
-    @pl.loop(0, count // 8)
-    def _(b):
-        for i in range(8):
-            s = b * 8 + i
-            wide[s] = natural[tile, pl.ds(s + offset, 8, stride=span), :]
-
-
-def convolve(wide, turned, natural_out, tile, span, causal):
+def spread(natural, tile, wide, count, span):
+    step = span // 8
+    for a in range(count // 8):
+        rows = [natural[tile, pl.ds(8 * (a + step * q), 8), :] for q in range(8)]
+        wide[pl.ds(8 * a, 8)] = jnp.swapaxes(jnp.stack(rows, 0), 0, 1)
+
+
+def convolve(wide, turned, natural_out, turn, tile, span, causal):
     tap_count = turned.shape[1]
     for rb in range(span // BLOCK):
 
         def body(jb, acc):
-            start = (rb - jb) * BLOCK + tap_count - BLOCK if causal else (rb + jb) * BLOCK
+            start = (rb - jb) * BLOCK + tap_count - BLOCK + 1 if causal else (rb + jb) * BLOCK
             window = [wide[start + i] for i in range(2 * BLOCK - 1)]
             acc = list(acc)
             for j in range(BLOCK):
@@ -140,7 +139,11 @@
         zero = jnp.zeros((8, LANES), F32)
         acc = lax.fori_loop(0, tap_count // BLOCK, body, (zero,) * BLOCK)
         for r in range(BLOCK):
-            natural_out[tile, pl.ds(rb * BLOCK + r, 8, stride=span), :] = acc[r]
+            turn[rb * BLOCK + r] = acc[r]
+    for a in range(span // 8):
+        eight = jnp.swapaxes(turn[pl.ds(8 * a, 8)], 0, 1)
+        for q in range(8):
+            natural_out[tile, pl.ds(q * span + 8 * a, 8), :] = eight[q]
 
 
 def columns(low, high, codes, group):
@@ -151,8 +154,7 @@
 
 
 def prepare_kernel(up, codes, low, high, key_codes, key_low, key_high, taps, *outs):
-    grad_conv, head, key, turned, mark = outs
-    mark[...] = jnp.zeros_like(mark)
+    grad_conv, head, key, turned = outs
     for l in range(codes.shape[1] // LANES):
         cols = pl.ds(l * LANES, LANES)
         g = (up[:, cols].astype(F32) * columns(low, high, codes, l)).astype(BF16)
@@ -169,7 +171,7 @@
     key_grad[...] = mix[...] * value[...]
 
 
-def mix_kernel(g, halo, turned, key, mix, value, turned_value, nat, wide, out):
+def mix_kernel(g, halo, turned, key, mix, value, turned_value, nat, wide, turn, out):
     rows, channels = g.shape
     tiles, tap_count = channels // LANES, halo.shape[0]
     for l in range(tiles):
@@ -179,8 +181,8 @@
 
     @pl.loop(0, tiles)
     def _(l):
-        spread(nat, l, wide, wide.shape[0], 0, rows // 8)
-        convolve(wide, turned, out, l, rows // 8, False)
+        spread(nat, l, wide, wide.shape[0], rows // 8)
+        convolve(wide, turned, out, turn, l, rows // 8, False)
 
     for l in range(tiles):
         cols = pl.ds(l * LANES, LANES)
@@ -203,15 +205,15 @@
         nat_g[l] = g[:, cols].astype(F32)
 
     for l in range(tiles):
-        spread(nat, l, wide, wide.shape[0], 1, span)
-        spread(nat_g, l, wide_g, span, 0, span)
+        spread(nat, l, wide, wide.shape[0], span)
+        spread(nat_g, l, wide_g, span, span)
 
         @pl.loop(0, tap_count // BLOCK)
         def _(jb):
             zero = jnp.zeros((8, LANES), F32)
             acc = [zero] * BLOCK
             for rb in range(span // BLOCK):
-                start = (rb - jb) * BLOCK + tap_count - BLOCK
+                start = (rb - jb) * BLOCK + tap_count - BLOCK + 1
                 window = [wide[start + i] for i in range(2 * BLOCK - 1)]
                 for r in range(BLOCK):
                     up = wide_g[rb * BLOCK + r]
@@ -232,7 +234,7 @@
     sent[...] = total[...].astype(BF16)
 
 
-def conv_kernel(p, halo, upstream, turned, query_grad, mark, nat, wide, out):
+def conv_kernel(p, halo, upstream, turned, query_grad, mark, nat, wide, turn, out):
     mark[...] = jnp.zeros_like(mark)
     rows, channels = p.shape
     tiles, tap_count = channels // LANES, halo.shape[0]
@@ -243,8 +245,8 @@
 
     @pl.loop(0, tiles)
     def _(l):
-        spread(nat, l, wide, wide.shape[0], 1, rows // 8)
-        convolve(wide, turned, out, l, rows // 8, True)
+        spread(nat, l, wide, wide.shape[0], rows // 8)
+        convolve(wide, turned, out, turn, l, rows // 8, True)
 
     for l in range(tiles):
         cols = pl.ds(l * LANES, LANES)
@@ -382,14 +384,15 @@
 
     mark = struct((8, LANES), F32)
     wide_shape = pltpu.VMEM((tap_count + span, 8, LANES), F32)
-    nat_shape = pltpu.VMEM((tiles, rows + tap_count + 8, LANES), F32)
+    nat_shape = pltpu.VMEM((tiles, rows + tap_count, LANES), F32)
+    turn_shape = pltpu.VMEM((span, 8, LANES), F32)
     out_scratch = pltpu.VMEM((tiles, rows, LANES), F32)
     plane = struct((rows, channels), F32)
     half_plane = struct((rows, channels), BF16)
 
     far = crossed(layer_input, "zh", 1)
     near_blocks = [layer_input] + [shifted(layer_input, "y", k) for k in (1, 2, 3)]
-    grad_conv, head, key, turned, prepare_mark = call(
+    grad_conv, head, key, turned = call(
         "prepare",
         prepare_kernel,
         (
@@ -397,22 +400,21 @@
             struct((tap_count, channels), BF16),
             plane,
             struct((tiles, tap_count, LANES), F32),
-            mark,
         ),
         [("in", v) for v in (out_grad, query_codes, query_low.T, query_high.T)]
         + [("in", v) for v in (key_codes, key_low.T, key_high.T, filter_taps)],
-        params=room(60),
+        params=room(57),
     )
     later_rows = along_tokens(head, -1)
-    far = after(far, *[("tie", b) for b in near_blocks[1:]], ("mark", prepare_mark))
+    far = after(far, *[("tie", b) for b in near_blocks[1:]], ("tie", later_rows))
     far_blocks = [far] + [shifted(far, "y", k) for k in (1, 2, 3)]
     grad_mix, grad_value, turned_value = call(
         "mix",
         mix_kernel,
         (plane, half_plane, struct((channels, rows), BF16)),
         [("in", grad_conv), ("in", later_rows), ("in", turned), ("in", key), ("tie", far)],
-        [nat_shape, wide_shape, out_scratch],
-        room(62.5),
+        [nat_shape, wide_shape, turn_shape, out_scratch],
+        room(52),
     )
 
     eight = pltpu.SemaphoreType.DMA((8,))
@@ -512,7 +514,7 @@
         (plane, mark),
         [("vmem", product), ("in", earlier_rows), ("in", out_grad), ("vmem", turned)]
         + [("mark", gather_mark), ("mark", split_mark)],
-        [nat_shape, wide_shape, out_scratch],
+        [nat_shape, wide_shape, turn_shape, out_scratch],
     )
     filter_sum, filter_sent, middle2_mark = call(
         "middle2",

time: 123 us -> 120 us (0.976)
  Pallas kernels: 47.4 us -> 41 us
  waiting for transfers between devices: 10.5 us -> 16.5 us
    pallas_call x19, Pallas kernels: 47.4 us -> 41 us  [call(): pl.pallas_call(kernel, out_shape=out, in_specs=[SPECS[kind] for kind in k...]
    ppermute x2, waiting for transfers between devices: 4.66 us -> 8.07 us  [along_tokens(): lax.ppermute(block, SEQ, [(i, i + step) for i in range(n) if 0 <= i + ste...]
    ppermute x14, waiting for transfers between devices: 5.82 us -> 7.95 us  [crossed(): lax.ppermute(block, axis, [(i, i ^ d) for i in range(lax.axis_size(axis))])]
    ppermute x14, starting transfers between devices: 37.1 us -> 35.8 us  [crossed(): lax.ppermute(block, axis, [(i, i ^ d) for i in range(lax.axis_size(axis))])]
    unnamed x24 -> x18, local copies, waits for them, and re-layouts: 3.26 us -> 2.72 us
  transfers between devices with their start and end apart: 25 -> 25, of which waited for: 5 -> 6; matrix products, arithmetic and copies ran while one was open for 0% -> 0% of each run, Pallas kernels for 35% -> 31%
where the time goes in v2:
time: 120 us
  starting transfers between devices  58.8 us (49%)
  Pallas kernels  41 us (34%)
  waiting for transfers between devices  16.5 us (14%)
  local copies, waits for them, and re-layouts  2.81 us (2%)
    pallas_call x19, Pallas kernels, call(): pl.pallas_call(kernel, out_shape=out, in_specs=[SPECS[kind] for kind in k...  41 us
    ppermute x14, starting transfers between devices, crossed(): lax.ppermute(block, axis, [(i, i ^ d) for i in range(lax.axis_size(axis))])  35.8 us
    ppermute x9, starting transfers between devices, shifted(): return lax.ppermute(block, axis, [(i, (i + k) % n) for i in range(n)])  13.9 us
    ppermute x2, starting transfers between devices, along_tokens(): lax.ppermute(block, SEQ, [(i, i + step) for i in range(n) if 0 <= i + ste...  9.08 us
    ppermute x2, waiting for transfers between devices, along_tokens(): lax.ppermute(block, SEQ, [(i, i + step) for i in range(n) if 0 <= i + ste...  8.07 us
    ppermute x14, waiting for transfers between devices, crossed(): lax.ppermute(block, axis, [(i, i ^ d) for i in range(lax.axis_size(axis))])  7.95 us
    unnamed x18, local copies, waits for them, and re-layouts  2.72 us
  transfers between devices with their start and end apart: 25, of which 6 were waited for; matrix products, arithmetic and copies ran while one was open for 0% of the time, Pallas kernels for 31%

profile of v2, /device:TPU:1, one launch (start us, length us, event | category | flops | bytes accessed | tf_op | source)
XLA Modules:
  0.0 120.2 jit_solution(580857631615349803)
XLA Ops:
  0.6 2.2 %collective-permute-start.2 = (bf16[256,512]{1,0:T(8,128)(2,1)}, bf16[256,512]{1,0:T(8,128)(2,1)S(1)}, u32[]{:S(2)}, u32[]{:S(2)}) collective-permute-start(bf16[256,512]{1,0:T(8,128)(2,1)} %refs_1_.3), channel_id=1, source_target_pairs={{0,2},{2,4},{4,6},{6,0},{1,3},{3,5},{5,7},{7,1},{8,10},{10,12},{12... | collective-permute-start | bytes 786440 | tf_op jit(solution)/shard_map/ppermute | solution.py:28
  2.8 2.6 %collective-permute-start.3 = (bf16[256,512]{1,0:T(8,128)(2,1)}, bf16[256,512]{1,0:T(8,128)(2,1)S(1)}, u32[]{:S(2)}, u32[]{:S(2)}) collective-permute-start(bf16[256,512]{1,0:T(8,128)(2,1)} %refs_1_.3), channel_id=1, source_target_pairs={{0,4},{2,6},{4,0},{6,2},{1,5},{3,7},{5,1},{7,3},{8,12},{10,14},{12... | collective-permute-start | bytes 786440 | tf_op jit(solution)/shard_map/ppermute | solution.py:28
  6.5 6.9 %collective-permute-start.1 = (bf16[256,512]{1,0:T(8,128)(2,1)}, bf16[256,512]{1,0:T(8,128)(2,1)S(1)}, u32[]{:S(2)}, u32[]{:S(2)}) collective-permute-start(bf16[256,512]{1,0:T(8,128)(2,1)} %refs_1_.3), channel_id=1, source_target_pairs={{0,1},{1,0},{2,3},{3,2},{4,5},{5,4},{6,7},{7,6},{8,9},{9,8},{10,11... | collective-permute-start | bytes 786440 | tf_op jit(solution)/shard_map/ppermute | solution.py:32
  13.4 2.9 %prepare.1 = (bf16[256,512]{1,0:T(8,128)(2,1)}, bf16[128,512]{1,0:T(8,128)(2,1)}, f32[256,512]{1,0:T(8,128)}, f32[4,128,128]{2,1,0:T(8,128)}) custom-call(bf16[256,512]{1,0:T(8,128)(2,1)} %refs_2_.1, s32[256,512]{1,0:T(8,128)} %refs_1_.2, f32[4,256]{1,0:T(4,128)} %bitcast.9, f32[4,256]{1,0:T(4,128)} %bitcast.10, s32[256,512]{1,0:T(8,128)} %refs_4_.1, ...), custom_call_target="tpu_custom_call" | custom-call | flops 1750000000 | bytes 5775000 | tf_op jit(solution)/shard_map/prepare/pallas_call | solution.py:88
  16.4 3.7 %collective-permute-start = (bf16[128,512]{1,0:T(8,128)(2,1)}, bf16[128,512]{1,0:T(8,128)(2,1)S(1)}, u32[]{:S(2)}, u32[]{:S(2)}) collective-permute-start(bf16[128,512]{1,0:T(8,128)(2,1)} %get-tuple-element.51), channel_id=1, source_target_pairs={{8,0},{16,8},{24,16},{32,24},{40,32},{48,40},{56,48},{64,56},{72,6... | collective-permute-start | bytes 393224 | tf_op jit(solution)/shard_map/ppermute | solution.py:37
  20.2 8.1 %collective-permute-done.refs_4_.refs_1_ = bf16[128,512]{1,0:T(8,128)(2,1)S(1)} collective-permute-done((bf16[128,512]{1,0:T(8,128)(2,1)}, bf16[128,512]{1,0:T(8,128)(2,1)S(1)}, u32[]{:S(2)}, u32[]{:S(2)}) %collective-permute-start) | collective-permute-done | bytes 131104 | tf_op jit(solution)/shard_map/ppermute | solution.py:37
  29.4 1.9 %collective-permute-start.7 = (bf16[256,512]{1,0:T(8,128)(2,1)S(1)}, bf16[256,512]{1,0:T(8,128)(2,1)S(1)}, u32[]{:S(2)}, u32[]{:S(2)}) collective-permute-start(bf16[256,512]{1,0:T(8,128)(2,1)S(1)} %after.1.refs_4_.refs_5_), channel_id=1, source_target_pairs={{0,6},{2,0},{4,2},{6,4},{1,7},{3,1},{5,3},{7,5},{8,14},{10,8},{12,... | collective-permute-start | bytes 786440 | tf_op jit(solution)/shard_map/ppermute | solution.py:28
  33.2 6.8 %mix.1 = (f32[256,512]{1,0:T(8,128)S(1)}, bf16[256,512]{1,0:T(8,128)(2,1)S(1)}, bf16[512,256]{1,0:T(8,128)(2,1)S(1)}) custom-call(bf16[256,512]{1,0:T(8,128)(2,1)S(1)} %copy-done.7, bf16[128,512]{1,0:T(8,128)(2,1)S(1)} %collective-permute-done.refs_4_.refs_1_, f32[4,128,128]{2,1,0:T(8,128)S(1)} %copy-done.5, f32[256,512]{1,0:T(8,128)} %get-tuple-element.53.refs_3_.refs_2_, ...), custom_call_target="tpu_custom_call" | custom-call | flops 5390000128 | bytes 17787000 | tf_op jit(solution)/shard_map/mix/pallas_call | solution.py:88
  40.8 3.4 %weight.1 = (f32[4,512,512]{2,1,0:T(8,128)S(1)}, bf16[4,512,512]{2,1,0:T(8,128)(2,1)S(1)}, bf16[8,256,512]{2,1,0:T(8,128)(2,1)S(1)}, f32[8,128]{1,0:T(8,128)S(1)}) custom-call(s32[5]{0:T(128)S(1)} %stack.23.refs_0_, bf16[256,512]{1,0:T(8,128)(2,1)S(1)} %copy-done, bf16[256,512]{1,0:T(8,128)(2,1)S(1)} %collective-permute-done.2.refs_1_.refs_2_, ...), custom_call_target="tpu_custom_call" | custom-call | flops 2800000000 | bytes 9240000 | tf_op jit(solution)/shard_map/weight/pallas_call | solution.py:88
  44.3 5.1 %back.1 = (f32[2,256,1024]{2,1,0:T(8,128)S(1)}, bf16[2,256,1024]{2,1,0:T(8,128)(2,1)S(1)}, f32[256,512]{1,0:T(8,128)S(1)}, f32[8,128]{1,0:T(8,128)}) custom-call(s32[5]{0:T(128)S(1)} %stack.23.refs_0_, bf16[256,512]{1,0:T(8,128)(2,1)S(1)} %get-tuple-element.54.refs_1_, bf16[8,256,512]{2,1,0:T(8,128)(2,1)S(1)} %get-tuple-element.56.refs_2_, ...), custom_call_target="tpu_custom_call" | custom-call | flops 2590000128 | bytes 8547000 | tf_op jit(solution)/shard_map/back/pallas_call | solution.py:88
  50.7 5.4 %collective-permute-start.9 = (bf16[128,512]{1,0:T(8,128)(2,1)S(1)}, bf16[128,512]{1,0:T(8,128)(2,1)S(1)}, u32[]{:S(2)}, u32[]{:S(2)}) collective-permute-start(bf16[128,512]{1,0:T(8,128)(2,1)S(1)} %get-tuple-element.63), channel_id=1, source_target_pairs={{0,8},{8,16},{16,24},{24,32},{32,40},{40,48},{48,56},{56,64},{64,7... | collective-permute-start | bytes 393224 | tf_op jit(solution)/shard_map/ppermute | solution.py:37
  56.8 1.5 %collective-permute-start.14 = (bf16[512,512]{1,0:T(8,128)(2,1)S(1)}, bf16[512,512]{1,0:T(8,128)(2,1)S(1)}, u32[]{:S(2)}, u32[]{:S(2)}) collective-permute-start(bf16[512,512]{1,0:T(8,128)(2,1)S(1)} %get-tuple-element.75), channel_id=1, source_target_pairs={{0,64},{64,128},{128,192},{192,0},{1,65},{65,129},{129,193},{193,1... | collective-permute-start | bytes 1572872 | tf_op jit(solution)/shard_map/ppermute | solution.py:28
  58.3 2.5 %collective-permute-start.15 = (bf16[512,512]{1,0:T(8,128)(2,1)S(1)}, bf16[512,512]{1,0:T(8,128)(2,1)S(1)}, u32[]{:S(2)}, u32[]{:S(2)}) collective-permute-start(bf16[512,512]{1,0:T(8,128)(2,1)S(1)} %get-tuple-element.76), channel_id=1, source_target_pairs={{0,128},{64,192},{128,0},{192,64},{1,129},{65,193},{129,1},{193,65... | collective-permute-start | bytes 1572872 | tf_op jit(solution)/shard_map/ppermute | solution.py:28
  60.8 1.1 collective-permute-start.16
  61.9 6.7 %taps.1 = (f32[64,512]{1,0:T(8,128)S(1)}, f32[64,512]{1,0:T(8,128)S(1)}, f32[8,128]{1,0:T(8,128)}) custom-call(s32[5]{0:T(128)S(1)} %stack.23.refs_0_, bf16[256,512]{1,0:T(8,128)(2,1)S(1)} %get-tuple-element.62.refs_1_.refs_0_, bf16[128,512]{1,0:T(8,128)(2,1)S(1)} %collective-permute-done.9.refs_2_.refs_1_, bf16[256,512]{1,0:T(8,128)(2,1)S(1)} %copy-done.8, ...), custom_call_target="tpu_custom_call" | custom-call | flops 5600000000 | bytes 18480000 | tf_op jit(solution)/shard_map/taps/pallas_call | solution.py:88
  68.7 1.3 %collective-permute-done.11.refs_1_ = f32[64,512]{1,0:T(8,128)S(1)} collective-permute-done((f32[64,512]{1,0:T(8,128)S(1)}, f32[64,512]{1,0:T(8,128)S(1)}, u32[]{:S(2)}, u32[]{:S(2)}) %collective-permute-start.11) | collective-permute-done | bytes 131104 | tf_op jit(solution)/shard_map/ppermute | solution.py:32
  70.2 3.5 %collective-permute-done.8.refs_1_ = bf16[2,256,1024]{2,1,0:T(8,128)(2,1)S(1)} collective-permute-done((bf16[2,256,1024]{2,1,0:T(8,128)(2,1)S(1)}, bf16[2,256,1024]{2,1,0:T(8,128)(2,1)S(1)}, u32[]{:S(2)}, u32[]{:S(2)}) %collective-permute-start.8) | collective-permute-done | bytes 1048608 | tf_op jit(solution)/shard_map/ppermute | solution.py:32
  74.4 1.3 %collective-permute-start.12 = (bf16[256,1024]{1,0:T(8,128)(2,1)S(1)}, bf16[256,1024]{1,0:T(8,128)(2,1)S(1)}, u32[]{:S(2)}, u32[]{:S(2)}) collective-permute-start(bf16[256,1024]{1,0:T(8,128)(2,1)S(1)} %get-tuple-element.71), channel_id=1, source_target_pairs={{0,6},{2,4},{4,2},{6,0},{1,7},{3,5},{5,3},{7,1},{8,14},{10,12},{12... | collective-permute-start | bytes 1572872 | tf_op jit(solution)/shard_map/ppermute | solution.py:32
  75.7 5.0 %collective-permute-start.20 = (bf16[64,512]{1,0:T(8,128)(2,1)S(1)}, bf16[64,512]{1,0:T(8,128)(2,1)S(1)}, u32[]{:S(2)}, u32[]{:S(2)}) collective-permute-start(bf16[64,512]{1,0:T(8,128)(2,1)S(1)} %get-tuple-element.86), channel_id=1, source_target_pairs={{0,16},{16,0},{32,48},{48,32},{1,17},{17,1},{33,49},{49,33},{2,18}... | collective-permute-start | bytes 196616 | tf_op jit(solution)/shard_map/ppermute | solution.py:32
  80.7 1.9 %collective-permute-done.20.refs_1_ = bf16[64,512]{1,0:T(8,128)(2,1)S(1)} collective-permute-done((bf16[64,512]{1,0:T(8,128)(2,1)S(1)}, bf16[64,512]{1,0:T(8,128)(2,1)S(1)}, u32[]{:S(2)}, u32[]{:S(2)}) %collective-permute-start.20) | collective-permute-done | bytes 65568 | tf_op jit(solution)/shard_map/ppermute | solution.py:32
  83.3 1.6 %collective-permute-start.21 = (bf16[64,512]{1,0:T(8,128)(2,1)S(1)}, bf16[64,512]{1,0:T(8,128)(2,1)S(1)}, u32[]{:S(2)}, u32[]{:S(2)}) collective-permute-start(bf16[64,512]{1,0:T(8,128)(2,1)S(1)} %get-tuple-element.88), channel_id=1, source_target_pairs={{0,32},{16,48},{32,0},{48,16},{1,33},{17,49},{33,1},{49,17},{2,34}... | collective-permute-start | bytes 196616 | tf_op jit(solution)/shard_map/ppermute | solution.py:32
  85.4 1.2 gather.1
  86.6 1.1 collective-permute-done.21.refs_1_
  88.4 1.3 %collective-permute-start.22 = (bf16[64,512]{1,0:T(8,128)(2,1)S(1)}, bf16[64,512]{1,0:T(8,128)(2,1)S(1)}, u32[]{:S(2)}, u32[]{:S(2)}) collective-permute-start(bf16[64,512]{1,0:T(8,128)(2,1)S(1)} %get-tuple-element.90), channel_id=1, source_target_pairs={{0,64},{64,0},{128,192},{192,128},{1,65},{65,1},{129,193},{193,129... | collective-permute-start | bytes 196616 | tf_op jit(solution)/shard_map/ppermute | solution.py:32
  89.7 1.5 %collective-permute-start.17 = (bf16[512,128]{1,0:T(8,128)(2,1)S(1)}, bf16[512,128]{1,0:T(8,128)(2,1)S(1)}, u32[]{:S(2)}, u32[]{:S(2)}) collective-permute-start(bf16[512,128]{1,0:T(8,128)(2,1)S(1)} %get-tuple-element.79), channel_id=1, source_target_pairs={{0,16},{16,0},{32,48},{48,32},{1,17},{17,1},{33,49},{49,33},{2,18}... | collective-permute-start | bytes 393224 | tf_op jit(solution)/shard_map/ppermute | solution.py:32
  91.8 1.5 %collective-permute-start.19 = (bf16[512,128]{1,0:T(8,128)(2,1)S(1)}, bf16[512,128]{1,0:T(8,128)(2,1)S(1)}, u32[]{:S(2)}, u32[]{:S(2)}) collective-permute-start(bf16[512,128]{1,0:T(8,128)(2,1)S(1)} %get-tuple-element.81), channel_id=1, source_target_pairs={{0,48},{16,32},{32,16},{48,0},{1,49},{17,33},{33,17},{49,1},{2,50}... | collective-permute-start | bytes 393224 | tf_op jit(solution)/shard_map/ppermute | solution.py:32
  94.0 2.0 %collective-permute-start.23 = (bf16[64,512]{1,0:T(8,128)(2,1)S(1)}, bf16[64,512]{1,0:T(8,128)(2,1)S(1)}, u32[]{:S(2)}, u32[]{:S(2)}) collective-permute-start(bf16[64,512]{1,0:T(8,128)(2,1)S(1)} %get-tuple-element.92), channel_id=1, source_target_pairs={{0,192},{64,128},{128,64},{192,0},{1,193},{65,129},{129,65},{193,1... | collective-permute-start | bytes 196616 | tf_op jit(solution)/shard_map/ppermute | solution.py:32
  96.2 4.1 %collective-permute-start.13 = (bf16[256,512]{1,0:T(8,128)(2,1)S(1)}, bf16[256,512]{1,0:T(8,128)(2,1)S(1)}, u32[]{:S(2)}, u32[]{:S(2)}) collective-permute-start(bf16[256,512]{1,0:T(8,128)(2,1)S(1)} %get-tuple-element.73), channel_id=1, source_target_pairs={{0,1},{1,0},{2,3},{3,2},{4,5},{5,4},{6,7},{7,6},{8,9},{9,8},{10,11... | collective-permute-start | bytes 786440 | tf_op jit(solution)/shard_map/ppermute | solution.py:32
  100.3 6.5 %conv.1 = (f32[256,512]{1,0:T(8,128)}, f32[8,128]{1,0:T(8,128)S(1)}) custom-call(bf16[256,512]{1,0:T(8,128)(2,1)S(1)} %get-tuple-element.62.refs_1_.refs_0_, bf16[128,512]{1,0:T(8,128)(2,1)S(1)} %collective-permute-done.9.refs_2_.refs_1_, bf16[256,512]{1,0:T(8,128)(2,1)S(1)} %copy-done.1, f32[4,128,128]{2,1,0:T(8,128)S(1)} %copy-done.6, ...), custom_call_target="tpu_custom_call" | custom-call | flops 5880000000 | bytes 19404000 | tf_op jit(solution)/shard_map/conv/pallas_call | solution.py:88
  106.9 9.4 %collective-permute-start.24 = (f32[64,512]{1,0:T(8,128)S(1)}, f32[64,512]{1,0:T(8,128)S(1)}, u32[]{:S(2)}, u32[]{:S(2)}) collective-permute-start(f32[64,512]{1,0:T(8,128)S(1)} %last.1.refs_1_), channel_id=1, source_target_pairs={{0,8},{8,0},{1,9},{9,1},{2,10},{10,2},{3,11},{11,3},{4,12},{12,4},... | collective-permute-start | bytes 393224 | tf_op jit(solution)/shard_map/ppermute | solution.py:32
  116.2 1.4 %finish.1 = f32[128,512]{1,0:T(8,128)} custom-call(f32[512,128]{1,0:T(8,128)S(1)} %get-tuple-element.78.refs_0_, bf16[512,128]{1,0:T(8,128)(2,1)S(1)} %collective-permute-done.17.refs_1_.refs_2_, bf16[512,128]{1,0:T(8,128)(2,1)S(1)} %collective-permute-done.18.refs_2_.refs_3_, bf16[512,128]{1,0:T(8,128)(2,1)S(1)} %collective-permute-done.19.refs_3_.refs_4_, ...), custom_call_target="tpu_custom_call" | custom-call | flops 910000000 | bytes 3003000 | tf_op jit(solution)/shard_map/finish/pallas_call | solution.py:88
  117.6 1.6 %ends.1 = f32[512,128]{1,0:T(8,128)} custom-call(s32[5]{0:T(128)S(1)} %stack.23.refs_0_, f32[64,512]{1,0:T(8,128)S(1)} %last.1.refs_1_, f32[64,512]{1,0:T(8,128)S(1)} %collective-permute-done.24.refs_2_), custom_call_target="tpu_custom_call" | custom-call | flops 910000000 | bytes 3003000 | tf_op jit(solution)/shard_map/ends/pallas_call | solution.py:88
  (57 shorter events, 12.3 us)
Async XLA Ops:
  0.6 27.6 %collective-permute-start.2 = (bf16[256,512]{1,0:T(8,128)(2,1)}, bf16[256,512]{1,0:T(8,128)(2,1)S(1)}, u32[]{:S(2)}, u32[]{:S(2)}) collective-permute-start(bf16[256,512]{1,0:T(8,128)(2,1)} %refs_1_.3), channel_id=1, source_target_pairs={{0,2},{2,4},{4,6},{6,0},{1,3},{3,5},{5,7},{7,1},{8,10},{10,12},{12... | collective-permute-start | bytes 786440 | tf_op jit(solution)/shard_map/ppermute | solution.py:28
  2.8 25.4 %collective-permute-start.3 = (bf16[256,512]{1,0:T(8,128)(2,1)}, bf16[256,512]{1,0:T(8,128)(2,1)S(1)}, u32[]{:S(2)}, u32[]{:S(2)}) collective-permute-start(bf16[256,512]{1,0:T(8,128)(2,1)} %refs_1_.3), channel_id=1, source_target_pairs={{0,4},{2,6},{4,0},{6,2},{1,5},{3,7},{5,1},{7,3},{8,12},{10,14},{12... | collective-permute-start | bytes 786440 | tf_op jit(solution)/shard_map/ppermute | solution.py:28
  5.5 22.8 %collective-permute-start.4 = (bf16[256,512]{1,0:T(8,128)(2,1)}, bf16[256,512]{1,0:T(8,128)(2,1)S(1)}, u32[]{:S(2)}, u32[]{:S(2)}) collective-permute-start(bf16[256,512]{1,0:T(8,128)(2,1)} %refs_1_.3), channel_id=1, source_target_pairs={{0,6},{2,0},{4,2},{6,4},{1,7},{3,1},{5,3},{7,5},{8,14},{10,8},{12,... | collective-permute-start | bytes 786440 | tf_op jit(solution)/shard_map/ppermute | solution.py:28
  6.5 21.8 %collective-permute-start.1 = (bf16[256,512]{1,0:T(8,128)(2,1)}, bf16[256,512]{1,0:T(8,128)(2,1)S(1)}, u32[]{:S(2)}, u32[]{:S(2)}) collective-permute-start(bf16[256,512]{1,0:T(8,128)(2,1)} %refs_1_.3), channel_id=1, source_target_pairs={{0,1},{1,0},{2,3},{3,2},{4,5},{5,4},{6,7},{7,6},{8,9},{9,8},{10,11... | collective-permute-start | bytes 786440 | tf_op jit(solution)/shard_map/ppermute | solution.py:32
  16.4 11.9 %collective-permute-start = (bf16[128,512]{1,0:T(8,128)(2,1)}, bf16[128,512]{1,0:T(8,128)(2,1)S(1)}, u32[]{:S(2)}, u32[]{:S(2)}) collective-permute-start(bf16[128,512]{1,0:T(8,128)(2,1)} %get-tuple-element.51), channel_id=1, source_target_pairs={{8,0},{16,8},{24,16},{32,24},{40,32},{48,40},{56,48},{64,56},{72,6... | collective-permute-start | bytes 393224 | tf_op jit(solution)/shard_map/ppermute | solution.py:37
  28.3 12.5 %collective-permute-start.5 = (bf16[256,512]{1,0:T(8,128)(2,1)S(1)}, bf16[256,512]{1,0:T(8,128)(2,1)S(1)}, u32[]{:S(2)}, u32[]{:S(2)}) collective-permute-start(bf16[256,512]{1,0:T(8,128)(2,1)S(1)} %after.1.refs_4_.refs_5_), channel_id=1, source_target_pairs={{0,2},{2,4},{4,6},{6,0},{1,3},{3,5},{5,7},{7,1},{8,10},{10,12},{12... | collective-permute-start | bytes 786440 | tf_op jit(solution)/shard_map/ppermute | solution.py:28
  28.8 12.0 %collective-permute-start.6 = (bf16[256,512]{1,0:T(8,128)(2,1)S(1)}, bf16[256,512]{1,0:T(8,128)(2,1)S(1)}, u32[]{:S(2)}, u32[]{:S(2)}) collective-permute-start(bf16[256,512]{1,0:T(8,128)(2,1)S(1)} %after.1.refs_4_.refs_5_), channel_id=1, source_target_pairs={{0,4},{2,6},{4,0},{6,2},{1,5},{3,7},{5,1},{7,3},{8,12},{10,14},{12... | collective-permute-start | bytes 786440 | tf_op jit(solution)/shard_map/ppermute | solution.py:28
  29.4 11.4 %collective-permute-start.7 = (bf16[256,512]{1,0:T(8,128)(2,1)S(1)}, bf16[256,512]{1,0:T(8,128)(2,1)S(1)}, u32[]{:S(2)}, u32[]{:S(2)}) collective-permute-start(bf16[256,512]{1,0:T(8,128)(2,1)S(1)} %after.1.refs_4_.refs_5_), channel_id=1, source_target_pairs={{0,6},{2,0},{4,2},{6,4},{1,7},{3,1},{5,3},{7,5},{8,14},{10,8},{12,... | collective-permute-start | bytes 786440 | tf_op jit(solution)/shard_map/ppermute | solution.py:28
  31.3 0.9 copy-start.5
  33.2 7.6 %copy-start = (bf16[256,512]{1,0:T(8,128)(2,1)S(1)}, bf16[256,512]{1,0:T(8,128)(2,1)}, u32[]{:S(2)}) copy-start(bf16[256,512]{1,0:T(8,128)(2,1)} %refs_1_.3) | copy-start | bytes 786436
  44.2 11.9 %collective-permute-start.10 = (bf16[4,512,512]{2,1,0:T(8,128)(2,1)S(1)}, bf16[4,512,512]{2,1,0:T(8,128)(2,1)S(1)}, u32[]{:S(2)}, u32[]{:S(2)}) collective-permute-start(bf16[4,512,512]{2,1,0:T(8,128)(2,1)S(1)} %get-tuple-element.65), channel_id=1, source_target_pairs={{0,8},{8,0},{1,9},{9,1},{2,10},{10,2},{3,11},{11,3},{4,12},{12,4},... | collective-permute-start | bytes 6291464 | tf_op jit(solution)/shard_map/ppermute | solution.py:32
  44.3 5.5 %copy-start.2 = (f32[256,512]{1,0:T(8,128)S(1)}, f32[256,512]{1,0:T(8,128)}, u32[]{:S(2)}) copy-start(f32[256,512]{1,0:T(8,128)} %get-tuple-element.53.refs_3_.refs_2_) | copy-start | bytes 1572868
  44.3 5.5 %copy-start.4 = (f32[256,512]{1,0:T(8,128)S(1)}, f32[256,512]{1,0:T(8,128)}, u32[]{:S(2)}) copy-start(f32[256,512]{1,0:T(8,128)} %copy-done.3) | copy-start | bytes 1572868
  49.4 24.3 %collective-permute-start.8 = (bf16[2,256,1024]{2,1,0:T(8,128)(2,1)S(1)}, bf16[2,256,1024]{2,1,0:T(8,128)(2,1)S(1)}, u32[]{:S(2)}, u32[]{:S(2)}) collective-permute-start(bf16[2,256,1024]{2,1,0:T(8,128)(2,1)S(1)} %get-tuple-element.59), channel_id=1, source_target_pairs={{0,2},{2,0},{4,6},{6,4},{1,3},{3,1},{5,7},{7,5},{8,10},{10,8},{12,... | collective-permute-start | bytes 3145736 | tf_op jit(solution)/shard_map/ppermute | solution.py:32
  50.7 11.2 %collective-permute-start.9 = (bf16[128,512]{1,0:T(8,128)(2,1)S(1)}, bf16[128,512]{1,0:T(8,128)(2,1)S(1)}, u32[]{:S(2)}, u32[]{:S(2)}) collective-permute-start(bf16[128,512]{1,0:T(8,128)(2,1)S(1)} %get-tuple-element.63), channel_id=1, source_target_pairs={{0,8},{8,16},{16,24},{24,32},{32,40},{40,48},{48,56},{56,64},{64,7... | collective-permute-start | bytes 393224 | tf_op jit(solution)/shard_map/ppermute | solution.py:37
  56.1 5.8 %copy-start.8 = (bf16[256,512]{1,0:T(8,128)(2,1)S(1)}, bf16[256,512]{1,0:T(8,128)(2,1)}, u32[]{:S(2)}) copy-start(bf16[256,512]{1,0:T(8,128)(2,1)} %get-tuple-element.50.refs_0_.refs_3_) | copy-start | bytes 786436
  56.8 28.1 %collective-permute-start.14 = (bf16[512,512]{1,0:T(8,128)(2,1)S(1)}, bf16[512,512]{1,0:T(8,128)(2,1)S(1)}, u32[]{:S(2)}, u32[]{:S(2)}) collective-permute-start(bf16[512,512]{1,0:T(8,128)(2,1)S(1)} %get-tuple-element.75), channel_id=1, source_target_pairs={{0,64},{64,128},{128,192},{192,0},{1,65},{65,129},{129,193},{193,1... | collective-permute-start | bytes 1572872 | tf_op jit(solution)/shard_map/ppermute | solution.py:28
  58.3 27.1 %collective-permute-start.15 = (bf16[512,512]{1,0:T(8,128)(2,1)S(1)}, bf16[512,512]{1,0:T(8,128)(2,1)S(1)}, u32[]{:S(2)}, u32[]{:S(2)}) collective-permute-start(bf16[512,512]{1,0:T(8,128)(2,1)S(1)} %get-tuple-element.76), channel_id=1, source_target_pairs={{0,128},{64,192},{128,0},{192,64},{1,129},{65,193},{129,1},{193,65... | collective-permute-start | bytes 1572872 | tf_op jit(solution)/shard_map/ppermute | solution.py:28
  60.8 24.7 %collective-permute-start.16 = (bf16[512,512]{1,0:T(8,128)(2,1)S(1)}, bf16[512,512]{1,0:T(8,128)(2,1)S(1)}, u32[]{:S(2)}, u32[]{:S(2)}) collective-permute-start(bf16[512,512]{1,0:T(8,128)(2,1)S(1)} %get-tuple-element.77), channel_id=1, source_target_pairs={{0,192},{64,0},{128,64},{192,128},{1,193},{65,1},{129,65},{193,129... | collective-permute-start | bytes 1572872 | tf_op jit(solution)/shard_map/ppermute | solution.py:28
  68.6 1.4 %collective-permute-start.11 = (f32[64,512]{1,0:T(8,128)S(1)}, f32[64,512]{1,0:T(8,128)S(1)}, u32[]{:S(2)}, u32[]{:S(2)}) collective-permute-start(f32[64,512]{1,0:T(8,128)S(1)} %get-tuple-element.68), channel_id=1, source_target_pairs={{0,8},{8,0},{1,9},{9,1},{2,10},{10,2},{3,11},{11,3},{4,12},{12,4},... | collective-permute-start | bytes 393224 | tf_op jit(solution)/shard_map/ppermute | solution.py:32
  74.4 21.6 %collective-permute-start.12 = (bf16[256,1024]{1,0:T(8,128)(2,1)S(1)}, bf16[256,1024]{1,0:T(8,128)(2,1)S(1)}, u32[]{:S(2)}, u32[]{:S(2)}) collective-permute-start(bf16[256,1024]{1,0:T(8,128)(2,1)S(1)} %get-tuple-element.71), channel_id=1, source_target_pairs={{0,6},{2,4},{4,2},{6,0},{1,7},{3,5},{5,3},{7,1},{8,14},{10,12},{12... | collective-permute-start | bytes 1572872 | tf_op jit(solution)/shard_map/ppermute | solution.py:32
  75.7 7.0 %collective-permute-start.20 = (bf16[64,512]{1,0:T(8,128)(2,1)S(1)}, bf16[64,512]{1,0:T(8,128)(2,1)S(1)}, u32[]{:S(2)}, u32[]{:S(2)}) collective-permute-start(bf16[64,512]{1,0:T(8,128)(2,1)S(1)} %get-tuple-element.86), channel_id=1, source_target_pairs={{0,16},{16,0},{32,48},{48,32},{1,17},{17,1},{33,49},{49,33},{2,18}... | collective-permute-start | bytes 196616 | tf_op jit(solution)/shard_map/ppermute | solution.py:32
  83.3 4.4 %collective-permute-start.21 = (bf16[64,512]{1,0:T(8,128)(2,1)S(1)}, bf16[64,512]{1,0:T(8,128)(2,1)S(1)}, u32[]{:S(2)}, u32[]{:S(2)}) collective-permute-start(bf16[64,512]{1,0:T(8,128)(2,1)S(1)} %get-tuple-element.88), channel_id=1, source_target_pairs={{0,32},{16,48},{32,0},{48,16},{1,33},{17,49},{33,1},{49,17},{2,34}... | collective-permute-start | bytes 196616 | tf_op jit(solution)/shard_map/ppermute | solution.py:32
  88.4 11.9 %copy-start.1 = (bf16[256,512]{1,0:T(8,128)(2,1)S(1)}, bf16[256,512]{1,0:T(8,128)(2,1)}, u32[]{:S(2)}) copy-start(bf16[256,512]{1,0:T(8,128)(2,1)} %refs_2_.1) | copy-start | bytes 786436
  88.4 11.8 %copy-start.6 = (f32[4,128,128]{2,1,0:T(8,128)S(1)}, f32[4,128,128]{2,1,0:T(8,128)}, u32[]{:S(2)}) copy-start(f32[4,128,128]{2,1,0:T(8,128)} %get-tuple-element.52.refs_2_.refs_3_) | copy-start | bytes 786436
  88.4 4.9 %collective-permute-start.22 = (bf16[64,512]{1,0:T(8,128)(2,1)S(1)}, bf16[64,512]{1,0:T(8,128)(2,1)S(1)}, u32[]{:S(2)}, u32[]{:S(2)}) collective-permute-start(bf16[64,512]{1,0:T(8,128)(2,1)S(1)} %get-tuple-element.90), channel_id=1, source_target_pairs={{0,64},{64,0},{128,192},{192,128},{1,65},{65,1},{129,193},{193,129... | collective-permute-start | bytes 196616 | tf_op jit(solution)/shard_map/ppermute | solution.py:32
  89.7 17.0 %collective-permute-start.17 = (bf16[512,128]{1,0:T(8,128)(2,1)S(1)}, bf16[512,128]{1,0:T(8,128)(2,1)S(1)}, u32[]{:S(2)}, u32[]{:S(2)}) collective-permute-start(bf16[512,128]{1,0:T(8,128)(2,1)S(1)} %get-tuple-element.79), channel_id=1, source_target_pairs={{0,16},{16,0},{32,48},{48,32},{1,17},{17,1},{33,49},{49,33},{2,18}... | collective-permute-start | bytes 393224 | tf_op jit(solution)/shard_map/ppermute | solution.py:32
  91.2 15.5 %collective-permute-start.18 = (bf16[512,128]{1,0:T(8,128)(2,1)S(1)}, bf16[512,128]{1,0:T(8,128)(2,1)S(1)}, u32[]{:S(2)}, u32[]{:S(2)}) collective-permute-start(bf16[512,128]{1,0:T(8,128)(2,1)S(1)} %get-tuple-element.80), channel_id=1, source_target_pairs={{0,32},{16,48},{32,0},{48,16},{1,33},{17,49},{33,1},{49,17},{2,34}... | collective-permute-start | bytes 393224 | tf_op jit(solution)/shard_map/ppermute | solution.py:32
  91.8 15.0 %collective-permute-start.19 = (bf16[512,128]{1,0:T(8,128)(2,1)S(1)}, bf16[512,128]{1,0:T(8,128)(2,1)S(1)}, u32[]{:S(2)}, u32[]{:S(2)}) collective-permute-start(bf16[512,128]{1,0:T(8,128)(2,1)S(1)} %get-tuple-element.81), channel_id=1, source_target_pairs={{0,48},{16,32},{32,16},{48,0},{1,49},{17,33},{33,17},{49,1},{2,50}... | collective-permute-start | bytes 393224 | tf_op jit(solution)/shard_map/ppermute | solution.py:32
  94.0 12.8 %collective-permute-start.23 = (bf16[64,512]{1,0:T(8,128)(2,1)S(1)}, bf16[64,512]{1,0:T(8,128)(2,1)S(1)}, u32[]{:S(2)}, u32[]{:S(2)}) collective-permute-start(bf16[64,512]{1,0:T(8,128)(2,1)S(1)} %get-tuple-element.92), channel_id=1, source_target_pairs={{0,192},{64,128},{128,64},{192,0},{1,193},{65,129},{129,65},{193,1... | collective-permute-start | bytes 196616 | tf_op jit(solution)/shard_map/ppermute | solution.py:32
  96.2 23.0 %collective-permute-start.13 = (bf16[256,512]{1,0:T(8,128)(2,1)S(1)}, bf16[256,512]{1,0:T(8,128)(2,1)S(1)}, u32[]{:S(2)}, u32[]{:S(2)}) collective-permute-start(bf16[256,512]{1,0:T(8,128)(2,1)S(1)} %get-tuple-element.73), channel_id=1, source_target_pairs={{0,1},{1,0},{2,3},{3,2},{4,5},{5,4},{6,7},{7,6},{8,9},{9,8},{10,11... | collective-permute-start | bytes 786440 | tf_op jit(solution)/shard_map/ppermute | solution.py:32
  106.9 10.7 %collective-permute-start.24 = (f32[64,512]{1,0:T(8,128)S(1)}, f32[64,512]{1,0:T(8,128)S(1)}, u32[]{:S(2)}, u32[]{:S(2)}) collective-permute-start(f32[64,512]{1,0:T(8,128)S(1)} %last.1.refs_1_), channel_id=1, source_target_pairs={{0,8},{8,0},{1,9},{9,1},{2,10},{10,2},{3,11},{11,3},{4,12},{12,4},... | collective-permute-start | bytes 393224 | tf_op jit(solution)/shard_map/ppermute | solution.py:32
  (2 other events, 1.7 us)

commit v3 on v2

--- a/solution.py
+++ b/solution.py
@@ -406,13 +406,14 @@
         params=room(57),
     )
     later_rows = along_tokens(head, -1)
-    far = after(far, *[("tie", b) for b in near_blocks[1:]], ("tie", later_rows))
+    far = after(far, ("tie", later_rows))
     far_blocks = [far] + [shifted(far, "y", k) for k in (1, 2, 3)]
     grad_mix, grad_value, turned_value = call(
         "mix",
         mix_kernel,
         (plane, half_plane, struct((channels, rows), BF16)),
-        [("in", grad_conv), ("in", later_rows), ("in", turned), ("in", key), ("tie", far)],
+        [("in", grad_conv), ("in", later_rows), ("in", turned), ("in", key), ("tie", far)]
+        + [("tie", b) for b in near_blocks[1:]],
         [nat_shape, wide_shape, turn_shape, out_scratch],
         room(52),
     )

time: 120 us -> 118 us (0.983)
  waiting for transfers between devices: 16.5 us -> 11.9 us
    ppermute x2, waiting for transfers between devices: 8.07 us -> 3.67 us  [along_tokens(): lax.ppermute(block, SEQ, [(i, i + step) for i in range(n) if 0 <= i + ste...]
    unnamed x18 -> x20, local copies, waits for them, and re-layouts: 2.72 us -> 3.58 us
  transfers between devices with their start and end apart: 25 -> 25, of which waited for: 6 -> 6; matrix products, arithmetic and copies ran while one was open for 0% -> 0% of each run, Pallas kernels for 31% -> 32%
where the time goes in v3:
time: 118 us
  starting transfers between devices  59.3 us (50%)
  Pallas kernels  41.7 us (35%)
  waiting for transfers between devices  11.9 us (10%)
  local copies, waits for them, and re-layouts  3.67 us (3%)
    pallas_call x19, Pallas kernels, call(): pl.pallas_call(kernel, out_shape=out, in_specs=[SPECS[kind] for kind in k...  41.7 us
    ppermute x14, starting transfers between devices, crossed(): lax.ppermute(block, axis, [(i, i ^ d) for i in range(lax.axis_size(axis))])  36 us
    ppermute x9, starting transfers between devices, shifted(): return lax.ppermute(block, axis, [(i, (i + k) % n) for i in range(n)])  14.5 us
    ppermute x2, starting transfers between devices, along_tokens(): lax.ppermute(block, SEQ, [(i, i + step) for i in range(n) if 0 <= i + ste...  8.79 us
    ppermute x14, waiting for transfers between devices, crossed(): lax.ppermute(block, axis, [(i, i ^ d) for i in range(lax.axis_size(axis))])  7.21 us
    ppermute x2, waiting for transfers between devices, along_tokens(): lax.ppermute(block, SEQ, [(i, i + step) for i in range(n) if 0 <= i + ste...  3.67 us
    unnamed x20, local copies, waits for them, and re-layouts  3.58 us
  transfers between devices with their start and end apart: 25, of which 6 were waited for; matrix products, arithmetic and copies ran while one was open for 0% of the time, Pallas kernels for 32%

profile of v3, /device:TPU:1, one launch (start us, length us, event | category | flops | bytes accessed | tf_op | source)
XLA Modules:
  0.0 117.6 jit_solution(13243498980690017074)
XLA Ops:
  0.6 7.8 %collective-permute-start.1 = (bf16[256,512]{1,0:T(8,128)(2,1)}, bf16[256,512]{1,0:T(8,128)(2,1)S(1)}, u32[]{:S(2)}, u32[]{:S(2)}) collective-permute-start(bf16[256,512]{1,0:T(8,128)(2,1)} %refs_1_.3), channel_id=1, source_target_pairs={{0,1},{1,0},{2,3},{3,2},{4,5},{5,4},{6,7},{7,6},{8,9},{9,8},{10,11... | collective-permute-start | bytes 786440 | tf_op jit(solution)/shard_map/ppermute | solution.py:32
  8.5 1.3 %collective-permute-start.2 = (bf16[256,512]{1,0:T(8,128)(2,1)}, bf16[256,512]{1,0:T(8,128)(2,1)S(1)}, u32[]{:S(2)}, u32[]{:S(2)}) collective-permute-start(bf16[256,512]{1,0:T(8,128)(2,1)} %refs_1_.3), channel_id=1, source_target_pairs={{0,2},{2,4},{4,6},{6,0},{1,3},{3,5},{5,7},{7,1},{8,10},{10,12},{12... | collective-permute-start | bytes 786440 | tf_op jit(solution)/shard_map/ppermute | solution.py:28
  9.8 2.6 %collective-permute-start.3 = (bf16[256,512]{1,0:T(8,128)(2,1)}, bf16[256,512]{1,0:T(8,128)(2,1)S(1)}, u32[]{:S(2)}, u32[]{:S(2)}) collective-permute-start(bf16[256,512]{1,0:T(8,128)(2,1)} %refs_1_.3), channel_id=1, source_target_pairs={{0,4},{2,6},{4,0},{6,2},{1,5},{3,7},{5,1},{7,3},{8,12},{10,14},{12... | collective-permute-start | bytes 786440 | tf_op jit(solution)/shard_map/ppermute | solution.py:28
  12.4 1.1 collective-permute-start.4
  13.4 2.9 %prepare.1 = (bf16[256,512]{1,0:T(8,128)(2,1)}, bf16[128,512]{1,0:T(8,128)(2,1)}, f32[256,512]{1,0:T(8,128)}, f32[4,128,128]{2,1,0:T(8,128)}) custom-call(bf16[256,512]{1,0:T(8,128)(2,1)} %refs_2_.1, s32[256,512]{1,0:T(8,128)} %refs_1_.2, f32[4,256]{1,0:T(4,128)} %bitcast.9, f32[4,256]{1,0:T(4,128)} %bitcast.10, s32[256,512]{1,0:T(8,128)} %refs_4_.1, ...), custom_call_target="tpu_custom_call" | custom-call | flops 1750000000 | bytes 5775000 | tf_op jit(solution)/shard_map/prepare/pallas_call | solution.py:88
  16.4 3.7 %collective-permute-start = (bf16[128,512]{1,0:T(8,128)(2,1)}, bf16[128,512]{1,0:T(8,128)(2,1)S(1)}, u32[]{:S(2)}, u32[]{:S(2)}) collective-permute-start(bf16[128,512]{1,0:T(8,128)(2,1)} %get-tuple-element.51), channel_id=1, source_target_pairs={{8,0},{16,8},{24,16},{32,24},{40,32},{48,40},{56,48},{64,56},{72,6... | collective-permute-start | bytes 393224 | tf_op jit(solution)/shard_map/ppermute | solution.py:37
  20.2 3.7 %collective-permute-done.refs_1_ = bf16[128,512]{1,0:T(8,128)(2,1)S(1)} collective-permute-done((bf16[128,512]{1,0:T(8,128)(2,1)}, bf16[128,512]{1,0:T(8,128)(2,1)S(1)}, u32[]{:S(2)}, u32[]{:S(2)}) %collective-permute-start) | collective-permute-done | bytes 131104 | tf_op jit(solution)/shard_map/ppermute | solution.py:37
  24.6 2.6 %collective-permute-start.6 = (bf16[256,512]{1,0:T(8,128)(2,1)S(1)}, bf16[256,512]{1,0:T(8,128)(2,1)S(1)}, u32[]{:S(2)}, u32[]{:S(2)}) collective-permute-start(bf16[256,512]{1,0:T(8,128)(2,1)S(1)} %after.1.refs_4_.refs_5_), channel_id=1, source_target_pairs={{0,4},{2,6},{4,0},{6,2},{1,5},{3,7},{5,1},{7,3},{8,12},{10,14},{12... | collective-permute-start | bytes 786440 | tf_op jit(solution)/shard_map/ppermute | solution.py:28
  27.2 1.1 collective-permute-start.7
  30.9 7.5 %mix.1 = (f32[256,512]{1,0:T(8,128)}, bf16[256,512]{1,0:T(8,128)(2,1)S(1)}, bf16[512,256]{1,0:T(8,128)(2,1)S(1)}) custom-call(bf16[256,512]{1,0:T(8,128)(2,1)S(1)} %copy-done.8, bf16[128,512]{1,0:T(8,128)(2,1)S(1)} %collective-permute-done.refs_1_, f32[4,128,128]{2,1,0:T(8,128)S(1)} %copy-done.6, f32[256,512]{1,0:T(8,128)} %get-tuple-element.53.refs_3_.refs_2_, ...), custom_call_target="tpu_custom_call" | custom-call | flops 5390000128 | bytes 17787000 | tf_op jit(solution)/shard_map/mix/pallas_call | solution.py:88
  39.4 3.3 %weight.1 = (f32[4,512,512]{2,1,0:T(8,128)S(1)}, bf16[4,512,512]{2,1,0:T(8,128)(2,1)S(1)}, bf16[8,256,512]{2,1,0:T(8,128)(2,1)S(1)}, f32[8,128]{1,0:T(8,128)S(1)}) custom-call(s32[5]{0:T(128)S(1)} %stack.23.refs_0_, bf16[256,512]{1,0:T(8,128)(2,1)S(1)} %copy-done, bf16[256,512]{1,0:T(8,128)(2,1)S(1)} %collective-permute-done.2.refs_5_.refs_2_, ...), custom_call_target="tpu_custom_call" | custom-call | flops 2800000000 | bytes 9240000 | tf_op jit(solution)/shard_map/weight/pallas_call | solution.py:88
  42.9 5.1 %back.1 = (f32[2,256,1024]{2,1,0:T(8,128)S(1)}, bf16[2,256,1024]{2,1,0:T(8,128)(2,1)S(1)}, f32[256,512]{1,0:T(8,128)S(1)}, f32[8,128]{1,0:T(8,128)}) custom-call(s32[5]{0:T(128)S(1)} %stack.23.refs_0_, bf16[256,512]{1,0:T(8,128)(2,1)S(1)} %get-tuple-element.54.refs_1_, bf16[8,256,512]{2,1,0:T(8,128)(2,1)S(1)} %get-tuple-element.56.refs_2_, ...), custom_call_target="tpu_custom_call" | custom-call | flops 2590000128 | bytes 8547000 | tf_op jit(solution)/shard_map/back/pallas_call | solution.py:88
  49.4 5.1 %collective-permute-start.9 = (bf16[128,512]{1,0:T(8,128)(2,1)S(1)}, bf16[128,512]{1,0:T(8,128)(2,1)S(1)}, u32[]{:S(2)}, u32[]{:S(2)}) collective-permute-start(bf16[128,512]{1,0:T(8,128)(2,1)S(1)} %get-tuple-element.63), channel_id=1, source_target_pairs={{0,8},{8,16},{16,24},{24,32},{32,40},{40,48},{48,56},{56,64},{64,7... | collective-permute-start | bytes 393224 | tf_op jit(solution)/shard_map/ppermute | solution.py:37
  55.2 1.5 %collective-permute-start.14 = (bf16[512,512]{1,0:T(8,128)(2,1)S(1)}, bf16[512,512]{1,0:T(8,128)(2,1)S(1)}, u32[]{:S(2)}, u32[]{:S(2)}) collective-permute-start(bf16[512,512]{1,0:T(8,128)(2,1)S(1)} %get-tuple-element.75), channel_id=1, source_target_pairs={{0,64},{64,128},{128,192},{192,0},{1,65},{65,129},{129,193},{193,1... | collective-permute-start | bytes 1572872 | tf_op jit(solution)/shard_map/ppermute | solution.py:28
  56.7 2.5 %collective-permute-start.15 = (bf16[512,512]{1,0:T(8,128)(2,1)S(1)}, bf16[512,512]{1,0:T(8,128)(2,1)S(1)}, u32[]{:S(2)}, u32[]{:S(2)}) collective-permute-start(bf16[512,512]{1,0:T(8,128)(2,1)S(1)} %get-tuple-element.76), channel_id=1, source_target_pairs={{0,128},{64,192},{128,0},{192,64},{1,129},{65,193},{129,1},{193,65... | collective-permute-start | bytes 1572872 | tf_op jit(solution)/shard_map/ppermute | solution.py:28
  59.1 1.2 collective-permute-start.16
  60.3 6.7 %taps.1 = (f32[64,512]{1,0:T(8,128)S(1)}, f32[64,512]{1,0:T(8,128)S(1)}, f32[8,128]{1,0:T(8,128)}) custom-call(s32[5]{0:T(128)S(1)} %stack.23.refs_0_, bf16[256,512]{1,0:T(8,128)(2,1)S(1)} %get-tuple-element.62.refs_1_.refs_0_, bf16[128,512]{1,0:T(8,128)(2,1)S(1)} %collective-permute-done.9.refs_2_.refs_1_, bf16[256,512]{1,0:T(8,128)(2,1)S(1)} %copy-done.9, ...), custom_call_target="tpu_custom_call" | custom-call | flops 5600000000 | bytes 18480000 | tf_op jit(solution)/shard_map/taps/pallas_call | solution.py:88
  67.1 1.3 %collective-permute-done.11.refs_1_ = f32[64,512]{1,0:T(8,128)S(1)} collective-permute-done((f32[64,512]{1,0:T(8,128)S(1)}, f32[64,512]{1,0:T(8,128)S(1)}, u32[]{:S(2)}, u32[]{:S(2)}) %collective-permute-start.11) | collective-permute-done | bytes 131104 | tf_op jit(solution)/shard_map/ppermute | solution.py:32
  68.5 3.8 %collective-permute-done.8.refs_1_ = bf16[2,256,1024]{2,1,0:T(8,128)(2,1)S(1)} collective-permute-done((bf16[2,256,1024]{2,1,0:T(8,128)(2,1)S(1)}, bf16[2,256,1024]{2,1,0:T(8,128)(2,1)S(1)}, u32[]{:S(2)}, u32[]{:S(2)}) %collective-permute-start.8) | collective-permute-done | bytes 1048608 | tf_op jit(solution)/shard_map/ppermute | solution.py:32
  73.0 2.5 %collective-permute-start.12 = (bf16[256,1024]{1,0:T(8,128)(2,1)S(1)}, bf16[256,1024]{1,0:T(8,128)(2,1)S(1)}, u32[]{:S(2)}, u32[]{:S(2)}) collective-permute-start(bf16[256,1024]{1,0:T(8,128)(2,1)S(1)} %get-tuple-element.71), channel_id=1, source_target_pairs={{0,6},{2,4},{4,2},{6,0},{1,7},{3,5},{5,3},{7,1},{8,14},{10,12},{12... | collective-permute-start | bytes 1572872 | tf_op jit(solution)/shard_map/ppermute | solution.py:32
  75.6 2.5 %collective-permute-start.20 = (bf16[64,512]{1,0:T(8,128)(2,1)S(1)}, bf16[64,512]{1,0:T(8,128)(2,1)S(1)}, u32[]{:S(2)}, u32[]{:S(2)}) collective-permute-start(bf16[64,512]{1,0:T(8,128)(2,1)S(1)} %get-tuple-element.86), channel_id=1, source_target_pairs={{0,16},{16,0},{32,48},{48,32},{1,17},{17,1},{33,49},{49,33},{2,18}... | collective-permute-start | bytes 196616 | tf_op jit(solution)/shard_map/ppermute | solution.py:32
  78.0 1.9 %collective-permute-done.20.refs_1_ = bf16[64,512]{1,0:T(8,128)(2,1)S(1)} collective-permute-done((bf16[64,512]{1,0:T(8,128)(2,1)S(1)}, bf16[64,512]{1,0:T(8,128)(2,1)S(1)}, u32[]{:S(2)}, u32[]{:S(2)}) %collective-permute-start.20) | collective-permute-done | bytes 65568 | tf_op jit(solution)/shard_map/ppermute | solution.py:32
  80.6 2.0 %collective-permute-start.21 = (bf16[64,512]{1,0:T(8,128)(2,1)S(1)}, bf16[64,512]{1,0:T(8,128)(2,1)S(1)}, u32[]{:S(2)}, u32[]{:S(2)}) collective-permute-start(bf16[64,512]{1,0:T(8,128)(2,1)S(1)} %get-tuple-element.88), channel_id=1, source_target_pairs={{0,32},{16,48},{32,0},{48,16},{1,33},{17,49},{33,1},{49,17},{2,34}... | collective-permute-start | bytes 196616 | tf_op jit(solution)/shard_map/ppermute | solution.py:32
  83.6 1.2 %gather.1 = (f32[512,128]{1,0:T(8,128)S(1)}, bf16[512,128]{1,0:T(8,128)(2,1)S(1)}, bf16[512,128]{1,0:T(8,128)(2,1)S(1)}, bf16[512,128]{1,0:T(8,128)(2,1)S(1)}, f32[8,128]{1,0:T(8,128)S(1)}) custom-call(s32[5]{0:T(128)S(1)} %stack.23.refs_0_, f32[512,512]{1,0:T(8,128)S(1)} %get-tuple-element.74.refs_1_, bf16[512,512]{1,0:T(8,128)(2,1)S(1)} %collective-permute-done.14.refs_2_, ...), custom_call_target="tpu_custom_call" | custom-call | flops 1050000000 | bytes 3465000 | tf_op jit(solution)/shard_map/gather/pallas_call | solution.py:88
  85.7 2.8 %collective-permute-start.22 = (bf16[64,512]{1,0:T(8,128)(2,1)S(1)}, bf16[64,512]{1,0:T(8,128)(2,1)S(1)}, u32[]{:S(2)}, u32[]{:S(2)}) collective-permute-start(bf16[64,512]{1,0:T(8,128)(2,1)S(1)} %get-tuple-element.90), channel_id=1, source_target_pairs={{0,64},{64,0},{128,192},{192,128},{1,65},{65,1},{129,193},{193,129... | collective-permute-start | bytes 196616 | tf_op jit(solution)/shard_map/ppermute | solution.py:32
  89.6 2.5 %collective-permute-start.19 = (bf16[512,128]{1,0:T(8,128)(2,1)S(1)}, bf16[512,128]{1,0:T(8,128)(2,1)S(1)}, u32[]{:S(2)}, u32[]{:S(2)}) collective-permute-start(bf16[512,128]{1,0:T(8,128)(2,1)S(1)} %get-tuple-element.81), channel_id=1, source_target_pairs={{0,48},{16,32},{32,16},{48,0},{1,49},{17,33},{33,17},{49,1},{2,50}... | collective-permute-start | bytes 393224 | tf_op jit(solution)/shard_map/ppermute | solution.py:32
  92.8 1.9 %collective-permute-start.23 = (bf16[64,512]{1,0:T(8,128)(2,1)S(1)}, bf16[64,512]{1,0:T(8,128)(2,1)S(1)}, u32[]{:S(2)}, u32[]{:S(2)}) collective-permute-start(bf16[64,512]{1,0:T(8,128)(2,1)S(1)} %get-tuple-element.92), channel_id=1, source_target_pairs={{0,192},{64,128},{128,64},{192,0},{1,193},{65,129},{129,65},{193,1... | collective-permute-start | bytes 196616 | tf_op jit(solution)/shard_map/ppermute | solution.py:32
  94.8 1.1 collective-permute-start.13
  95.9 6.5 %conv.1 = (f32[256,512]{1,0:T(8,128)}, f32[8,128]{1,0:T(8,128)S(1)}) custom-call(bf16[256,512]{1,0:T(8,128)(2,1)S(1)} %get-tuple-element.62.refs_1_.refs_0_, bf16[128,512]{1,0:T(8,128)(2,1)S(1)} %collective-permute-done.9.refs_2_.refs_1_, bf16[256,512]{1,0:T(8,128)(2,1)S(1)} %copy-done.1, f32[4,128,128]{2,1,0:T(8,128)S(1)} %copy-done.7, ...), custom_call_target="tpu_custom_call" | custom-call | flops 5880000000 | bytes 19404000 | tf_op jit(solution)/shard_map/conv/pallas_call | solution.py:88
  102.5 11.1 %collective-permute-start.24 = (f32[64,512]{1,0:T(8,128)S(1)}, f32[64,512]{1,0:T(8,128)S(1)}, u32[]{:S(2)}, u32[]{:S(2)}) collective-permute-start(f32[64,512]{1,0:T(8,128)S(1)} %last.1.refs_1_), channel_id=1, source_target_pairs={{0,8},{8,0},{1,9},{9,1},{2,10},{10,2},{3,11},{11,3},{4,12},{12,4},... | collective-permute-start | bytes 393224 | tf_op jit(solution)/shard_map/ppermute | solution.py:32
  113.6 1.4 %finish.1 = f32[128,512]{1,0:T(8,128)} custom-call(f32[512,128]{1,0:T(8,128)S(1)} %get-tuple-element.78.refs_0_, bf16[512,128]{1,0:T(8,128)(2,1)S(1)} %collective-permute-done.17.refs_1_.refs_2_, bf16[512,128]{1,0:T(8,128)(2,1)S(1)} %collective-permute-done.18.refs_2_.refs_3_, bf16[512,128]{1,0:T(8,128)(2,1)S(1)} %collective-permute-done.19.refs_3_.refs_4_, ...), custom_call_target="tpu_custom_call" | custom-call | flops 910000000 | bytes 3003000 | tf_op jit(solution)/shard_map/finish/pallas_call | solution.py:88
  115.0 1.6 %ends.1 = f32[512,128]{1,0:T(8,128)} custom-call(s32[5]{0:T(128)S(1)} %stack.23.refs_0_, f32[64,512]{1,0:T(8,128)S(1)} %last.1.refs_1_, f32[64,512]{1,0:T(8,128)S(1)} %collective-permute-done.24.refs_2_), custom_call_target="tpu_custom_call" | custom-call | flops 910000000 | bytes 3003000 | tf_op jit(solution)/shard_map/ends/pallas_call | solution.py:88
  (59 shorter events, 12.9 us)
Async XLA Ops:
  0.6 23.2 %collective-permute-start.1 = (bf16[256,512]{1,0:T(8,128)(2,1)}, bf16[256,512]{1,0:T(8,128)(2,1)S(1)}, u32[]{:S(2)}, u32[]{:S(2)}) collective-permute-start(bf16[256,512]{1,0:T(8,128)(2,1)} %refs_1_.3), channel_id=1, source_target_pairs={{0,1},{1,0},{2,3},{3,2},{4,5},{5,4},{6,7},{7,6},{8,9},{9,8},{10,11... | collective-permute-start | bytes 786440 | tf_op jit(solution)/shard_map/ppermute | solution.py:32
  8.5 18.8 %collective-permute-start.2 = (bf16[256,512]{1,0:T(8,128)(2,1)}, bf16[256,512]{1,0:T(8,128)(2,1)S(1)}, u32[]{:S(2)}, u32[]{:S(2)}) collective-permute-start(bf16[256,512]{1,0:T(8,128)(2,1)} %refs_1_.3), channel_id=1, source_target_pairs={{0,2},{2,4},{4,6},{6,0},{1,3},{3,5},{5,7},{7,1},{8,10},{10,12},{12... | collective-permute-start | bytes 786440 | tf_op jit(solution)/shard_map/ppermute | solution.py:28
  9.8 18.5 %collective-permute-start.3 = (bf16[256,512]{1,0:T(8,128)(2,1)}, bf16[256,512]{1,0:T(8,128)(2,1)S(1)}, u32[]{:S(2)}, u32[]{:S(2)}) collective-permute-start(bf16[256,512]{1,0:T(8,128)(2,1)} %refs_1_.3), channel_id=1, source_target_pairs={{0,4},{2,6},{4,0},{6,2},{1,5},{3,7},{5,1},{7,3},{8,12},{10,14},{12... | collective-permute-start | bytes 786440 | tf_op jit(solution)/shard_map/ppermute | solution.py:28
  12.4 15.9 %collective-permute-start.4 = (bf16[256,512]{1,0:T(8,128)(2,1)}, bf16[256,512]{1,0:T(8,128)(2,1)S(1)}, u32[]{:S(2)}, u32[]{:S(2)}) collective-permute-start(bf16[256,512]{1,0:T(8,128)(2,1)} %refs_1_.3), channel_id=1, source_target_pairs={{0,6},{2,0},{4,2},{6,4},{1,7},{3,1},{5,3},{7,5},{8,14},{10,8},{12,... | collective-permute-start | bytes 786440 | tf_op jit(solution)/shard_map/ppermute | solution.py:28
  16.4 7.5 %collective-permute-start = (bf16[128,512]{1,0:T(8,128)(2,1)}, bf16[128,512]{1,0:T(8,128)(2,1)S(1)}, u32[]{:S(2)}, u32[]{:S(2)}) collective-permute-start(bf16[128,512]{1,0:T(8,128)(2,1)} %get-tuple-element.51), channel_id=1, source_target_pairs={{8,0},{16,8},{24,16},{32,24},{40,32},{48,40},{56,48},{64,56},{72,6... | collective-permute-start | bytes 393224 | tf_op jit(solution)/shard_map/ppermute | solution.py:37
  23.9 14.6 %collective-permute-start.5 = (bf16[256,512]{1,0:T(8,128)(2,1)S(1)}, bf16[256,512]{1,0:T(8,128)(2,1)S(1)}, u32[]{:S(2)}, u32[]{:S(2)}) collective-permute-start(bf16[256,512]{1,0:T(8,128)(2,1)S(1)} %after.1.refs_4_.refs_5_), channel_id=1, source_target_pairs={{0,2},{2,4},{4,6},{6,0},{1,3},{3,5},{5,7},{7,1},{8,10},{10,12},{12... | collective-permute-start | bytes 786440 | tf_op jit(solution)/shard_map/ppermute | solution.py:28
  24.6 13.9 %collective-permute-start.6 = (bf16[256,512]{1,0:T(8,128)(2,1)S(1)}, bf16[256,512]{1,0:T(8,128)(2,1)S(1)}, u32[]{:S(2)}, u32[]{:S(2)}) collective-permute-start(bf16[256,512]{1,0:T(8,128)(2,1)S(1)} %after.1.refs_4_.refs_5_), channel_id=1, source_target_pairs={{0,4},{2,6},{4,0},{6,2},{1,5},{3,7},{5,1},{7,3},{8,12},{10,14},{12... | collective-permute-start | bytes 786440 | tf_op jit(solution)/shard_map/ppermute | solution.py:28
  27.2 11.2 %collective-permute-start.7 = (bf16[256,512]{1,0:T(8,128)(2,1)S(1)}, bf16[256,512]{1,0:T(8,128)(2,1)S(1)}, u32[]{:S(2)}, u32[]{:S(2)}) collective-permute-start(bf16[256,512]{1,0:T(8,128)(2,1)S(1)} %after.1.refs_4_.refs_5_), channel_id=1, source_target_pairs={{0,6},{2,0},{4,2},{6,4},{1,7},{3,1},{5,3},{7,5},{8,14},{10,8},{12,... | collective-permute-start | bytes 786440 | tf_op jit(solution)/shard_map/ppermute | solution.py:28
  30.9 7.6 %copy-start = (bf16[256,512]{1,0:T(8,128)(2,1)S(1)}, bf16[256,512]{1,0:T(8,128)(2,1)}, u32[]{:S(2)}) copy-start(bf16[256,512]{1,0:T(8,128)(2,1)} %refs_1_.3) | copy-start | bytes 786436
  38.5 1.0 copy-start.3
  42.8 11.7 %collective-permute-start.10 = (bf16[4,512,512]{2,1,0:T(8,128)(2,1)S(1)}, bf16[4,512,512]{2,1,0:T(8,128)(2,1)S(1)}, u32[]{:S(2)}, u32[]{:S(2)}) collective-permute-start(bf16[4,512,512]{2,1,0:T(8,128)(2,1)S(1)} %get-tuple-element.65), channel_id=1, source_target_pairs={{0,8},{8,0},{1,9},{9,1},{2,10},{10,2},{3,11},{11,3},{4,12},{12,4},... | collective-permute-start | bytes 6291464 | tf_op jit(solution)/shard_map/ppermute | solution.py:32
  42.9 5.6 %copy-start.4 = (f32[256,512]{1,0:T(8,128)S(1)}, f32[256,512]{1,0:T(8,128)}, u32[]{:S(2)}) copy-start(f32[256,512]{1,0:T(8,128)} %get-tuple-element.53.refs_3_.refs_2_) | copy-start | bytes 1572868
  42.9 5.6 %copy-start.5 = (f32[256,512]{1,0:T(8,128)S(1)}, f32[256,512]{1,0:T(8,128)}, u32[]{:S(2)}) copy-start(f32[256,512]{1,0:T(8,128)} %get-tuple-element.61.refs_1_) | copy-start | bytes 1572868
  48.0 24.3 %collective-permute-start.8 = (bf16[2,256,1024]{2,1,0:T(8,128)(2,1)S(1)}, bf16[2,256,1024]{2,1,0:T(8,128)(2,1)S(1)}, u32[]{:S(2)}, u32[]{:S(2)}) collective-permute-start(bf16[2,256,1024]{2,1,0:T(8,128)(2,1)S(1)} %get-tuple-element.59), channel_id=1, source_target_pairs={{0,2},{2,0},{4,6},{6,4},{1,3},{3,1},{5,7},{7,5},{8,10},{10,8},{12,... | collective-permute-start | bytes 3145736 | tf_op jit(solution)/shard_map/ppermute | solution.py:32
  49.4 10.9 %collective-permute-start.9 = (bf16[128,512]{1,0:T(8,128)(2,1)S(1)}, bf16[128,512]{1,0:T(8,128)(2,1)S(1)}, u32[]{:S(2)}, u32[]{:S(2)}) collective-permute-start(bf16[128,512]{1,0:T(8,128)(2,1)S(1)} %get-tuple-element.63), channel_id=1, source_target_pairs={{0,8},{8,16},{16,24},{24,32},{32,40},{40,48},{48,56},{56,64},{64,7... | collective-permute-start | bytes 393224 | tf_op jit(solution)/shard_map/ppermute | solution.py:37
  54.5 5.8 %copy-start.9 = (bf16[256,512]{1,0:T(8,128)(2,1)S(1)}, bf16[256,512]{1,0:T(8,128)(2,1)}, u32[]{:S(2)}) copy-start(bf16[256,512]{1,0:T(8,128)(2,1)} %get-tuple-element.50.refs_0_.refs_3_) | copy-start | bytes 786436
  55.2 27.5 %collective-permute-start.14 = (bf16[512,512]{1,0:T(8,128)(2,1)S(1)}, bf16[512,512]{1,0:T(8,128)(2,1)S(1)}, u32[]{:S(2)}, u32[]{:S(2)}) collective-permute-start(bf16[512,512]{1,0:T(8,128)(2,1)S(1)} %get-tuple-element.75), channel_id=1, source_target_pairs={{0,64},{64,128},{128,192},{192,0},{1,65},{65,129},{129,193},{193,1... | collective-permute-start | bytes 1572872 | tf_op jit(solution)/shard_map/ppermute | solution.py:28
  56.7 27.0 %collective-permute-start.15 = (bf16[512,512]{1,0:T(8,128)(2,1)S(1)}, bf16[512,512]{1,0:T(8,128)(2,1)S(1)}, u32[]{:S(2)}, u32[]{:S(2)}) collective-permute-start(bf16[512,512]{1,0:T(8,128)(2,1)S(1)} %get-tuple-element.76), channel_id=1, source_target_pairs={{0,128},{64,192},{128,0},{192,64},{1,129},{65,193},{129,1},{193,65... | collective-permute-start | bytes 1572872 | tf_op jit(solution)/shard_map/ppermute | solution.py:28
  59.1 24.5 %collective-permute-start.16 = (bf16[512,512]{1,0:T(8,128)(2,1)S(1)}, bf16[512,512]{1,0:T(8,128)(2,1)S(1)}, u32[]{:S(2)}, u32[]{:S(2)}) collective-permute-start(bf16[512,512]{1,0:T(8,128)(2,1)S(1)} %get-tuple-element.77), channel_id=1, source_target_pairs={{0,192},{64,0},{128,64},{192,128},{1,193},{65,1},{129,65},{193,129... | collective-permute-start | bytes 1572872 | tf_op jit(solution)/shard_map/ppermute | solution.py:28
  66.9 1.4 %collective-permute-start.11 = (f32[64,512]{1,0:T(8,128)S(1)}, f32[64,512]{1,0:T(8,128)S(1)}, u32[]{:S(2)}, u32[]{:S(2)}) collective-permute-start(f32[64,512]{1,0:T(8,128)S(1)} %get-tuple-element.68), channel_id=1, source_target_pairs={{0,8},{8,0},{1,9},{9,1},{2,10},{10,2},{3,11},{11,3},{4,12},{12,4},... | collective-permute-start | bytes 393224 | tf_op jit(solution)/shard_map/ppermute | solution.py:32
  73.0 21.7 %collective-permute-start.12 = (bf16[256,1024]{1,0:T(8,128)(2,1)S(1)}, bf16[256,1024]{1,0:T(8,128)(2,1)S(1)}, u32[]{:S(2)}, u32[]{:S(2)}) collective-permute-start(bf16[256,1024]{1,0:T(8,128)(2,1)S(1)} %get-tuple-element.71), channel_id=1, source_target_pairs={{0,6},{2,4},{4,2},{6,0},{1,7},{3,5},{5,3},{7,1},{8,14},{10,12},{12... | collective-permute-start | bytes 1572872 | tf_op jit(solution)/shard_map/ppermute | solution.py:32
  75.6 4.4 %collective-permute-start.20 = (bf16[64,512]{1,0:T(8,128)(2,1)S(1)}, bf16[64,512]{1,0:T(8,128)(2,1)S(1)}, u32[]{:S(2)}, u32[]{:S(2)}) collective-permute-start(bf16[64,512]{1,0:T(8,128)(2,1)S(1)} %get-tuple-element.86), channel_id=1, source_target_pairs={{0,16},{16,0},{32,48},{48,32},{1,17},{17,1},{33,49},{49,33},{2,18}... | collective-permute-start | bytes 196616 | tf_op jit(solution)/shard_map/ppermute | solution.py:32
  80.6 4.4 %collective-permute-start.21 = (bf16[64,512]{1,0:T(8,128)(2,1)S(1)}, bf16[64,512]{1,0:T(8,128)(2,1)S(1)}, u32[]{:S(2)}, u32[]{:S(2)}) collective-permute-start(bf16[64,512]{1,0:T(8,128)(2,1)S(1)} %get-tuple-element.88), channel_id=1, source_target_pairs={{0,32},{16,48},{32,0},{48,16},{1,33},{17,49},{33,1},{49,17},{2,34}... | collective-permute-start | bytes 196616 | tf_op jit(solution)/shard_map/ppermute | solution.py:32
  85.7 10.2 %copy-start.1 = (bf16[256,512]{1,0:T(8,128)(2,1)S(1)}, bf16[256,512]{1,0:T(8,128)(2,1)}, u32[]{:S(2)}) copy-start(bf16[256,512]{1,0:T(8,128)(2,1)} %refs_2_.1) | copy-start | bytes 786436
  85.7 10.2 %copy-start.7 = (f32[4,128,128]{2,1,0:T(8,128)S(1)}, f32[4,128,128]{2,1,0:T(8,128)}, u32[]{:S(2)}) copy-start(f32[4,128,128]{2,1,0:T(8,128)} %get-tuple-element.52.refs_2_.refs_3_) | copy-start | bytes 786436
  85.7 6.4 %collective-permute-start.22 = (bf16[64,512]{1,0:T(8,128)(2,1)S(1)}, bf16[64,512]{1,0:T(8,128)(2,1)S(1)}, u32[]{:S(2)}, u32[]{:S(2)}) collective-permute-start(bf16[64,512]{1,0:T(8,128)(2,1)S(1)} %get-tuple-element.90), channel_id=1, source_target_pairs={{0,64},{64,0},{128,192},{192,128},{1,65},{65,1},{129,193},{193,129... | collective-permute-start | bytes 196616 | tf_op jit(solution)/shard_map/ppermute | solution.py:32
  88.5 13.9 %collective-permute-start.17 = (bf16[512,128]{1,0:T(8,128)(2,1)S(1)}, bf16[512,128]{1,0:T(8,128)(2,1)S(1)}, u32[]{:S(2)}, u32[]{:S(2)}) collective-permute-start(bf16[512,128]{1,0:T(8,128)(2,1)S(1)} %get-tuple-element.79), channel_id=1, source_target_pairs={{0,16},{16,0},{32,48},{48,32},{1,17},{17,1},{33,49},{49,33},{2,18}... | collective-permute-start | bytes 393224 | tf_op jit(solution)/shard_map/ppermute | solution.py:32
  88.6 13.9 %collective-permute-start.18 = (bf16[512,128]{1,0:T(8,128)(2,1)S(1)}, bf16[512,128]{1,0:T(8,128)(2,1)S(1)}, u32[]{:S(2)}, u32[]{:S(2)}) collective-permute-start(bf16[512,128]{1,0:T(8,128)(2,1)S(1)} %get-tuple-element.80), channel_id=1, source_target_pairs={{0,32},{16,48},{32,0},{48,16},{1,33},{17,49},{33,1},{49,17},{2,34}... | collective-permute-start | bytes 393224 | tf_op jit(solution)/shard_map/ppermute | solution.py:32
  89.6 12.9 %collective-permute-start.19 = (bf16[512,128]{1,0:T(8,128)(2,1)S(1)}, bf16[512,128]{1,0:T(8,128)(2,1)S(1)}, u32[]{:S(2)}, u32[]{:S(2)}) collective-permute-start(bf16[512,128]{1,0:T(8,128)(2,1)S(1)} %get-tuple-element.81), channel_id=1, source_target_pairs={{0,48},{16,32},{32,16},{48,0},{1,49},{17,33},{33,17},{49,1},{2,50}... | collective-permute-start | bytes 393224 | tf_op jit(solution)/shard_map/ppermute | solution.py:32
  92.8 9.6 %collective-permute-start.23 = (bf16[64,512]{1,0:T(8,128)(2,1)S(1)}, bf16[64,512]{1,0:T(8,128)(2,1)S(1)}, u32[]{:S(2)}, u32[]{:S(2)}) collective-permute-start(bf16[64,512]{1,0:T(8,128)(2,1)S(1)} %get-tuple-element.92), channel_id=1, source_target_pairs={{0,192},{64,128},{128,64},{192,0},{1,193},{65,129},{129,65},{193,1... | collective-permute-start | bytes 196616 | tf_op jit(solution)/shard_map/ppermute | solution.py:32
  94.8 21.7 %collective-permute-start.13 = (bf16[256,512]{1,0:T(8,128)(2,1)S(1)}, bf16[256,512]{1,0:T(8,128)(2,1)S(1)}, u32[]{:S(2)}, u32[]{:S(2)}) collective-permute-start(bf16[256,512]{1,0:T(8,128)(2,1)S(1)} %get-tuple-element.73), channel_id=1, source_target_pairs={{0,1},{1,0},{2,3},{3,2},{4,5},{5,4},{6,7},{7,6},{8,9},{9,8},{10,11... | collective-permute-start | bytes 786440 | tf_op jit(solution)/shard_map/ppermute | solution.py:32
  102.5 12.5 %collective-permute-start.24 = (f32[64,512]{1,0:T(8,128)S(1)}, f32[64,512]{1,0:T(8,128)S(1)}, u32[]{:S(2)}, u32[]{:S(2)}) collective-permute-start(f32[64,512]{1,0:T(8,128)S(1)} %last.1.refs_1_), channel_id=1, source_target_pairs={{0,8},{8,0},{1,9},{9,1},{2,10},{10,2},{3,11},{11,3},{4,12},{12,4},... | collective-permute-start | bytes 393224 | tf_op jit(solution)/shard_map/ppermute | solution.py:32
  (3 other events, 2.6 us)

commit v4 on v3

--- a/solution.py
+++ b/solution.py
@@ -253,40 +253,43 @@
         query_grad[:, cols] = upstream[:, cols].astype(F32) * out[l]
 
 
-def back_kernel(place, value, held_x, weight, keep, give, values, mark, held, sems):
+def back_kernel(place, value, held_x, weight, *refs):
+    gives, keeps, (values, mark, held, sems) = refs[:2], refs[2:4], refs[4:]
     mark[...] = jnp.zeros_like(mark)
     x, y, zh = place[0], place[3], place[4]
     depth = held.shape[1]
-    copies = []
-    order = [(out, q, h) for out in (give, keep) for q in range(2) for h in range(2)]
-    owners = [y ^ (1 if out is give else 0) ^ (3 if q else 0) for out, q, h in order]
-    for i, (out, q, h) in enumerate(order):
+    copies, owners = [], []
+    order = [(give, h, q) for give in (True, False) for h in (1, 0) for q in range(2)]
+    for i, (give, h, q) in enumerate(order):
+        first, second = 1, 3
+        owners.append(y ^ (first if give else 0) ^ (second if q else 0))
         rows = pl.ds(pl.multiple_of((owners[i] * 2 + (zh ^ h)) * depth, depth), depth)
         copies.append(pltpu.make_async_copy(weight.at[rows, :], held.at[i], sems.at[i]))
     for copy in copies:
         copy.start()
     g = value[...]
-    for i, (out, q, h) in enumerate(order):
+    for i, (give, h, q) in enumerate(order):
         copies[i].wait()
         part = lax.dot_general(g, held[i], (((1,), (1,)), ((), ())), preferred_element_type=F32)
-        out[q, :, h * depth : (h + 1) * depth] = part.astype(out.dtype)
+        target = (gives if give else keeps)[h]
+        target[q] = part.astype(target.dtype)
         block = held_x[lax.rem(owners[i] - x + 4, 4) * 2 + h]
         part = jnp.dot(block, held[i], preferred_element_type=F32)
         values[...] = part if i == 0 else values[...] + part
 
 
-def pair_kernel(keep, received, own, sent, mark):
+def pair_kernel(keep, received, *refs):
+    own, sent, mark = refs[-3:] if len(refs) == 3 else refs[1:4]
     mark[...] = jnp.zeros_like(mark)
     own[...] = keep[0] + received[0].astype(F32)
     sent[...] = (keep[1] + received[1].astype(F32)).astype(BF16)
-
-
-def split_kernel(own, received, passing, staying, mark):
-    mark[...] = jnp.zeros_like(mark)
-    width = staying.shape[1]
-    for h, out in ((0, staying), (1, passing)):
-        cols = pl.ds(h * width, width)
-        out[...] = (own[:, cols] + received[:, cols].astype(F32)).astype(out.dtype)
+    if len(refs) > 3:
+        refs[4][...] = refs[0][...]
+
+
+def split_kernel(own, received, passing, mark):
+    mark[...] = jnp.zeros_like(mark)
+    passing[...] = (own[...] + received[...].astype(F32)).astype(BF16)
 
 
 def fetch(place, blocks, held, sems):
@@ -353,8 +356,8 @@
     out[...] = own[...] + received[...].astype(F32)
 
 
-def input_kernel(staying, arrived, out):
-    out[...] = staying[...].astype(F32) + arrived[...].astype(F32)
+def input_kernel(own, received, arrived, out):
+    out[...] = own[...] + received[...].astype(F32) + arrived[...].astype(F32)
 
 
 def ends_kernel(scale, place, own, other, out, both):
@@ -434,15 +437,12 @@
         room(40),
     )
     given_terms = crossed(give, "core", 1)
-    back_keep, back_give, values, _ = call(
+    give0, give1, keep0, keep1, values, _ = call(
         "back",
         back_kernel,
-        (
-            struct((2, rows, 2 * width), F32),
-            struct((2, rows, 2 * width), BF16),
-            plane,
-            mark,
-        ),
+        (struct((2, rows, width), BF16),) * 2
+        + (struct((2, rows, width), F32),) * 2
+        + (plane, mark),
         [("smem", place), ("vmem", grad_value), ("vmem", gathered), ("hbm", value_weight)]
         + [("mark", weight_mark)],
         [pltpu.VMEM((8, width, channels), BF16), eight],
@@ -485,17 +485,20 @@
         (half_taps, struct((tap_count // 2, channels), BF16), mark),
         [("vmem", kept), ("in", crossed(given, "core", 1))],
     )
-    back_own, back_sent, pair_mark = call(
+    block, half_block = struct((rows, width), F32), struct((rows, width), BF16)
+    own1, sent1, _, give0 = call(
         "pair",
         pair_kernel,
-        (struct((rows, 2 * width), F32), struct((rows, 2 * width), BF16), mark),
-        [("vmem", back_keep), ("in", crossed(back_give, "y", 1)), ("mark", middle1_mark)],
-    )
-    passing, staying, split_mark = call(
+        (block, half_block, mark, struct((2, rows, width), BF16)),
+        [("vmem", keep1), ("in", crossed(give1, "y", 1)), ("vmem", give0)]
+        + [("mark", taps_mark)],
+    )
+    received0 = crossed(give0, "y", 1)
+    passing, split_mark = call(
         "split",
         split_kernel,
-        (struct((rows, width), BF16), struct((rows, width), F32), mark),
-        [("vmem", back_own), ("in", crossed(back_sent, "y", 3))],
+        (half_block, mark),
+        [("vmem", own1), ("in", crossed(sent1, "y", 3))],
     )
     arrived_input = crossed(passing, "zh", 1)
     own, *ahead, gather_mark = call(
@@ -505,7 +508,8 @@
         + (struct((channels, LANES), BF16),) * 3
         + (mark,),
         [("smem", place), ("vmem", terms[0])]
-        + [("in", v) for v in sent],
+        + [("in", v) for v in sent]
+        + [("mark", split_mark)],
         [pltpu.VMEM((4, channels, LANES), F32)],
     )
     arrived = [crossed(ahead[d - 1], "zl", d) for d in (1, 2, 3)]
@@ -514,7 +518,7 @@
         conv_kernel,
         (plane, mark),
         [("vmem", product), ("in", earlier_rows), ("in", out_grad), ("vmem", turned)]
-        + [("mark", gather_mark), ("mark", split_mark)],
+        + [("mark", gather_mark)],
         [nat_shape, wide_shape, turn_shape, out_scratch],
     )
     filter_sum, filter_sent, middle2_mark = call(
@@ -534,7 +538,8 @@
         "middle4",
         middle_kernel,
         (half_taps, struct((tap_count // 2, channels), BF16), mark),
-        [("vmem", filter_sum), ("in", crossed(filter_sent, "x", 1))],
+        [("vmem", filter_sum), ("in", crossed(filter_sent, "x", 1))]
+        + [("tie", arrived_input)],
     )
     filter_sum = call(
         "last",
@@ -544,11 +549,17 @@
         + [("tie", v) for v in arrived]
         + [("mark", conv_mark)],
     )
+    own0, sent0, pair_mark = call(
+        "pair",
+        pair_kernel,
+        (block, half_block, mark),
+        [("vmem", keep0), ("in", received0), ("mark", gather_mark)],
+    )
     grad_input = call(
         "input",
         input_kernel,
-        struct((rows, width), F32),
-        [("vmem", staying), ("in", arrived_input)],
+        block,
+        [("vmem", own0), ("in", crossed(sent0, "y", 3)), ("in", arrived_input)],
     )
     grad_weight = call(
         "finish",

time: 118 us -> 123 us (1.042)
  waiting for transfers between devices: 11.9 us -> 26.9 us
  starting transfers between devices: 59.3 us -> 48.1 us
    ppermute x14 -> x16, waiting for transfers between devices: 7.21 us -> 23.2 us  [crossed(): lax.ppermute(block, axis, [(i, i ^ d) for i in range(lax.axis_size(axis))])]
    ppermute x14 -> x16, starting transfers between devices: 36 us -> 26.2 us  [crossed(): lax.ppermute(block, axis, [(i, i ^ d) for i in range(lax.axis_size(axis))])]
    ppermute x2, starting transfers between devices: 8.79 us -> 7.46 us  [along_tokens(): lax.ppermute(block, SEQ, [(i, i + step) for i in range(n) if 0 <= i + ste...]
    pallas_call x19 -> x20, Pallas kernels: 41.7 us -> 42.5 us  [call(): pl.pallas_call(kernel, out_shape=out, in_specs=[SPECS[kind] for kind in k...]
  transfers between devices with their start and end apart: 25 -> 27, of which waited for: 6 -> 4; matrix products, arithmetic and copies ran while one was open for 0% -> 0% of each run, Pallas kernels for 32% -> 31%
where the time goes in v4:
time: 123 us; the launch traced here: 122 us
  starting transfers between devices  48.1 us (39%)
  Pallas kernels  42.5 us (35%)
  waiting for transfers between devices  26.9 us (22%)
  local copies, waits for them, and re-layouts  3.66 us (3%)
    pallas_call x20, Pallas kernels, call(): pl.pallas_call(kernel, out_shape=out, in_specs=[SPECS[kind] for kind in k...  42.5 us
    ppermute x16, starting transfers between devices, crossed(): lax.ppermute(block, axis, [(i, i ^ d) for i in range(lax.axis_size(axis))])  26.2 us
    ppermute x16, waiting for transfers between devices, crossed(): lax.ppermute(block, axis, [(i, i ^ d) for i in range(lax.axis_size(axis))])  23.2 us
    ppermute x9, starting transfers between devices, shifted(): return lax.ppermute(block, axis, [(i, (i + k) % n) for i in range(n)])  14.5 us
    ppermute x2, starting transfers between devices, along_tokens(): lax.ppermute(block, SEQ, [(i, i + step) for i in range(n) if 0 <= i + ste...  7.46 us
    ppermute x2, waiting for transfers between devices, along_tokens(): lax.ppermute(block, SEQ, [(i, i + step) for i in range(n) if 0 <= i + ste...  3.67 us
    unnamed x20, local copies, waits for them, and re-layouts  3.57 us
  transfers between devices with their start and end apart: 27, of which 4 were waited for; matrix products, arithmetic and copies ran while one was open for 0% of the time, Pallas kernels for 31%

profile of v4, /device:TPU:1, one launch (start us, length us, event | category | flops | bytes accessed | tf_op | source)
XLA Modules:
  0.0 122.2 jit_solution(914777667528887799)
XLA Ops:
  0.6 7.8 %collective-permute-start.1 = (bf16[256,512]{1,0:T(8,128)(2,1)}, bf16[256,512]{1,0:T(8,128)(2,1)S(1)}, u32[]{:S(2)}, u32[]{:S(2)}) collective-permute-start(bf16[256,512]{1,0:T(8,128)(2,1)} %refs_1_.3), channel_id=1, source_target_pairs={{0,1},{1,0},{2,3},{3,2},{4,5},{5,4},{6,7},{7,6},{8,9},{9,8},{10,11... | collective-permute-start | bytes 786440 | tf_op jit(solution)/shard_map/ppermute | solution.py:32
  8.5 1.3 %collective-permute-start.2 = (bf16[256,512]{1,0:T(8,128)(2,1)}, bf16[256,512]{1,0:T(8,128)(2,1)S(1)}, u32[]{:S(2)}, u32[]{:S(2)}) collective-permute-start(bf16[256,512]{1,0:T(8,128)(2,1)} %refs_1_.3), channel_id=1, source_target_pairs={{0,2},{2,4},{4,6},{6,0},{1,3},{3,5},{5,7},{7,1},{8,10},{10,12},{12... | collective-permute-start | bytes 786440 | tf_op jit(solution)/shard_map/ppermute | solution.py:28
  9.8 2.6 %collective-permute-start.3 = (bf16[256,512]{1,0:T(8,128)(2,1)}, bf16[256,512]{1,0:T(8,128)(2,1)S(1)}, u32[]{:S(2)}, u32[]{:S(2)}) collective-permute-start(bf16[256,512]{1,0:T(8,128)(2,1)} %refs_1_.3), channel_id=1, source_target_pairs={{0,4},{2,6},{4,0},{6,2},{1,5},{3,7},{5,1},{7,3},{8,12},{10,14},{12... | collective-permute-start | bytes 786440 | tf_op jit(solution)/shard_map/ppermute | solution.py:28
  12.4 1.1 collective-permute-start.4
  13.4 2.9 %prepare.1 = (bf16[256,512]{1,0:T(8,128)(2,1)}, bf16[128,512]{1,0:T(8,128)(2,1)}, f32[256,512]{1,0:T(8,128)}, f32[4,128,128]{2,1,0:T(8,128)}) custom-call(bf16[256,512]{1,0:T(8,128)(2,1)} %refs_2_.1, s32[256,512]{1,0:T(8,128)} %refs_1_.2, f32[4,256]{1,0:T(4,128)} %bitcast.9, f32[4,256]{1,0:T(4,128)} %bitcast.10, s32[256,512]{1,0:T(8,128)} %refs_4_.1, ...), custom_call_target="tpu_custom_call" | custom-call | flops 1750000000 | bytes 5775000 | tf_op jit(solution)/shard_map/prepare/pallas_call | solution.py:88
  16.4 3.7 %collective-permute-start = (bf16[128,512]{1,0:T(8,128)(2,1)}, bf16[128,512]{1,0:T(8,128)(2,1)S(1)}, u32[]{:S(2)}, u32[]{:S(2)}) collective-permute-start(bf16[128,512]{1,0:T(8,128)(2,1)} %get-tuple-element.55), channel_id=1, source_target_pairs={{8,0},{16,8},{24,16},{32,24},{40,32},{48,40},{56,48},{64,56},{72,6... | collective-permute-start | bytes 393224 | tf_op jit(solution)/shard_map/ppermute | solution.py:37
  20.2 3.7 %collective-permute-done.refs_1_ = bf16[128,512]{1,0:T(8,128)(2,1)S(1)} collective-permute-done((bf16[128,512]{1,0:T(8,128)(2,1)}, bf16[128,512]{1,0:T(8,128)(2,1)S(1)}, u32[]{:S(2)}, u32[]{:S(2)}) %collective-permute-start) | collective-permute-done | bytes 131104 | tf_op jit(solution)/shard_map/ppermute | solution.py:37
  24.6 2.6 %collective-permute-start.6 = (bf16[256,512]{1,0:T(8,128)(2,1)S(1)}, bf16[256,512]{1,0:T(8,128)(2,1)S(1)}, u32[]{:S(2)}, u32[]{:S(2)}) collective-permute-start(bf16[256,512]{1,0:T(8,128)(2,1)S(1)} %after.1.refs_4_.refs_5_), channel_id=1, source_target_pairs={{0,4},{2,6},{4,0},{6,2},{1,5},{3,7},{5,1},{7,3},{8,12},{10,14},{12... | collective-permute-start | bytes 786440 | tf_op jit(solution)/shard_map/ppermute | solution.py:28
  27.2 1.1 collective-permute-start.7
  30.9 7.5 %mix.1 = (f32[256,512]{1,0:T(8,128)}, bf16[256,512]{1,0:T(8,128)(2,1)S(1)}, bf16[512,256]{1,0:T(8,128)(2,1)S(1)}) custom-call(bf16[256,512]{1,0:T(8,128)(2,1)S(1)} %copy-done.8, bf16[128,512]{1,0:T(8,128)(2,1)S(1)} %collective-permute-done.refs_1_, f32[4,128,128]{2,1,0:T(8,128)S(1)} %copy-done.6, f32[256,512]{1,0:T(8,128)} %get-tuple-element.57.refs_3_.refs_2_, ...), custom_call_target="tpu_custom_call" | custom-call | flops 5390000128 | bytes 17787000 | tf_op jit(solution)/shard_map/mix/pallas_call | solution.py:88
  39.4 3.3 %weight.1 = (f32[4,512,512]{2,1,0:T(8,128)S(1)}, bf16[4,512,512]{2,1,0:T(8,128)(2,1)S(1)}, bf16[8,256,512]{2,1,0:T(8,128)(2,1)S(1)}, f32[8,128]{1,0:T(8,128)S(1)}) custom-call(s32[5]{0:T(128)S(1)} %stack.23.refs_0_, bf16[256,512]{1,0:T(8,128)(2,1)S(1)} %copy-done, bf16[256,512]{1,0:T(8,128)(2,1)S(1)} %collective-permute-done.2.refs_5_.refs_2_, ...), custom_call_target="tpu_custom_call" | custom-call | flops 2800000000 | bytes 9240000 | tf_op jit(solution)/shard_map/weight/pallas_call | solution.py:88
  42.9 5.1 %back.1 = (bf16[2,256,512]{2,1,0:T(8,128)(2,1)S(1)}, bf16[2,256,512]{2,1,0:T(8,128)(2,1)S(1)}, f32[2,256,512]{2,1,0:T(8,128)S(1)}, f32[2,256,512]{2,1,0:T(8,128)...) custom-call(s32[5]{0:T(128)S(1)} %stack.23.refs_0_, bf16[256,512]{1,0:T(8,128)(2,1)S(1)} %get-tuple-element.58.refs_1_, ...), custom_call_target="tpu_custom_call" | custom-call | flops 2590000128 | bytes 8547000 | tf_op jit(solution)/shard_map/back/pallas_call | solution.py:88
  48.9 3.8 %collective-permute-start.9 = (bf16[128,512]{1,0:T(8,128)(2,1)S(1)}, bf16[128,512]{1,0:T(8,128)(2,1)S(1)}, u32[]{:S(2)}, u32[]{:S(2)}) collective-permute-start(bf16[128,512]{1,0:T(8,128)(2,1)S(1)} %get-tuple-element.69), channel_id=1, source_target_pairs={{0,8},{8,16},{16,24},{24,32},{32,40},{40,48},{48,56},{56,64},{64,7... | collective-permute-start | bytes 393224 | tf_op jit(solution)/shard_map/ppermute | solution.py:37
  52.7 1.5 %collective-permute-start.8 = (bf16[2,256,512]{2,1,0:T(8,128)(2,1)S(1)}, bf16[2,256,512]{2,1,0:T(8,128)(2,1)S(1)}, u32[]{:S(2)}, u32[]{:S(2)}) collective-permute-start(bf16[2,256,512]{2,1,0:T(8,128)(2,1)S(1)} %get-tuple-element.64), channel_id=1, source_target_pairs={{0,2},{2,0},{4,6},{6,4},{1,3},{3,1},{5,7},{7,5},{8,10},{10,8},{12,... | collective-permute-start | bytes 1572872 | tf_op jit(solution)/shard_map/ppermute | solution.py:32
  54.9 1.5 %collective-permute-start.12 = (bf16[512,512]{1,0:T(8,128)(2,1)S(1)}, bf16[512,512]{1,0:T(8,128)(2,1)S(1)}, u32[]{:S(2)}, u32[]{:S(2)}) collective-permute-start(bf16[512,512]{1,0:T(8,128)(2,1)S(1)} %get-tuple-element.76), channel_id=1, source_target_pairs={{0,64},{64,128},{128,192},{192,0},{1,65},{65,129},{129,193},{193,1... | collective-permute-start | bytes 1572872 | tf_op jit(solution)/shard_map/ppermute | solution.py:28
  56.4 2.5 %collective-permute-start.13 = (bf16[512,512]{1,0:T(8,128)(2,1)S(1)}, bf16[512,512]{1,0:T(8,128)(2,1)S(1)}, u32[]{:S(2)}, u32[]{:S(2)}) collective-permute-start(bf16[512,512]{1,0:T(8,128)(2,1)S(1)} %get-tuple-element.77), channel_id=1, source_target_pairs={{0,128},{64,192},{128,0},{192,64},{1,129},{65,193},{129,1},{193,65... | collective-permute-start | bytes 1572872 | tf_op jit(solution)/shard_map/ppermute | solution.py:28
  58.8 1.2 collective-permute-start.14
  60.0 6.2 %taps.1 = (f32[64,512]{1,0:T(8,128)S(1)}, f32[64,512]{1,0:T(8,128)S(1)}, f32[8,128]{1,0:T(8,128)S(1)}) custom-call(s32[5]{0:T(128)S(1)} %stack.23.refs_0_, bf16[256,512]{1,0:T(8,128)(2,1)S(1)} %get-tuple-element.68.refs_1_.refs_0_, bf16[128,512]{1,0:T(8,128)(2,1)S(1)} %collective-permute-done.9.refs_2_.refs_1_, bf16[256,512]{1,0:T(8,128)(2,1)S(1)} %copy-done.9, ...), custom_call_target="tpu_custom_call" | custom-call | flops 5600000000 | bytes 18480000 | tf_op jit(solution)/shard_map/taps/pallas_call | solution.py:88
  68.4 2.3 %collective-permute-start.15 = (bf16[256,512]{1,0:T(8,128)(2,1)S(1)}, bf16[256,512]{1,0:T(8,128)(2,1)S(1)}, u32[]{:S(2)}, u32[]{:S(2)}) collective-permute-start(bf16[256,512]{1,0:T(8,128)(2,1)S(1)} %get-tuple-element.80), channel_id=1, source_target_pairs={{0,6},{2,4},{4,2},{6,0},{1,7},{3,5},{5,3},{7,1},{8,14},{10,12},{12... | collective-permute-start | bytes 786440 | tf_op jit(solution)/shard_map/ppermute | solution.py:32
  71.4 5.8 %collective-permute-done.15.refs_1_ = bf16[256,512]{1,0:T(8,128)(2,1)S(1)} collective-permute-done((bf16[256,512]{1,0:T(8,128)(2,1)S(1)}, bf16[256,512]{1,0:T(8,128)(2,1)S(1)}, u32[]{:S(2)}, u32[]{:S(2)}) %collective-permute-start.15) | collective-permute-done | bytes 262176 | tf_op jit(solution)/shard_map/ppermute | solution.py:32
  77.3 3.3 %collective-permute-done.22.refs_1_ = bf16[64,512]{1,0:T(8,128)(2,1)S(1)} collective-permute-done((bf16[64,512]{1,0:T(8,128)(2,1)S(1)}, bf16[64,512]{1,0:T(8,128)(2,1)S(1)}, u32[]{:S(2)}, u32[]{:S(2)}) %collective-permute-start.22) | collective-permute-done | bytes 65568 | tf_op jit(solution)/shard_map/ppermute | solution.py:32
  80.6 2.3 %collective-permute-start.17 = (bf16[256,512]{1,0:T(8,128)(2,1)S(1)}, bf16[256,512]{1,0:T(8,128)(2,1)S(1)}, u32[]{:S(2)}, u32[]{:S(2)}) collective-permute-start(bf16[256,512]{1,0:T(8,128)(2,1)S(1)} %get-tuple-element.85), channel_id=1, source_target_pairs={{0,1},{1,0},{2,3},{3,2},{4,5},{5,4},{6,7},{7,6},{8,9},{9,8},{10,11... | collective-permute-start | bytes 786440 | tf_op jit(solution)/shard_map/ppermute | solution.py:32
  83.6 1.5 %collective-permute-start.23 = (bf16[64,512]{1,0:T(8,128)(2,1)S(1)}, bf16[64,512]{1,0:T(8,128)(2,1)S(1)}, u32[]{:S(2)}, u32[]{:S(2)}) collective-permute-start(bf16[64,512]{1,0:T(8,128)(2,1)S(1)} %get-tuple-element.96), channel_id=1, source_target_pairs={{0,32},{16,48},{32,0},{48,16},{1,33},{17,49},{33,1},{49,17},{2,34}... | collective-permute-start | bytes 196616 | tf_op jit(solution)/shard_map/ppermute | solution.py:32
  85.1 1.2 gather.1
  86.3 14.1 %collective-permute-done.23.refs_1_ = bf16[64,512]{1,0:T(8,128)(2,1)S(1)} collective-permute-done((bf16[64,512]{1,0:T(8,128)(2,1)S(1)}, bf16[64,512]{1,0:T(8,128)(2,1)S(1)}, u32[]{:S(2)}, u32[]{:S(2)}) %collective-permute-start.23) | collective-permute-done | bytes 65568 | tf_op jit(solution)/shard_map/ppermute | solution.py:32
  101.1 1.8 %collective-permute-start.24 = (bf16[64,512]{1,0:T(8,128)(2,1)S(1)}, bf16[64,512]{1,0:T(8,128)(2,1)S(1)}, u32[]{:S(2)}, u32[]{:S(2)}) collective-permute-start(bf16[64,512]{1,0:T(8,128)(2,1)S(1)} %get-tuple-element.98), channel_id=1, source_target_pairs={{0,64},{64,0},{128,192},{192,128},{1,65},{65,1},{129,193},{193,129... | collective-permute-start | bytes 196616 | tf_op jit(solution)/shard_map/ppermute | solution.py:32
  103.7 2.8 %collective-permute-start.20 = (bf16[512,128]{1,0:T(8,128)(2,1)S(1)}, bf16[512,128]{1,0:T(8,128)(2,1)S(1)}, u32[]{:S(2)}, u32[]{:S(2)}) collective-permute-start(bf16[512,128]{1,0:T(8,128)(2,1)S(1)} %get-tuple-element.89), channel_id=1, source_target_pairs={{0,48},{16,32},{32,16},{48,0},{1,49},{17,33},{33,17},{49,1},{2,50}... | collective-permute-start | bytes 393224 | tf_op jit(solution)/shard_map/ppermute | solution.py:32
  108.2 1.3 %collective-permute-start.25 = (bf16[64,512]{1,0:T(8,128)(2,1)S(1)}, bf16[64,512]{1,0:T(8,128)(2,1)S(1)}, u32[]{:S(2)}, u32[]{:S(2)}) collective-permute-start(bf16[64,512]{1,0:T(8,128)(2,1)S(1)} %get-tuple-element.100), channel_id=1, source_target_pairs={{0,192},{64,128},{128,64},{192,0},{1,193},{65,129},{129,65},{193,1... | collective-permute-start | bytes 196616 | tf_op jit(solution)/shard_map/ppermute | solution.py:32
  109.5 6.5 %conv.1 = (f32[256,512]{1,0:T(8,128)}, f32[8,128]{1,0:T(8,128)S(1)}) custom-call(bf16[256,512]{1,0:T(8,128)(2,1)S(1)} %get-tuple-element.68.refs_1_.refs_0_, bf16[128,512]{1,0:T(8,128)(2,1)S(1)} %collective-permute-done.9.refs_2_.refs_1_, bf16[256,512]{1,0:T(8,128)(2,1)S(1)} %copy-done.1, f32[4,128,128]{2,1,0:T(8,128)S(1)} %copy-done.7, ...), custom_call_target="tpu_custom_call" | custom-call | flops 5880000000 | bytes 19404000 | tf_op jit(solution)/shard_map/conv/pallas_call | solution.py:88
  116.1 2.1 %collective-permute-start.26 = (f32[64,512]{1,0:T(8,128)S(1)}, f32[64,512]{1,0:T(8,128)S(1)}, u32[]{:S(2)}, u32[]{:S(2)}) collective-permute-start(f32[64,512]{1,0:T(8,128)S(1)} %last.1.refs_1_), channel_id=1, source_target_pairs={{0,8},{8,0},{1,9},{9,1},{2,10},{10,2},{3,11},{11,3},{4,12},{12,4},... | collective-permute-start | bytes 393224 | tf_op jit(solution)/shard_map/ppermute | solution.py:32
  118.2 1.4 %finish.1 = f32[128,512]{1,0:T(8,128)} custom-call(f32[512,128]{1,0:T(8,128)S(1)} %get-tuple-element.86.refs_0_, bf16[512,128]{1,0:T(8,128)(2,1)S(1)} %collective-permute-done.18.refs_1_.refs_2_, bf16[512,128]{1,0:T(8,128)(2,1)S(1)} %collective-permute-done.19.refs_2_.refs_3_, bf16[512,128]{1,0:T(8,128)(2,1)S(1)} %collective-permute-done.20.refs_3_.refs_4_, ...), custom_call_target="tpu_custom_call" | custom-call | flops 910000000 | bytes 3003000 | tf_op jit(solution)/shard_map/finish/pallas_call | solution.py:88
  119.5 1.6 %ends.1 = f32[512,128]{1,0:T(8,128)} custom-call(s32[5]{0:T(128)S(1)} %stack.23.refs_0_, f32[64,512]{1,0:T(8,128)S(1)} %last.1.refs_1_, f32[64,512]{1,0:T(8,128)S(1)} %collective-permute-done.26.refs_2_), custom_call_target="tpu_custom_call" | custom-call | flops 910000000 | bytes 3003000 | tf_op jit(solution)/shard_map/ends/pallas_call | solution.py:88
  (64 shorter events, 14.0 us)
Async XLA Ops:
  0.6 23.2 %collective-permute-start.1 = (bf16[256,512]{1,0:T(8,128)(2,1)}, bf16[256,512]{1,0:T(8,128)(2,1)S(1)}, u32[]{:S(2)}, u32[]{:S(2)}) collective-permute-start(bf16[256,512]{1,0:T(8,128)(2,1)} %refs_1_.3), channel_id=1, source_target_pairs={{0,1},{1,0},{2,3},{3,2},{4,5},{5,4},{6,7},{7,6},{8,9},{9,8},{10,11... | collective-permute-start | bytes 786440 | tf_op jit(solution)/shard_map/ppermute | solution.py:32
  8.5 18.8 %collective-permute-start.2 = (bf16[256,512]{1,0:T(8,128)(2,1)}, bf16[256,512]{1,0:T(8,128)(2,1)S(1)}, u32[]{:S(2)}, u32[]{:S(2)}) collective-permute-start(bf16[256,512]{1,0:T(8,128)(2,1)} %refs_1_.3), channel_id=1, source_target_pairs={{0,2},{2,4},{4,6},{6,0},{1,3},{3,5},{5,7},{7,1},{8,10},{10,12},{12... | collective-permute-start | bytes 786440 | tf_op jit(solution)/shard_map/ppermute | solution.py:28
  9.8 18.5 %collective-permute-start.3 = (bf16[256,512]{1,0:T(8,128)(2,1)}, bf16[256,512]{1,0:T(8,128)(2,1)S(1)}, u32[]{:S(2)}, u32[]{:S(2)}) collective-permute-start(bf16[256,512]{1,0:T(8,128)(2,1)} %refs_1_.3), channel_id=1, source_target_pairs={{0,4},{2,6},{4,0},{6,2},{1,5},{3,7},{5,1},{7,3},{8,12},{10,14},{12... | collective-permute-start | bytes 786440 | tf_op jit(solution)/shard_map/ppermute | solution.py:28
  12.4 15.9 %collective-permute-start.4 = (bf16[256,512]{1,0:T(8,128)(2,1)}, bf16[256,512]{1,0:T(8,128)(2,1)S(1)}, u32[]{:S(2)}, u32[]{:S(2)}) collective-permute-start(bf16[256,512]{1,0:T(8,128)(2,1)} %refs_1_.3), channel_id=1, source_target_pairs={{0,6},{2,0},{4,2},{6,4},{1,7},{3,1},{5,3},{7,5},{8,14},{10,8},{12,... | collective-permute-start | bytes 786440 | tf_op jit(solution)/shard_map/ppermute | solution.py:28
  16.4 7.5 %collective-permute-start = (bf16[128,512]{1,0:T(8,128)(2,1)}, bf16[128,512]{1,0:T(8,128)(2,1)S(1)}, u32[]{:S(2)}, u32[]{:S(2)}) collective-permute-start(bf16[128,512]{1,0:T(8,128)(2,1)} %get-tuple-element.55), channel_id=1, source_target_pairs={{8,0},{16,8},{24,16},{32,24},{40,32},{48,40},{56,48},{64,56},{72,6... | collective-permute-start | bytes 393224 | tf_op jit(solution)/shard_map/ppermute | solution.py:37
  23.9 14.6 %collective-permute-start.5 = (bf16[256,512]{1,0:T(8,128)(2,1)S(1)}, bf16[256,512]{1,0:T(8,128)(2,1)S(1)}, u32[]{:S(2)}, u32[]{:S(2)}) collective-permute-start(bf16[256,512]{1,0:T(8,128)(2,1)S(1)} %after.1.refs_4_.refs_5_), channel_id=1, source_target_pairs={{0,2},{2,4},{4,6},{6,0},{1,3},{3,5},{5,7},{7,1},{8,10},{10,12},{12... | collective-permute-start | bytes 786440 | tf_op jit(solution)/shard_map/ppermute | solution.py:28
  24.6 13.9 %collective-permute-start.6 = (bf16[256,512]{1,0:T(8,128)(2,1)S(1)}, bf16[256,512]{1,0:T(8,128)(2,1)S(1)}, u32[]{:S(2)}, u32[]{:S(2)}) collective-permute-start(bf16[256,512]{1,0:T(8,128)(2,1)S(1)} %after.1.refs_4_.refs_5_), channel_id=1, source_target_pairs={{0,4},{2,6},{4,0},{6,2},{1,5},{3,7},{5,1},{7,3},{8,12},{10,14},{12... | collective-permute-start | bytes 786440 | tf_op jit(solution)/shard_map/ppermute | solution.py:28
  27.2 11.2 %collective-permute-start.7 = (bf16[256,512]{1,0:T(8,128)(2,1)S(1)}, bf16[256,512]{1,0:T(8,128)(2,1)S(1)}, u32[]{:S(2)}, u32[]{:S(2)}) collective-permute-start(bf16[256,512]{1,0:T(8,128)(2,1)S(1)} %after.1.refs_4_.refs_5_), channel_id=1, source_target_pairs={{0,6},{2,0},{4,2},{6,4},{1,7},{3,1},{5,3},{7,5},{8,14},{10,8},{12,... | collective-permute-start | bytes 786440 | tf_op jit(solution)/shard_map/ppermute | solution.py:28
  30.9 7.6 %copy-start = (bf16[256,512]{1,0:T(8,128)(2,1)S(1)}, bf16[256,512]{1,0:T(8,128)(2,1)}, u32[]{:S(2)}) copy-start(bf16[256,512]{1,0:T(8,128)(2,1)} %refs_1_.3) | copy-start | bytes 786436
  42.8 11.4 %collective-permute-start.10 = (bf16[4,512,512]{2,1,0:T(8,128)(2,1)S(1)}, bf16[4,512,512]{2,1,0:T(8,128)(2,1)S(1)}, u32[]{:S(2)}, u32[]{:S(2)}) collective-permute-start(bf16[4,512,512]{2,1,0:T(8,128)(2,1)S(1)} %get-tuple-element.71), channel_id=1, source_target_pairs={{0,8},{8,0},{1,9},{9,1},{2,10},{10,2},{3,11},{11,3},{4,12},{12,4},... | collective-permute-start | bytes 6291464 | tf_op jit(solution)/shard_map/ppermute | solution.py:32
  42.9 5.1 %copy-start.4 = (f32[256,512]{1,0:T(8,128)S(1)}, f32[256,512]{1,0:T(8,128)}, u32[]{:S(2)}) copy-start(f32[256,512]{1,0:T(8,128)} %get-tuple-element.57.refs_3_.refs_2_) | copy-start | bytes 1572868
  42.9 5.1 %copy-start.5 = (f32[256,512]{1,0:T(8,128)S(1)}, f32[256,512]{1,0:T(8,128)}, u32[]{:S(2)}) copy-start(f32[256,512]{1,0:T(8,128)} %get-tuple-element.67.refs_1_) | copy-start | bytes 1572868
  48.9 11.1 %collective-permute-start.9 = (bf16[128,512]{1,0:T(8,128)(2,1)S(1)}, bf16[128,512]{1,0:T(8,128)(2,1)S(1)}, u32[]{:S(2)}, u32[]{:S(2)}) collective-permute-start(bf16[128,512]{1,0:T(8,128)(2,1)S(1)} %get-tuple-element.69), channel_id=1, source_target_pairs={{0,8},{8,16},{16,24},{24,32},{32,40},{40,48},{48,56},{56,64},{64,7... | collective-permute-start | bytes 393224 | tf_op jit(solution)/shard_map/ppermute | solution.py:37
  52.7 14.2 %collective-permute-start.8 = (bf16[2,256,512]{2,1,0:T(8,128)(2,1)S(1)}, bf16[2,256,512]{2,1,0:T(8,128)(2,1)S(1)}, u32[]{:S(2)}, u32[]{:S(2)}) collective-permute-start(bf16[2,256,512]{2,1,0:T(8,128)(2,1)S(1)} %get-tuple-element.64), channel_id=1, source_target_pairs={{0,2},{2,0},{4,6},{6,4},{1,3},{3,1},{5,7},{7,5},{8,10},{10,8},{12,... | collective-permute-start | bytes 1572872 | tf_op jit(solution)/shard_map/ppermute | solution.py:32
  54.2 5.8 %copy-start.9 = (bf16[256,512]{1,0:T(8,128)(2,1)S(1)}, bf16[256,512]{1,0:T(8,128)(2,1)}, u32[]{:S(2)}) copy-start(bf16[256,512]{1,0:T(8,128)(2,1)} %get-tuple-element.54.refs_0_.refs_3_) | copy-start | bytes 786436
  54.9 28.7 %collective-permute-start.12 = (bf16[512,512]{1,0:T(8,128)(2,1)S(1)}, bf16[512,512]{1,0:T(8,128)(2,1)S(1)}, u32[]{:S(2)}, u32[]{:S(2)}) collective-permute-start(bf16[512,512]{1,0:T(8,128)(2,1)S(1)} %get-tuple-element.76), channel_id=1, source_target_pairs={{0,64},{64,128},{128,192},{192,0},{1,65},{65,129},{129,193},{193,1... | collective-permute-start | bytes 1572872 | tf_op jit(solution)/shard_map/ppermute | solution.py:28
  56.4 28.7 %collective-permute-start.13 = (bf16[512,512]{1,0:T(8,128)(2,1)S(1)}, bf16[512,512]{1,0:T(8,128)(2,1)S(1)}, u32[]{:S(2)}, u32[]{:S(2)}) collective-permute-start(bf16[512,512]{1,0:T(8,128)(2,1)S(1)} %get-tuple-element.77), channel_id=1, source_target_pairs={{0,128},{64,192},{128,0},{192,64},{1,129},{65,193},{129,1},{193,65... | collective-permute-start | bytes 1572872 | tf_op jit(solution)/shard_map/ppermute | solution.py:28
  58.8 26.3 %collective-permute-start.14 = (bf16[512,512]{1,0:T(8,128)(2,1)S(1)}, bf16[512,512]{1,0:T(8,128)(2,1)S(1)}, u32[]{:S(2)}, u32[]{:S(2)}) collective-permute-start(bf16[512,512]{1,0:T(8,128)(2,1)S(1)} %get-tuple-element.78), channel_id=1, source_target_pairs={{0,192},{64,0},{128,64},{192,128},{1,193},{65,1},{129,65},{193,129... | collective-permute-start | bytes 1572872 | tf_op jit(solution)/shard_map/ppermute | solution.py:28
  66.2 2.2 %collective-permute-start.21 = (f32[64,512]{1,0:T(8,128)S(1)}, f32[64,512]{1,0:T(8,128)S(1)}, u32[]{:S(2)}, u32[]{:S(2)}) collective-permute-start(f32[64,512]{1,0:T(8,128)S(1)} %get-tuple-element.92), channel_id=1, source_target_pairs={{0,8},{8,0},{1,9},{9,1},{2,10},{10,2},{3,11},{11,3},{4,12},{12,4},... | collective-permute-start | bytes 393224 | tf_op jit(solution)/shard_map/ppermute | solution.py:32
  67.6 36.1 %collective-permute-start.11 = (bf16[2,256,512]{2,1,0:T(8,128)(2,1)S(1)}, bf16[2,256,512]{2,1,0:T(8,128)(2,1)S(1)}, u32[]{:S(2)}, u32[]{:S(2)}) collective-permute-start(bf16[2,256,512]{2,1,0:T(8,128)(2,1)S(1)} %get-tuple-element.74), channel_id=1, source_target_pairs={{0,2},{2,0},{4,6},{6,4},{1,3},{3,1},{5,7},{7,5},{8,10},{10,8},{12,... | collective-permute-start | bytes 1572872 | tf_op jit(solution)/shard_map/ppermute | solution.py:32
  68.4 8.8 %collective-permute-start.15 = (bf16[256,512]{1,0:T(8,128)(2,1)S(1)}, bf16[256,512]{1,0:T(8,128)(2,1)S(1)}, u32[]{:S(2)}, u32[]{:S(2)}) collective-permute-start(bf16[256,512]{1,0:T(8,128)(2,1)S(1)} %get-tuple-element.80), channel_id=1, source_target_pairs={{0,6},{2,4},{4,2},{6,0},{1,7},{3,5},{5,3},{7,1},{8,14},{10,12},{12... | collective-permute-start | bytes 786440 | tf_op jit(solution)/shard_map/ppermute | solution.py:32
  77.2 3.4 %collective-permute-start.22 = (bf16[64,512]{1,0:T(8,128)(2,1)S(1)}, bf16[64,512]{1,0:T(8,128)(2,1)S(1)}, u32[]{:S(2)}, u32[]{:S(2)}) collective-permute-start(bf16[64,512]{1,0:T(8,128)(2,1)S(1)} %get-tuple-element.94), channel_id=1, source_target_pairs={{0,16},{16,0},{32,48},{48,32},{1,17},{17,1},{33,49},{49,33},{2,18}... | collective-permute-start | bytes 196616 | tf_op jit(solution)/shard_map/ppermute | solution.py:32
  80.6 26.5 %collective-permute-start.17 = (bf16[256,512]{1,0:T(8,128)(2,1)S(1)}, bf16[256,512]{1,0:T(8,128)(2,1)S(1)}, u32[]{:S(2)}, u32[]{:S(2)}) collective-permute-start(bf16[256,512]{1,0:T(8,128)(2,1)S(1)} %get-tuple-element.85), channel_id=1, source_target_pairs={{0,1},{1,0},{2,3},{3,2},{4,5},{5,4},{6,7},{7,6},{8,9},{9,8},{10,11... | collective-permute-start | bytes 786440 | tf_op jit(solution)/shard_map/ppermute | solution.py:32
  83.6 16.8 %collective-permute-start.23 = (bf16[64,512]{1,0:T(8,128)(2,1)S(1)}, bf16[64,512]{1,0:T(8,128)(2,1)S(1)}, u32[]{:S(2)}, u32[]{:S(2)}) collective-permute-start(bf16[64,512]{1,0:T(8,128)(2,1)S(1)} %get-tuple-element.96), channel_id=1, source_target_pairs={{0,32},{16,48},{32,0},{48,16},{1,33},{17,49},{33,1},{49,17},{2,34}... | collective-permute-start | bytes 196616 | tf_op jit(solution)/shard_map/ppermute | solution.py:32
  101.1 6.4 %collective-permute-start.24 = (bf16[64,512]{1,0:T(8,128)(2,1)S(1)}, bf16[64,512]{1,0:T(8,128)(2,1)S(1)}, u32[]{:S(2)}, u32[]{:S(2)}) collective-permute-start(bf16[64,512]{1,0:T(8,128)(2,1)S(1)} %get-tuple-element.98), channel_id=1, source_target_pairs={{0,64},{64,0},{128,192},{192,128},{1,65},{65,1},{129,193},{193,129... | collective-permute-start | bytes 196616 | tf_op jit(solution)/shard_map/ppermute | solution.py:32
  102.9 13.1 %collective-permute-start.18 = (bf16[512,128]{1,0:T(8,128)(2,1)S(1)}, bf16[512,128]{1,0:T(8,128)(2,1)S(1)}, u32[]{:S(2)}, u32[]{:S(2)}) collective-permute-start(bf16[512,128]{1,0:T(8,128)(2,1)S(1)} %get-tuple-element.87), channel_id=1, source_target_pairs={{0,16},{16,0},{32,48},{48,32},{1,17},{17,1},{33,49},{49,33},{2,18}... | collective-permute-start | bytes 393224 | tf_op jit(solution)/shard_map/ppermute | solution.py:32
  102.9 13.1 %collective-permute-start.19 = (bf16[512,128]{1,0:T(8,128)(2,1)S(1)}, bf16[512,128]{1,0:T(8,128)(2,1)S(1)}, u32[]{:S(2)}, u32[]{:S(2)}) collective-permute-start(bf16[512,128]{1,0:T(8,128)(2,1)S(1)} %get-tuple-element.88), channel_id=1, source_target_pairs={{0,32},{16,48},{32,0},{48,16},{1,33},{17,49},{33,1},{49,17},{2,34}... | collective-permute-start | bytes 393224 | tf_op jit(solution)/shard_map/ppermute | solution.py:32
  103.7 12.3 %collective-permute-start.20 = (bf16[512,128]{1,0:T(8,128)(2,1)S(1)}, bf16[512,128]{1,0:T(8,128)(2,1)S(1)}, u32[]{:S(2)}, u32[]{:S(2)}) collective-permute-start(bf16[512,128]{1,0:T(8,128)(2,1)S(1)} %get-tuple-element.89), channel_id=1, source_target_pairs={{0,48},{16,32},{32,16},{48,0},{1,49},{17,33},{33,17},{49,1},{2,50}... | collective-permute-start | bytes 393224 | tf_op jit(solution)/shard_map/ppermute | solution.py:32
  106.4 3.1 %copy-start.7 = (f32[4,128,128]{2,1,0:T(8,128)S(1)}, f32[4,128,128]{2,1,0:T(8,128)}, u32[]{:S(2)}) copy-start(f32[4,128,128]{2,1,0:T(8,128)} %get-tuple-element.56.refs_2_.refs_3_) | copy-start | bytes 786436
  107.1 14.1 %collective-permute-start.16 = (bf16[256,512]{1,0:T(8,128)(2,1)S(1)}, bf16[256,512]{1,0:T(8,128)(2,1)S(1)}, u32[]{:S(2)}, u32[]{:S(2)}) collective-permute-start(bf16[256,512]{1,0:T(8,128)(2,1)S(1)} %get-tuple-element.84), channel_id=1, source_target_pairs={{0,6},{2,4},{4,2},{6,0},{1,7},{3,5},{5,3},{7,1},{8,14},{10,12},{12... | collective-permute-start | bytes 786440 | tf_op jit(solution)/shard_map/ppermute | solution.py:32
  108.2 7.8 %collective-permute-start.25 = (bf16[64,512]{1,0:T(8,128)(2,1)S(1)}, bf16[64,512]{1,0:T(8,128)(2,1)S(1)}, u32[]{:S(2)}, u32[]{:S(2)}) collective-permute-start(bf16[64,512]{1,0:T(8,128)(2,1)S(1)} %get-tuple-element.100), channel_id=1, source_target_pairs={{0,192},{64,128},{128,64},{192,0},{1,193},{65,129},{129,65},{193,1... | collective-permute-start | bytes 196616 | tf_op jit(solution)/shard_map/ppermute | solution.py:32
  116.1 3.4 %collective-permute-start.26 = (f32[64,512]{1,0:T(8,128)S(1)}, f32[64,512]{1,0:T(8,128)S(1)}, u32[]{:S(2)}, u32[]{:S(2)}) collective-permute-start(f32[64,512]{1,0:T(8,128)S(1)} %last.1.refs_1_), channel_id=1, source_target_pairs={{0,8},{8,0},{1,9},{9,1},{2,10},{10,2},{3,11},{11,3},{4,12},{12,4},... | collective-permute-start | bytes 393224 | tf_op jit(solution)/shard_map/ppermute | solution.py:32
  (5 other events, 6.6 us)

commit v5 on v4

--- a/solution.py
+++ b/solution.py
@@ -532,7 +532,7 @@
         middle_kernel,
         (half_taps, struct((tap_count // 2, channels), BF16), mark),
         [("vmem", filter_sum), ("in", crossed(filter_sent, "zl", 2))]
-        + [("mark", gather_mark)],
+        + [("mark", conv_mark)] + [("tie", v) for v in arrived[:1]],
     )
     filter_sum, filter_sent, middle4_mark = call(
         "middle4",

time: 123 us -> 117 us (0.951)
  waiting for transfers between devices: 26.9 us -> 13.5 us
  starting transfers between devices: 48.1 us -> 55.7 us
    ppermute x16, waiting for transfers between devices: 23.2 us -> 7.36 us  [crossed(): lax.ppermute(block, axis, [(i, i ^ d) for i in range(lax.axis_size(axis))])]
    ppermute x16, starting transfers between devices: 26.2 us -> 33.8 us  [crossed(): lax.ppermute(block, axis, [(i, i ^ d) for i in range(lax.axis_size(axis))])]
    ppermute x9, waiting for transfers between devices: 0.02 us -> 2.5 us  [shifted(): return lax.ppermute(block, axis, [(i, (i + k) % n) for i in range(n)])]
  transfers between devices with their start and end apart: 27 -> 27, of which waited for: 4 -> 6; matrix products, arithmetic and copies ran while one was open for 0% -> 0% of each run, Pallas kernels for 31% -> 32%
where the time goes in v5:
time: 117 us; the launch traced here: 116 us
  starting transfers between devices  55.7 us (48%)
  Pallas kernels  42.4 us (36%)
  waiting for transfers between devices  13.5 us (12%)
  local copies, waits for them, and re-layouts  3.66 us (3%)
    pallas_call x20, Pallas kernels, call(): pl.pallas_call(kernel, out_shape=out, in_specs=[SPECS[kind] for kind in k...  42.4 us
    ppermute x16, starting transfers between devices, crossed(): lax.ppermute(block, axis, [(i, i ^ d) for i in range(lax.axis_size(axis))])  33.8 us
    ppermute x9, starting transfers between devices, shifted(): return lax.ppermute(block, axis, [(i, (i + k) % n) for i in range(n)])  14.5 us
    ppermute x2, starting transfers between devices, along_tokens(): lax.ppermute(block, SEQ, [(i, i + step) for i in range(n) if 0 <= i + ste...  7.46 us
    ppermute x16, waiting for transfers between devices, crossed(): lax.ppermute(block, axis, [(i, i ^ d) for i in range(lax.axis_size(axis))])  7.36 us
    ppermute x2, waiting for transfers between devices, along_tokens(): lax.ppermute(block, SEQ, [(i, i + step) for i in range(n) if 0 <= i + ste...  3.67 us
    unnamed x20, local copies, waits for them, and re-layouts  3.58 us
    ppermute x9, waiting for transfers between devices, shifted(): return lax.ppermute(block, axis, [(i, (i + k) % n) for i in range(n)])  2.5 us
  transfers between devices with their start and end apart: 27, of which 6 were waited for; matrix products, arithmetic and copies ran while one was open for 0% of the time, Pallas kernels for 32%

profile of v5, /device:TPU:1, one launch (start us, length us, event | category | flops | bytes accessed | tf_op | source)
XLA Modules:
  0.0 116.5 jit_solution(14493289739852622589)
XLA Ops:
  0.6 7.8 %collective-permute-start.1 = (bf16[256,512]{1,0:T(8,128)(2,1)}, bf16[256,512]{1,0:T(8,128)(2,1)S(1)}, u32[]{:S(2)}, u32[]{:S(2)}) collective-permute-start(bf16[256,512]{1,0:T(8,128)(2,1)} %refs_1_.3), channel_id=1, source_target_pairs={{0,1},{1,0},{2,3},{3,2},{4,5},{5,4},{6,7},{7,6},{8,9},{9,8},{10,11... | collective-permute-start | bytes 786440 | tf_op jit(solution)/shard_map/ppermute | solution.py:32
  8.5 1.3 %collective-permute-start.2 = (bf16[256,512]{1,0:T(8,128)(2,1)}, bf16[256,512]{1,0:T(8,128)(2,1)S(1)}, u32[]{:S(2)}, u32[]{:S(2)}) collective-permute-start(bf16[256,512]{1,0:T(8,128)(2,1)} %refs_1_.3), channel_id=1, source_target_pairs={{0,2},{2,4},{4,6},{6,0},{1,3},{3,5},{5,7},{7,1},{8,10},{10,12},{12... | collective-permute-start | bytes 786440 | tf_op jit(solution)/shard_map/ppermute | solution.py:28
  9.8 2.6 %collective-permute-start.3 = (bf16[256,512]{1,0:T(8,128)(2,1)}, bf16[256,512]{1,0:T(8,128)(2,1)S(1)}, u32[]{:S(2)}, u32[]{:S(2)}) collective-permute-start(bf16[256,512]{1,0:T(8,128)(2,1)} %refs_1_.3), channel_id=1, source_target_pairs={{0,4},{2,6},{4,0},{6,2},{1,5},{3,7},{5,1},{7,3},{8,12},{10,14},{12... | collective-permute-start | bytes 786440 | tf_op jit(solution)/shard_map/ppermute | solution.py:28
  13.4 2.9 %prepare.1 = (bf16[256,512]{1,0:T(8,128)(2,1)}, bf16[128,512]{1,0:T(8,128)(2,1)}, f32[256,512]{1,0:T(8,128)}, f32[4,128,128]{2,1,0:T(8,128)}) custom-call(bf16[256,512]{1,0:T(8,128)(2,1)} %refs_2_.1, s32[256,512]{1,0:T(8,128)} %refs_1_.2, f32[4,256]{1,0:T(4,128)} %bitcast.9, f32[4,256]{1,0:T(4,128)} %bitcast.10, s32[256,512]{1,0:T(8,128)} %refs_4_.1, ...), custom_call_target="tpu_custom_call" | custom-call | flops 1750000000 | bytes 5775000 | tf_op jit(solution)/shard_map/prepare/pallas_call | solution.py:88
  16.4 3.7 %collective-permute-start = (bf16[128,512]{1,0:T(8,128)(2,1)}, bf16[128,512]{1,0:T(8,128)(2,1)S(1)}, u32[]{:S(2)}, u32[]{:S(2)}) collective-permute-start(bf16[128,512]{1,0:T(8,128)(2,1)} %get-tuple-element.55), channel_id=1, source_target_pairs={{8,0},{16,8},{24,16},{32,24},{40,32},{48,40},{56,48},{64,56},{72,6... | collective-permute-start | bytes 393224 | tf_op jit(solution)/shard_map/ppermute | solution.py:37
  20.2 3.7 %collective-permute-done.refs_1_ = bf16[128,512]{1,0:T(8,128)(2,1)S(1)} collective-permute-done((bf16[128,512]{1,0:T(8,128)(2,1)}, bf16[128,512]{1,0:T(8,128)(2,1)S(1)}, u32[]{:S(2)}, u32[]{:S(2)}) %collective-permute-start) | collective-permute-done | bytes 131104 | tf_op jit(solution)/shard_map/ppermute | solution.py:37
  24.6 2.6 %collective-permute-start.6 = (bf16[256,512]{1,0:T(8,128)(2,1)S(1)}, bf16[256,512]{1,0:T(8,128)(2,1)S(1)}, u32[]{:S(2)}, u32[]{:S(2)}) collective-permute-start(bf16[256,512]{1,0:T(8,128)(2,1)S(1)} %after.1.refs_4_.refs_5_), channel_id=1, source_target_pairs={{0,4},{2,6},{4,0},{6,2},{1,5},{3,7},{5,1},{7,3},{8,12},{10,14},{12... | collective-permute-start | bytes 786440 | tf_op jit(solution)/shard_map/ppermute | solution.py:28
  30.9 7.5 %mix.1 = (f32[256,512]{1,0:T(8,128)}, bf16[256,512]{1,0:T(8,128)(2,1)S(1)}, bf16[512,256]{1,0:T(8,128)(2,1)S(1)}) custom-call(bf16[256,512]{1,0:T(8,128)(2,1)S(1)} %copy-done.8, bf16[128,512]{1,0:T(8,128)(2,1)S(1)} %collective-permute-done.refs_1_, f32[4,128,128]{2,1,0:T(8,128)S(1)} %copy-done.6, f32[256,512]{1,0:T(8,128)} %get-tuple-element.57.refs_3_.refs_2_, ...), custom_call_target="tpu_custom_call" | custom-call | flops 5390000128 | bytes 17787000 | tf_op jit(solution)/shard_map/mix/pallas_call | solution.py:88
  39.4 3.3 %weight.1 = (f32[4,512,512]{2,1,0:T(8,128)S(1)}, bf16[4,512,512]{2,1,0:T(8,128)(2,1)S(1)}, bf16[8,256,512]{2,1,0:T(8,128)(2,1)S(1)}, f32[8,128]{1,0:T(8,128)S(1)}) custom-call(s32[5]{0:T(128)S(1)} %stack.23.refs_0_, bf16[256,512]{1,0:T(8,128)(2,1)S(1)} %copy-done, bf16[256,512]{1,0:T(8,128)(2,1)S(1)} %collective-permute-done.2.refs_5_.refs_2_, ...), custom_call_target="tpu_custom_call" | custom-call | flops 2800000000 | bytes 9240000 | tf_op jit(solution)/shard_map/weight/pallas_call | solution.py:88
  42.9 5.1 %back.1 = (bf16[2,256,512]{2,1,0:T(8,128)(2,1)S(1)}, bf16[2,256,512]{2,1,0:T(8,128)(2,1)S(1)}, f32[2,256,512]{2,1,0:T(8,128)S(1)}, f32[2,256,512]{2,1,0:T(8,128)...) custom-call(s32[5]{0:T(128)S(1)} %stack.23.refs_0_, bf16[256,512]{1,0:T(8,128)(2,1)S(1)} %get-tuple-element.58.refs_1_, ...), custom_call_target="tpu_custom_call" | custom-call | flops 2590000128 | bytes 8547000 | tf_op jit(solution)/shard_map/back/pallas_call | solution.py:88
  48.9 3.8 %collective-permute-start.9 = (bf16[128,512]{1,0:T(8,128)(2,1)S(1)}, bf16[128,512]{1,0:T(8,128)(2,1)S(1)}, u32[]{:S(2)}, u32[]{:S(2)}) collective-permute-start(bf16[128,512]{1,0:T(8,128)(2,1)S(1)} %get-tuple-element.69), channel_id=1, source_target_pairs={{0,8},{8,16},{16,24},{24,32},{32,40},{40,48},{48,56},{56,64},{64,7... | collective-permute-start | bytes 393224 | tf_op jit(solution)/shard_map/ppermute | solution.py:37
  52.7 1.5 %collective-permute-start.8 = (bf16[2,256,512]{2,1,0:T(8,128)(2,1)S(1)}, bf16[2,256,512]{2,1,0:T(8,128)(2,1)S(1)}, u32[]{:S(2)}, u32[]{:S(2)}) collective-permute-start(bf16[2,256,512]{2,1,0:T(8,128)(2,1)S(1)} %get-tuple-element.64), channel_id=1, source_target_pairs={{0,2},{2,0},{4,6},{6,4},{1,3},{3,1},{5,7},{7,5},{8,10},{10,8},{12,... | collective-permute-start | bytes 1572872 | tf_op jit(solution)/shard_map/ppermute | solution.py:32
  54.9 1.5 %collective-permute-start.12 = (bf16[512,512]{1,0:T(8,128)(2,1)S(1)}, bf16[512,512]{1,0:T(8,128)(2,1)S(1)}, u32[]{:S(2)}, u32[]{:S(2)}) collective-permute-start(bf16[512,512]{1,0:T(8,128)(2,1)S(1)} %get-tuple-element.76), channel_id=1, source_target_pairs={{0,64},{64,128},{128,192},{192,0},{1,65},{65,129},{129,193},{193,1... | collective-permute-start | bytes 1572872 | tf_op jit(solution)/shard_map/ppermute | solution.py:28
  56.4 2.5 %collective-permute-start.13 = (bf16[512,512]{1,0:T(8,128)(2,1)S(1)}, bf16[512,512]{1,0:T(8,128)(2,1)S(1)}, u32[]{:S(2)}, u32[]{:S(2)}) collective-permute-start(bf16[512,512]{1,0:T(8,128)(2,1)S(1)} %get-tuple-element.77), channel_id=1, source_target_pairs={{0,128},{64,192},{128,0},{192,64},{1,129},{65,193},{129,1},{193,65... | collective-permute-start | bytes 1572872 | tf_op jit(solution)/shard_map/ppermute | solution.py:28
  58.8 1.2 collective-permute-start.14
  60.0 6.2 %taps.1 = (f32[64,512]{1,0:T(8,128)S(1)}, f32[64,512]{1,0:T(8,128)S(1)}, f32[8,128]{1,0:T(8,128)S(1)}) custom-call(s32[5]{0:T(128)S(1)} %stack.23.refs_0_, bf16[256,512]{1,0:T(8,128)(2,1)S(1)} %get-tuple-element.68.refs_1_.refs_0_, bf16[128,512]{1,0:T(8,128)(2,1)S(1)} %collective-permute-done.9.refs_2_.refs_1_, bf16[256,512]{1,0:T(8,128)(2,1)S(1)} %copy-done.9, ...), custom_call_target="tpu_custom_call" | custom-call | flops 5600000000 | bytes 18480000 | tf_op jit(solution)/shard_map/taps/pallas_call | solution.py:88
  67.6 1.4 %collective-permute-start.15 = (bf16[256,512]{1,0:T(8,128)(2,1)S(1)}, bf16[256,512]{1,0:T(8,128)(2,1)S(1)}, u32[]{:S(2)}, u32[]{:S(2)}) collective-permute-start(bf16[256,512]{1,0:T(8,128)(2,1)S(1)} %get-tuple-element.80), channel_id=1, source_target_pairs={{0,6},{2,4},{4,2},{6,0},{1,7},{3,5},{5,3},{7,1},{8,14},{10,12},{12... | collective-permute-start | bytes 786440 | tf_op jit(solution)/shard_map/ppermute | solution.py:32
  69.7 1.5 %collective-permute-start.22 = (bf16[64,512]{1,0:T(8,128)(2,1)S(1)}, bf16[64,512]{1,0:T(8,128)(2,1)S(1)}, u32[]{:S(2)}, u32[]{:S(2)}) collective-permute-start(bf16[64,512]{1,0:T(8,128)(2,1)S(1)} %get-tuple-element.94), channel_id=1, source_target_pairs={{0,16},{16,0},{32,48},{48,32},{1,17},{17,1},{33,49},{49,33},{2,18}... | collective-permute-start | bytes 196616 | tf_op jit(solution)/shard_map/ppermute | solution.py:32
  71.2 2.0 %collective-permute-done.22.refs_1_ = bf16[64,512]{1,0:T(8,128)(2,1)S(1)} collective-permute-done((bf16[64,512]{1,0:T(8,128)(2,1)S(1)}, bf16[64,512]{1,0:T(8,128)(2,1)S(1)}, u32[]{:S(2)}, u32[]{:S(2)}) %collective-permute-start.22) | collective-permute-done | bytes 65568 | tf_op jit(solution)/shard_map/ppermute | solution.py:32
  75.0 1.8 %collective-permute-done.15.refs_1_ = bf16[256,512]{1,0:T(8,128)(2,1)S(1)} collective-permute-done((bf16[256,512]{1,0:T(8,128)(2,1)S(1)}, bf16[256,512]{1,0:T(8,128)(2,1)S(1)}, u32[]{:S(2)}, u32[]{:S(2)}) %collective-permute-start.15) | collective-permute-done | bytes 262176 | tf_op jit(solution)/shard_map/ppermute | solution.py:32
  77.4 3.8 %collective-permute-start.17 = (bf16[256,512]{1,0:T(8,128)(2,1)S(1)}, bf16[256,512]{1,0:T(8,128)(2,1)S(1)}, u32[]{:S(2)}, u32[]{:S(2)}) collective-permute-start(bf16[256,512]{1,0:T(8,128)(2,1)S(1)} %get-tuple-element.85), channel_id=1, source_target_pairs={{0,1},{1,0},{2,3},{3,2},{4,5},{5,4},{6,7},{7,6},{8,9},{9,8},{10,11... | collective-permute-start | bytes 786440 | tf_op jit(solution)/shard_map/ppermute | solution.py:32
  81.2 2.5 %collective-permute-done.13.refs_3_ = bf16[512,512]{1,0:T(8,128)(2,1)S(1)} collective-permute-done((bf16[512,512]{1,0:T(8,128)(2,1)S(1)}, bf16[512,512]{1,0:T(8,128)(2,1)S(1)}, u32[]{:S(2)}, u32[]{:S(2)}) %collective-permute-start.13) | collective-permute-done | bytes 524320 | tf_op jit(solution)/shard_map/ppermute | solution.py:28
  83.7 1.2 %gather.1 = (f32[512,128]{1,0:T(8,128)S(1)}, bf16[512,128]{1,0:T(8,128)(2,1)S(1)}, bf16[512,128]{1,0:T(8,128)(2,1)S(1)}, bf16[512,128]{1,0:T(8,128)(2,1)S(1)}, f32[8,128]{1,0:T(8,128)S(1)}) custom-call(s32[5]{0:T(128)S(1)} %stack.23.refs_0_, f32[512,512]{1,0:T(8,128)S(1)} %get-tuple-element.75.refs_1_, bf16[512,512]{1,0:T(8,128)(2,1)S(1)} %collective-permute-done.12.refs_2_, ...), custom_call_target="tpu_custom_call" | custom-call | flops 1050000000 | bytes 3465000 | tf_op jit(solution)/shard_map/gather/pallas_call | solution.py:88
  85.0 2.3 %collective-permute-start.19 = (bf16[512,128]{1,0:T(8,128)(2,1)S(1)}, bf16[512,128]{1,0:T(8,128)(2,1)S(1)}, u32[]{:S(2)}, u32[]{:S(2)}) collective-permute-start(bf16[512,128]{1,0:T(8,128)(2,1)S(1)} %get-tuple-element.88), channel_id=1, source_target_pairs={{0,32},{16,48},{32,0},{48,16},{1,33},{17,49},{33,1},{49,17},{2,34}... | collective-permute-start | bytes 393224 | tf_op jit(solution)/shard_map/ppermute | solution.py:32
  87.4 6.5 %conv.1 = (f32[256,512]{1,0:T(8,128)}, f32[8,128]{1,0:T(8,128)S(1)}) custom-call(bf16[256,512]{1,0:T(8,128)(2,1)S(1)} %get-tuple-element.68.refs_1_.refs_0_, bf16[128,512]{1,0:T(8,128)(2,1)S(1)} %collective-permute-done.9.refs_2_.refs_1_, bf16[256,512]{1,0:T(8,128)(2,1)S(1)} %copy-done.1, f32[4,128,128]{2,1,0:T(8,128)S(1)} %copy-done.7, ...), custom_call_target="tpu_custom_call" | custom-call | flops 5880000000 | bytes 19404000 | tf_op jit(solution)/shard_map/conv/pallas_call | solution.py:88
  93.9 1.3 %collective-permute-start.20 = (bf16[512,128]{1,0:T(8,128)(2,1)S(1)}, bf16[512,128]{1,0:T(8,128)(2,1)S(1)}, u32[]{:S(2)}, u32[]{:S(2)}) collective-permute-start(bf16[512,128]{1,0:T(8,128)(2,1)S(1)} %get-tuple-element.89), channel_id=1, source_target_pairs={{0,48},{16,32},{32,16},{48,0},{1,49},{17,33},{33,17},{49,1},{2,50}... | collective-permute-start | bytes 393224 | tf_op jit(solution)/shard_map/ppermute | solution.py:32
  95.8 7.1 %collective-permute-start.24 = (bf16[64,512]{1,0:T(8,128)(2,1)S(1)}, bf16[64,512]{1,0:T(8,128)(2,1)S(1)}, u32[]{:S(2)}, u32[]{:S(2)}) collective-permute-start(bf16[64,512]{1,0:T(8,128)(2,1)S(1)} %get-tuple-element.98), channel_id=1, source_target_pairs={{0,64},{64,0},{128,192},{192,128},{1,65},{65,1},{129,193},{193,129... | collective-permute-start | bytes 196616 | tf_op jit(solution)/shard_map/ppermute | solution.py:32
  105.2 2.1 %collective-permute-start.25 = (bf16[64,512]{1,0:T(8,128)(2,1)S(1)}, bf16[64,512]{1,0:T(8,128)(2,1)S(1)}, u32[]{:S(2)}, u32[]{:S(2)}) collective-permute-start(bf16[64,512]{1,0:T(8,128)(2,1)S(1)} %get-tuple-element.100), channel_id=1, source_target_pairs={{0,192},{64,128},{128,64},{192,0},{1,193},{65,129},{129,65},{193,1... | collective-permute-start | bytes 196616 | tf_op jit(solution)/shard_map/ppermute | solution.py:32
  107.3 2.6 %collective-permute-done.25.refs_1_ = bf16[64,512]{1,0:T(8,128)(2,1)S(1)} collective-permute-done((bf16[64,512]{1,0:T(8,128)(2,1)S(1)}, bf16[64,512]{1,0:T(8,128)(2,1)S(1)}, u32[]{:S(2)}, u32[]{:S(2)}) %collective-permute-start.25) | collective-permute-done | bytes 65568 | tf_op jit(solution)/shard_map/ppermute | solution.py:32
  110.0 2.4 %collective-permute-start.26 = (f32[64,512]{1,0:T(8,128)S(1)}, f32[64,512]{1,0:T(8,128)S(1)}, u32[]{:S(2)}, u32[]{:S(2)}) collective-permute-start(f32[64,512]{1,0:T(8,128)S(1)} %last.1.refs_1_), channel_id=1, source_target_pairs={{0,8},{8,0},{1,9},{9,1},{2,10},{10,2},{3,11},{11,3},{4,12},{12,4},... | collective-permute-start | bytes 393224 | tf_op jit(solution)/shard_map/ppermute | solution.py:32
  112.4 1.4 %finish.1 = f32[128,512]{1,0:T(8,128)} custom-call(f32[512,128]{1,0:T(8,128)S(1)} %get-tuple-element.86.refs_0_, bf16[512,128]{1,0:T(8,128)(2,1)S(1)} %collective-permute-done.18.refs_1_.refs_3_.refs_2_, bf16[512,128]{1,0:T(8,128)(2,1)S(1)} %collective-permute-done.19.refs_2_.refs_3_, bf16[512,128]{1,0:T(8,128)(2,1)S(1)} %collective-permute-done.20.refs_3_.refs_4_, ...), custom_call_target="tpu_custom_call" | custom-call | flops 910000000 | bytes 3003000 | tf_op jit(solution)/shard_map/finish/pallas_call | solution.py:88
  114.8 1.6 %ends.1 = f32[512,128]{1,0:T(8,128)} custom-call(s32[5]{0:T(128)S(1)} %stack.23.refs_0_, f32[64,512]{1,0:T(8,128)S(1)} %last.1.refs_1_, f32[64,512]{1,0:T(8,128)S(1)} %collective-permute-done.26.refs_2_), custom_call_target="tpu_custom_call" | custom-call | flops 910000000 | bytes 3003000 | tf_op jit(solution)/shard_map/ends/pallas_call | solution.py:88
  (64 shorter events, 16.8 us)
Async XLA Ops:
  0.6 23.2 %collective-permute-start.1 = (bf16[256,512]{1,0:T(8,128)(2,1)}, bf16[256,512]{1,0:T(8,128)(2,1)S(1)}, u32[]{:S(2)}, u32[]{:S(2)}) collective-permute-start(bf16[256,512]{1,0:T(8,128)(2,1)} %refs_1_.3), channel_id=1, source_target_pairs={{0,1},{1,0},{2,3},{3,2},{4,5},{5,4},{6,7},{7,6},{8,9},{9,8},{10,11... | collective-permute-start | bytes 786440 | tf_op jit(solution)/shard_map/ppermute | solution.py:32
  8.5 18.8 %collective-permute-start.2 = (bf16[256,512]{1,0:T(8,128)(2,1)}, bf16[256,512]{1,0:T(8,128)(2,1)S(1)}, u32[]{:S(2)}, u32[]{:S(2)}) collective-permute-start(bf16[256,512]{1,0:T(8,128)(2,1)} %refs_1_.3), channel_id=1, source_target_pairs={{0,2},{2,4},{4,6},{6,0},{1,3},{3,5},{5,7},{7,1},{8,10},{10,12},{12... | collective-permute-start | bytes 786440 | tf_op jit(solution)/shard_map/ppermute | solution.py:28
  9.8 18.5 %collective-permute-start.3 = (bf16[256,512]{1,0:T(8,128)(2,1)}, bf16[256,512]{1,0:T(8,128)(2,1)S(1)}, u32[]{:S(2)}, u32[]{:S(2)}) collective-permute-start(bf16[256,512]{1,0:T(8,128)(2,1)} %refs_1_.3), channel_id=1, source_target_pairs={{0,4},{2,6},{4,0},{6,2},{1,5},{3,7},{5,1},{7,3},{8,12},{10,14},{12... | collective-permute-start | bytes 786440 | tf_op jit(solution)/shard_map/ppermute | solution.py:28
  12.4 15.9 %collective-permute-start.4 = (bf16[256,512]{1,0:T(8,128)(2,1)}, bf16[256,512]{1,0:T(8,128)(2,1)S(1)}, u32[]{:S(2)}, u32[]{:S(2)}) collective-permute-start(bf16[256,512]{1,0:T(8,128)(2,1)} %refs_1_.3), channel_id=1, source_target_pairs={{0,6},{2,0},{4,2},{6,4},{1,7},{3,1},{5,3},{7,5},{8,14},{10,8},{12,... | collective-permute-start | bytes 786440 | tf_op jit(solution)/shard_map/ppermute | solution.py:28
  16.4 7.5 %collective-permute-start = (bf16[128,512]{1,0:T(8,128)(2,1)}, bf16[128,512]{1,0:T(8,128)(2,1)S(1)}, u32[]{:S(2)}, u32[]{:S(2)}) collective-permute-start(bf16[128,512]{1,0:T(8,128)(2,1)} %get-tuple-element.55), channel_id=1, source_target_pairs={{8,0},{16,8},{24,16},{32,24},{40,32},{48,40},{56,48},{64,56},{72,6... | collective-permute-start | bytes 393224 | tf_op jit(solution)/shard_map/ppermute | solution.py:37
  23.9 14.6 %collective-permute-start.5 = (bf16[256,512]{1,0:T(8,128)(2,1)S(1)}, bf16[256,512]{1,0:T(8,128)(2,1)S(1)}, u32[]{:S(2)}, u32[]{:S(2)}) collective-permute-start(bf16[256,512]{1,0:T(8,128)(2,1)S(1)} %after.1.refs_4_.refs_5_), channel_id=1, source_target_pairs={{0,2},{2,4},{4,6},{6,0},{1,3},{3,5},{5,7},{7,1},{8,10},{10,12},{12... | collective-permute-start | bytes 786440 | tf_op jit(solution)/shard_map/ppermute | solution.py:28
  24.6 13.9 %collective-permute-start.6 = (bf16[256,512]{1,0:T(8,128)(2,1)S(1)}, bf16[256,512]{1,0:T(8,128)(2,1)S(1)}, u32[]{:S(2)}, u32[]{:S(2)}) collective-permute-start(bf16[256,512]{1,0:T(8,128)(2,1)S(1)} %after.1.refs_4_.refs_5_), channel_id=1, source_target_pairs={{0,4},{2,6},{4,0},{6,2},{1,5},{3,7},{5,1},{7,3},{8,12},{10,14},{12... | collective-permute-start | bytes 786440 | tf_op jit(solution)/shard_map/ppermute | solution.py:28
  27.2 11.2 %collective-permute-start.7 = (bf16[256,512]{1,0:T(8,128)(2,1)S(1)}, bf16[256,512]{1,0:T(8,128)(2,1)S(1)}, u32[]{:S(2)}, u32[]{:S(2)}) collective-permute-start(bf16[256,512]{1,0:T(8,128)(2,1)S(1)} %after.1.refs_4_.refs_5_), channel_id=1, source_target_pairs={{0,6},{2,0},{4,2},{6,4},{1,7},{3,1},{5,3},{7,5},{8,14},{10,8},{12,... | collective-permute-start | bytes 786440 | tf_op jit(solution)/shard_map/ppermute | solution.py:28
  30.9 7.6 %copy-start = (bf16[256,512]{1,0:T(8,128)(2,1)S(1)}, bf16[256,512]{1,0:T(8,128)(2,1)}, u32[]{:S(2)}) copy-start(bf16[256,512]{1,0:T(8,128)(2,1)} %refs_1_.3) | copy-start | bytes 786436
  42.8 11.4 %collective-permute-start.10 = (bf16[4,512,512]{2,1,0:T(8,128)(2,1)S(1)}, bf16[4,512,512]{2,1,0:T(8,128)(2,1)S(1)}, u32[]{:S(2)}, u32[]{:S(2)}) collective-permute-start(bf16[4,512,512]{2,1,0:T(8,128)(2,1)S(1)} %get-tuple-element.71), channel_id=1, source_target_pairs={{0,8},{8,0},{1,9},{9,1},{2,10},{10,2},{3,11},{11,3},{4,12},{12,4},... | collective-permute-start | bytes 6291464 | tf_op jit(solution)/shard_map/ppermute | solution.py:32
  42.9 5.1 %copy-start.4 = (f32[256,512]{1,0:T(8,128)S(1)}, f32[256,512]{1,0:T(8,128)}, u32[]{:S(2)}) copy-start(f32[256,512]{1,0:T(8,128)} %get-tuple-element.57.refs_3_.refs_2_) | copy-start | bytes 1572868
  48.9 11.1 %collective-permute-start.9 = (bf16[128,512]{1,0:T(8,128)(2,1)S(1)}, bf16[128,512]{1,0:T(8,128)(2,1)S(1)}, u32[]{:S(2)}, u32[]{:S(2)}) collective-permute-start(bf16[128,512]{1,0:T(8,128)(2,1)S(1)} %get-tuple-element.69), channel_id=1, source_target_pairs={{0,8},{8,16},{16,24},{24,32},{32,40},{40,48},{48,56},{56,64},{64,7... | collective-permute-start | bytes 393224 | tf_op jit(solution)/shard_map/ppermute | solution.py:37
  52.7 14.2 %collective-permute-start.8 = (bf16[2,256,512]{2,1,0:T(8,128)(2,1)S(1)}, bf16[2,256,512]{2,1,0:T(8,128)(2,1)S(1)}, u32[]{:S(2)}, u32[]{:S(2)}) collective-permute-start(bf16[2,256,512]{2,1,0:T(8,128)(2,1)S(1)} %get-tuple-element.64), channel_id=1, source_target_pairs={{0,2},{2,0},{4,6},{6,4},{1,3},{3,1},{5,7},{7,5},{8,10},{10,8},{12,... | collective-permute-start | bytes 1572872 | tf_op jit(solution)/shard_map/ppermute | solution.py:32
  54.2 5.8 %copy-start.9 = (bf16[256,512]{1,0:T(8,128)(2,1)S(1)}, bf16[256,512]{1,0:T(8,128)(2,1)}, u32[]{:S(2)}) copy-start(bf16[256,512]{1,0:T(8,128)(2,1)} %get-tuple-element.54.refs_0_.refs_3_) | copy-start | bytes 786436
  54.9 22.5 %collective-permute-start.12 = (bf16[512,512]{1,0:T(8,128)(2,1)S(1)}, bf16[512,512]{1,0:T(8,128)(2,1)S(1)}, u32[]{:S(2)}, u32[]{:S(2)}) collective-permute-start(bf16[512,512]{1,0:T(8,128)(2,1)S(1)} %get-tuple-element.76), channel_id=1, source_target_pairs={{0,64},{64,128},{128,192},{192,0},{1,65},{65,129},{129,193},{193,1... | collective-permute-start | bytes 1572872 | tf_op jit(solution)/shard_map/ppermute | solution.py:28
  56.4 27.4 %collective-permute-start.13 = (bf16[512,512]{1,0:T(8,128)(2,1)S(1)}, bf16[512,512]{1,0:T(8,128)(2,1)S(1)}, u32[]{:S(2)}, u32[]{:S(2)}) collective-permute-start(bf16[512,512]{1,0:T(8,128)(2,1)S(1)} %get-tuple-element.77), channel_id=1, source_target_pairs={{0,128},{64,192},{128,0},{192,64},{1,129},{65,193},{129,1},{193,65... | collective-permute-start | bytes 1572872 | tf_op jit(solution)/shard_map/ppermute | solution.py:28
  58.8 24.9 %collective-permute-start.14 = (bf16[512,512]{1,0:T(8,128)(2,1)S(1)}, bf16[512,512]{1,0:T(8,128)(2,1)S(1)}, u32[]{:S(2)}, u32[]{:S(2)}) collective-permute-start(bf16[512,512]{1,0:T(8,128)(2,1)S(1)} %get-tuple-element.78), channel_id=1, source_target_pairs={{0,192},{64,0},{128,64},{192,128},{1,193},{65,1},{129,65},{193,129... | collective-permute-start | bytes 1572872 | tf_op jit(solution)/shard_map/ppermute | solution.py:28
  66.2 2.7 %collective-permute-start.21 = (f32[64,512]{1,0:T(8,128)S(1)}, f32[64,512]{1,0:T(8,128)S(1)}, u32[]{:S(2)}, u32[]{:S(2)}) collective-permute-start(f32[64,512]{1,0:T(8,128)S(1)} %get-tuple-element.92), channel_id=1, source_target_pairs={{0,8},{8,0},{1,9},{9,1},{2,10},{10,2},{3,11},{11,3},{4,12},{12,4},... | collective-permute-start | bytes 393224 | tf_op jit(solution)/shard_map/ppermute | solution.py:32
  67.6 9.2 %collective-permute-start.15 = (bf16[256,512]{1,0:T(8,128)(2,1)S(1)}, bf16[256,512]{1,0:T(8,128)(2,1)S(1)}, u32[]{:S(2)}, u32[]{:S(2)}) collective-permute-start(bf16[256,512]{1,0:T(8,128)(2,1)S(1)} %get-tuple-element.80), channel_id=1, source_target_pairs={{0,6},{2,4},{4,2},{6,0},{1,7},{3,5},{5,3},{7,1},{8,14},{10,12},{12... | collective-permute-start | bytes 786440 | tf_op jit(solution)/shard_map/ppermute | solution.py:32
  69.7 3.5 %collective-permute-start.22 = (bf16[64,512]{1,0:T(8,128)(2,1)S(1)}, bf16[64,512]{1,0:T(8,128)(2,1)S(1)}, u32[]{:S(2)}, u32[]{:S(2)}) collective-permute-start(bf16[64,512]{1,0:T(8,128)(2,1)S(1)} %get-tuple-element.94), channel_id=1, source_target_pairs={{0,16},{16,0},{32,48},{48,32},{1,17},{17,1},{33,49},{49,33},{2,18}... | collective-permute-start | bytes 196616 | tf_op jit(solution)/shard_map/ppermute | solution.py:32
  73.2 29.7 %collective-permute-start.11 = (bf16[2,256,512]{2,1,0:T(8,128)(2,1)S(1)}, bf16[2,256,512]{2,1,0:T(8,128)(2,1)S(1)}, u32[]{:S(2)}, u32[]{:S(2)}) collective-permute-start(bf16[2,256,512]{2,1,0:T(8,128)(2,1)S(1)} %get-tuple-element.74), channel_id=1, source_target_pairs={{0,2},{2,0},{4,6},{6,4},{1,3},{3,1},{5,7},{7,5},{8,10},{10,8},{12,... | collective-permute-start | bytes 1572872 | tf_op jit(solution)/shard_map/ppermute | solution.py:32
  76.8 17.1 %collective-permute-start.23 = (bf16[64,512]{1,0:T(8,128)(2,1)S(1)}, bf16[64,512]{1,0:T(8,128)(2,1)S(1)}, u32[]{:S(2)}, u32[]{:S(2)}) collective-permute-start(bf16[64,512]{1,0:T(8,128)(2,1)S(1)} %get-tuple-element.96), channel_id=1, source_target_pairs={{0,32},{16,48},{32,0},{48,16},{1,33},{17,49},{33,1},{49,17},{2,34}... | collective-permute-start | bytes 196616 | tf_op jit(solution)/shard_map/ppermute | solution.py:32
  77.4 10.0 %copy-start.1 = (bf16[256,512]{1,0:T(8,128)(2,1)S(1)}, bf16[256,512]{1,0:T(8,128)(2,1)}, u32[]{:S(2)}) copy-start(bf16[256,512]{1,0:T(8,128)(2,1)} %refs_2_.1) | copy-start | bytes 786436
  77.4 10.0 %copy-start.7 = (f32[4,128,128]{2,1,0:T(8,128)S(1)}, f32[4,128,128]{2,1,0:T(8,128)}, u32[]{:S(2)}) copy-start(f32[4,128,128]{2,1,0:T(8,128)} %get-tuple-element.56.refs_2_.refs_3_) | copy-start | bytes 786436
  77.4 26.3 %collective-permute-start.17 = (bf16[256,512]{1,0:T(8,128)(2,1)S(1)}, bf16[256,512]{1,0:T(8,128)(2,1)S(1)}, u32[]{:S(2)}, u32[]{:S(2)}) collective-permute-start(bf16[256,512]{1,0:T(8,128)(2,1)S(1)} %get-tuple-element.85), channel_id=1, source_target_pairs={{0,1},{1,0},{2,3},{3,2},{4,5},{5,4},{6,7},{7,6},{8,9},{9,8},{10,11... | collective-permute-start | bytes 786440 | tf_op jit(solution)/shard_map/ppermute | solution.py:32
  84.9 10.2 %collective-permute-start.18 = (bf16[512,128]{1,0:T(8,128)(2,1)S(1)}, bf16[512,128]{1,0:T(8,128)(2,1)S(1)}, u32[]{:S(2)}, u32[]{:S(2)}) collective-permute-start(bf16[512,128]{1,0:T(8,128)(2,1)S(1)} %get-tuple-element.87), channel_id=1, source_target_pairs={{0,16},{16,0},{32,48},{48,32},{1,17},{17,1},{33,49},{49,33},{2,18}... | collective-permute-start | bytes 393224 | tf_op jit(solution)/shard_map/ppermute | solution.py:32
  85.0 22.3 %collective-permute-start.19 = (bf16[512,128]{1,0:T(8,128)(2,1)S(1)}, bf16[512,128]{1,0:T(8,128)(2,1)S(1)}, u32[]{:S(2)}, u32[]{:S(2)}) collective-permute-start(bf16[512,128]{1,0:T(8,128)(2,1)S(1)} %get-tuple-element.88), channel_id=1, source_target_pairs={{0,32},{16,48},{32,0},{48,16},{1,33},{17,49},{33,1},{49,17},{2,34}... | collective-permute-start | bytes 393224 | tf_op jit(solution)/shard_map/ppermute | solution.py:32
  93.9 13.5 %collective-permute-start.20 = (bf16[512,128]{1,0:T(8,128)(2,1)S(1)}, bf16[512,128]{1,0:T(8,128)(2,1)S(1)}, u32[]{:S(2)}, u32[]{:S(2)}) collective-permute-start(bf16[512,128]{1,0:T(8,128)(2,1)S(1)} %get-tuple-element.89), channel_id=1, source_target_pairs={{0,48},{16,32},{32,16},{48,0},{1,49},{17,33},{33,17},{49,1},{2,50}... | collective-permute-start | bytes 393224 | tf_op jit(solution)/shard_map/ppermute | solution.py:32
  95.8 8.7 %collective-permute-start.24 = (bf16[64,512]{1,0:T(8,128)(2,1)S(1)}, bf16[64,512]{1,0:T(8,128)(2,1)S(1)}, u32[]{:S(2)}, u32[]{:S(2)}) collective-permute-start(bf16[64,512]{1,0:T(8,128)(2,1)S(1)} %get-tuple-element.98), channel_id=1, source_target_pairs={{0,64},{64,0},{128,192},{192,128},{1,65},{65,1},{129,193},{193,129... | collective-permute-start | bytes 196616 | tf_op jit(solution)/shard_map/ppermute | solution.py:32
  103.5 10.2 %collective-permute-start.16 = (bf16[256,512]{1,0:T(8,128)(2,1)S(1)}, bf16[256,512]{1,0:T(8,128)(2,1)S(1)}, u32[]{:S(2)}, u32[]{:S(2)}) collective-permute-start(bf16[256,512]{1,0:T(8,128)(2,1)S(1)} %get-tuple-element.84), channel_id=1, source_target_pairs={{0,6},{2,4},{4,2},{6,0},{1,7},{3,5},{5,3},{7,1},{8,14},{10,12},{12... | collective-permute-start | bytes 786440 | tf_op jit(solution)/shard_map/ppermute | solution.py:32
  105.2 4.7 %collective-permute-start.25 = (bf16[64,512]{1,0:T(8,128)(2,1)S(1)}, bf16[64,512]{1,0:T(8,128)(2,1)S(1)}, u32[]{:S(2)}, u32[]{:S(2)}) collective-permute-start(bf16[64,512]{1,0:T(8,128)(2,1)S(1)} %get-tuple-element.100), channel_id=1, source_target_pairs={{0,192},{64,128},{128,64},{192,0},{1,193},{65,129},{129,65},{193,1... | collective-permute-start | bytes 196616 | tf_op jit(solution)/shard_map/ppermute | solution.py:32
  110.0 4.7 %collective-permute-start.26 = (f32[64,512]{1,0:T(8,128)S(1)}, f32[64,512]{1,0:T(8,128)S(1)}, u32[]{:S(2)}, u32[]{:S(2)}) collective-permute-start(f32[64,512]{1,0:T(8,128)S(1)} %last.1.refs_1_), channel_id=1, source_target_pairs={{0,8},{8,0},{1,9},{9,1},{2,10},{10,2},{3,11},{11,3},{4,12},{12,4},... | collective-permute-start | bytes 393224 | tf_op jit(solution)/shard_map/ppermute | solution.py:32
  (5 other events, 8.7 us)
